TPU v7x, 32 devices: a whole 2x2x4 slice. The times are simulated.
32 devices in a mesh: dp: 16 (over z, y, x), mp: 2 (over core).
Axes of the slice: x: 2, y: 2, z: 4, core: 2. Of those that a mesh axis runs over, the one named last changes fastest.
Arguments:
- tokens: bfloat16 [64, 144, 512], P(('dp', 'mp')), may hold values from -6 to 6
- cotangent: bfloat16 [64, 144, 512], P(('dp', 'mp')), may hold values from -6 to 6
- region_ids: int32 [64, 144], P(('dp', 'mp')), may hold values from 0 to 3
- rel_bucket: int32 [144, 144], replicated, may hold values from 0 to 758
- norm_gain: float32 [512], replicated, may hold values from 0.5 to 1.5
- in_weight: bfloat16 [512, 1536], P('mp'), may hold values from -0.25 to 0.25
- out_weight: bfloat16 [512, 512], P('mp'), may hold values from -0.25 to 0.25
- bias_table: float32 [8, 759], replicated, may hold values from -3 to 250
- in_error: float32 [16, 512, 1536], P('dp', 'mp'), may hold values from -12 to 12
- out_error: float32 [16, 512, 512], P('dp', 'mp'), may hold values from -6 to 6
- in_basis: float32 [2, 1536, 32], P('mp'), may hold values from -6 to 6
- out_basis: float32 [2, 512, 32], P('mp'), may hold values from -6 to 6
Outputs:
- token_grad: bfloat16 [64, 144, 512], P(('dp', 'mp'))
- gain_grad: float32 [512], replicated
- table_grad: float32 [8, 759], replicated
- in_update: float32 [512, 1536], P('mp')
- out_update: float32 [512, 512], P('mp')
- in_new_error: float32 [16, 512, 1536], P('dp', 'mp')
- out_new_error: float32 [16, 512, 512], P('dp', 'mp')
- in_new_basis: float32 [2, 1536, 32], P('mp')
- out_new_basis: float32 [2, 512, 32], P('mp')
All inputs are finite; a program needn't handle non-finite values.
Results may differ from a plain program's by a relative error of at most 0.024.
Values may be sent and summed in bfloat16 or wider, within the bound.
No kernel may reach another device: no remote copies, remote signals or barrier semaphores. Data moves between devices by JAX's collectives and lax.ppermute only.
A program may use at most 64 MiB of HBM per device.

v0:
```python
import jax
import jax.numpy as jnp
from jax import lax
from jax.sharding import PartitionSpec as P

NORM_EPS = 1e-05
BASIS_EPS = 1e-06
MASKED = -1e30
HIGH = lax.Precision.HIGHEST


def norm_forward(token_rows):
    tokens_wide = token_rows.astype(jnp.float32)
    mean_x = jnp.mean(tokens_wide, axis=-1, keepdims=True)
    centered = tokens_wide - mean_x
    variance = jnp.mean(centered * centered, axis=-1, keepdims=True)
    inv_sigma = lax.rsqrt(variance + NORM_EPS)
    return (centered * inv_sigma, inv_sigma)


def orthonormal(left_factor):

    def next_column(j, finished):
        j = j.astype(jnp.int32)
        column = lax.dynamic_slice_in_dim(left_factor, j, 1, 1)
        for repeat in range(2):
            column = column - jnp.dot(
                finished, jnp.dot(finished.T, column, precision=HIGH), precision=HIGH
            )
        column = column * lax.rsqrt(jnp.sum(column * column) + BASIS_EPS)
        return lax.dynamic_update_slice_in_dim(finished, column, j, 1)

    return lax.fori_loop(0, left_factor.shape[1], next_column, jnp.zeros_like(left_factor))


def left_term(merged, basis):
    return jnp.dot(merged, basis, precision=HIGH)


def right_term(merged, left_basis):
    return jnp.einsum("rc,rk->ck", merged, left_basis, precision=HIGH)


def attention_forward(tokens, region_ids, rel_bucket, norm_gain, full_in, bias_table):
    window_count, win_span, feature_count = tokens.shape
    head_count = bias_table.shape[0]
    head_size = feature_count // head_count
    row_count = window_count * win_span
    score_scale = head_size ** (-0.5)
    x_hat, inv_sigma = norm_forward(tokens.reshape(row_count, feature_count))
    normed = (x_hat * norm_gain).astype(jnp.bfloat16)
    projected = jnp.dot(normed, full_in, preferred_element_type=jnp.float32).astype(jnp.bfloat16)
    projected = projected.reshape(window_count, win_span, 3, head_count, head_size)
    queries = projected[:, :, 0]
    key_rows = projected[:, :, 1]
    value_rows = projected[:, :, 2]
    pos_bias = jnp.take(bias_table, rel_bucket, axis=1)
    allowed = region_ids[:, :, None] == region_ids[:, None, :]
    scores = (
        jnp.einsum("wihd,wjhd->whij", queries, key_rows, preferred_element_type=jnp.float32)
        * score_scale
        + pos_bias[None]
    )
    scores = jnp.where(allowed[:, None], scores, MASKED)
    row_top = jnp.max(scores, axis=-1, keepdims=True)
    exp_scores = jnp.exp(scores - row_top)
    attn_prob = exp_scores / jnp.sum(exp_scores, axis=-1, keepdims=True)
    prob_b = attn_prob.astype(jnp.bfloat16)
    mixed_out = jnp.einsum(
        "whij,wjhd->wihd", prob_b, value_rows, preferred_element_type=jnp.float32
    )
    mixed_out = mixed_out.astype(jnp.bfloat16).reshape(row_count, feature_count)
    return (x_hat, inv_sigma, normed, queries, key_rows, value_rows, attn_prob, prob_b, mixed_out)


def attention_backward(saved, cot_rows, rel_bucket, norm_gain, full_in, full_out, table_size):
    x_hat, inv_sigma, normed, queries, key_rows, value_rows, attn_prob, prob_b, mixed_out = saved
    window_count, win_span, head_count, head_size = queries.shape
    row_count = window_count * win_span
    feature_count = head_count * head_size
    score_scale = head_size ** (-0.5)
    mixed_grad = jnp.einsum("te,de->td", cot_rows, full_out, preferred_element_type=jnp.float32)
    mixed_grad = mixed_grad.astype(jnp.bfloat16).reshape(
        window_count, win_span, head_count, head_size
    )
    prob_grad = jnp.einsum(
        "wihd,wjhd->whij", mixed_grad, value_rows, preferred_element_type=jnp.float32
    )
    value_grad = jnp.einsum(
        "whij,wihd->wjhd", prob_b, mixed_grad, preferred_element_type=jnp.float32
    )
    score_grad = attn_prob * (prob_grad - jnp.sum(attn_prob * prob_grad, axis=-1, keepdims=True))
    score_sum = jnp.sum(score_grad, axis=0).reshape(head_count, win_span * win_span)
    table_term = jax.ops.segment_sum(score_sum.T, rel_bucket.reshape(-1), num_segments=table_size).T
    score_b = score_grad.astype(jnp.bfloat16)
    query_grad = (
        jnp.einsum("whij,wjhd->wihd", score_b, key_rows, preferred_element_type=jnp.float32)
        * score_scale
    )
    key_grad = (
        jnp.einsum("whij,wihd->wjhd", score_b, queries, preferred_element_type=jnp.float32)
        * score_scale
    )
    packed_grad = jnp.stack([query_grad, key_grad, value_grad], axis=2).astype(jnp.bfloat16)
    packed_grad = packed_grad.reshape(row_count, 3 * feature_count)
    normed_grad = jnp.einsum("tc,dc->td", packed_grad, full_in, preferred_element_type=jnp.float32)
    gain_term = jnp.sum(normed_grad * x_hat, axis=0)
    hat_grad = normed_grad * norm_gain
    token_delta = inv_sigma * (
        hat_grad
        - jnp.mean(hat_grad, axis=-1, keepdims=True)
        - x_hat * jnp.mean(hat_grad * x_hat, axis=-1, keepdims=True)
    )
    token_grad = (cot_rows.astype(jnp.float32) + token_delta).astype(jnp.bfloat16)
    in_term = jnp.einsum("td,tc->dc", normed, packed_grad, preferred_element_type=jnp.float32)
    return (token_grad, in_term, gain_term, table_term)


def shards(
    tokens,
    cotangent,
    region_ids,
    rel_bucket,
    norm_gain,
    in_weight,
    out_weight,
    bias_table,
    in_error,
    out_error,
    in_basis,
    out_basis,
):
    n_dp = lax.axis_size("dp")
    n_mp = lax.axis_size("mp")
    full_in, full_out = (
        lax.all_gather(in_weight, "mp", axis=0, tiled=True),
        lax.all_gather(out_weight, "mp", axis=0, tiled=True),
    )
    saved = attention_forward(tokens, region_ids, rel_bucket, norm_gain, full_in, bias_table)
    row_count = tokens.shape[0] * tokens.shape[1]
    cot_rows = cotangent.reshape(row_count, tokens.shape[2])
    mixed_out = saved[8]
    out_term = jnp.einsum("td,te->de", mixed_out, cot_rows, preferred_element_type=jnp.float32)
    table_size = bias_table.shape[1]
    token_grad, in_term, gain_term, table_term = attention_backward(
        saved, cot_rows, rel_bucket, norm_gain, full_in, full_out, table_size
    )
    in_shard, out_shard = (
        lax.psum_scatter(
            in_term.astype(jnp.bfloat16), "mp", scatter_dimension=0, tiled=True
        ).astype(jnp.float32),
        lax.psum_scatter(
            out_term.astype(jnp.bfloat16), "mp", scatter_dimension=0, tiled=True
        ).astype(jnp.float32),
    )
    in_merged = in_shard / n_mp + in_error[0]
    out_merged = out_shard / n_mp + out_error[0]
    in_left, out_left = lax.psum(
        (left_term(in_merged, in_basis[0]), left_term(out_merged, out_basis[0])), "dp"
    )
    in_ortho = orthonormal(in_left / n_dp)
    out_ortho = orthonormal(out_left / n_dp)
    in_right, out_right = lax.psum(
        (right_term(in_merged, in_ortho), right_term(out_merged, out_ortho)), "dp"
    )
    in_right = in_right / n_dp
    out_right = out_right / n_dp
    in_update = jnp.dot(in_ortho, in_right.T, precision=HIGH)
    out_update = jnp.dot(out_ortho, out_right.T, precision=HIGH)
    in_new_error = in_merged - in_update
    out_new_error = out_merged - out_update
    gain_total, table_total = lax.psum((gain_term, table_term), ("dp", "mp"))
    devices = n_dp * n_mp
    return (
        token_grad.reshape(tokens.shape),
        gain_total / devices,
        table_total / devices,
        in_update,
        out_update,
        in_new_error[None],
        out_new_error[None],
        in_right[None],
        out_right[None],
    )


def solution(mesh):
    placed = (
        P(("dp", "mp"), None, None),
        P(("dp", "mp"), None, None),
        P(("dp", "mp"), None),
        P(),
        P(),
        P("mp", None),
        P("mp", None),
        P(),
        P("dp", "mp", None),
        P("dp", "mp", None),
        P("mp", None, None),
        P("mp", None, None),
    )
    return jax.shard_map(
        shards,
        mesh=mesh,
        in_specs=placed,
        out_specs=(
            P(("dp", "mp"), None, None),
            P(),
            P(),
            P("mp", None),
            P("mp", None),
            P("dp", "mp", None),
            P("dp", "mp", None),
            P("mp", None, None),
            P("mp", None, None),
        ),
        check_vma=False,
    )
```

profile of v0, /device:TPU:0, one launch (start us, length us, event | category | flops | bytes accessed | tf_op | source)
XLA Modules:
  0.0 624.5 jit_solution(11795333347090401598)
XLA Ops:
  9.1 1.2 multiply_reduce_fusion.5
  10.3 2.5 all_gather.7
  13.7 1.2 copy.72
  15.2 38.9 %gather_fusion = f32[20736,8]{1,0:T(8,128)} fusion(f32[8,759]{0,1:T(8,128)S(1)} %copy.69, s32[21504]{0:T(1024)S(1)} %pad_clamp_fusion), kind=kCustom, calls=%fused_computation | custom fusion | bytes 1410048 | tf_op jit(solution)/shard_map/jit(_take)/gather | solution.py:57
  54.1 11.3 %copy.70 = f32[144,144,8]{0,1,2:T(8,128)S(1)} copy(f32[144,144,8]{2,1,0:T(8,128)} %bitcast.201) | data formatting | bytes 1327104 | tf_op jit(solution)/shard_map/jit(_take)/gather | solution.py:57
  66.8 1.2 select_bitcast_fusion
  68.0 2.0 convolution_convert_fusion.1
  70.0 2.0 reshape.164
  72.0 1.5 fusion.65
  74.8 3.8 fusion.66
  78.5 2.1 fusion.12
  81.0 2.0 multiply_reduce_fusion.2
  83.7 1.2 convolution_convert_fusion.2
  85.2 3.2 fusion.17
  91.5 2.5 copy.77
  94.1 2.9 convert_element_type.79
  97.0 2.1 convolution_convert_fusion
  100.5 6.2 copy.79
  106.7 112.5 %scatter_custom_fusion = f32[759,8]{1,0:T(8,128)S(1)} fusion(s32[20736]{0:T(1024)S(1)} %reshape.180, f32[20736,8]{1,0:T(8,128)} %copy.79, f32[]{:T(128)} %constant.109.clone.1), kind=kCustom, calls=%fused_computation.78 | custom fusion | flops 165888 | bytes 24800 | tf_op jit(solution)/shard_map/scatter-add | solution.py:94
  219.3 3.0 multiply_reduce_fusion.6
  222.3 46.9 %all-reduce = (f32[512]{0:T(512)S(1)}, f32[8,759]{0,1:T(8,128)S(1)}) all-reduce(f32[512]{0:T(512)S(1)} %get-tuple-element.183, f32[8,759]{0,1:T(8,128)S(1)} %bitcast.203), channel_id=1, replica_groups=mesh['dp'=16,'mp'=2] {'dp','mp'}, use_global_device_ids=true, to_apply=%region_8.9 | all-reduce | flops 6584 | bytes 52672 | tf_op jit(solution)/shard_map/psum | solution.py:172
  270.0 2.1 fusion.47
  272.1 3.3 fusion.31
  275.8 100.9 %all-reduce.6.cloned.1.call-done = (f32[256,32]{0,1:T(8,128)}, f32[256,32]{0,1:T(8,128)}) async-done(((f32[256,32]{0,1:T(8,128)}, f32[256,32]{0,1:T(8,128)}), (f32[256,32]{0,1:T(8,128)}, f32[256,32]{0,1:T(8,128)})) %all-reduce.6.cloned.1.call-update) | async-done | bytes 65552 | tf_op jit(solution)/shard_map/psum | solution.py:158
  377.4 62.1 %while.26 = (s32[]{:T(128)}, f32[256,32]{0,1:T(8,128)S(1)}, f32[256,32]{0,1:T(8,128)S(1)}, s32[]{:T(128)}, f32[]{:T(128)}, /*index=5*/s32[]{:T(128)}) while((s32[]{:T(128)}, f32[256,32]{0,1:T(8,128)S(1)}, f32[256,32]{0,1:T(8,128)S(1)}, s32[]{:T(128)}, f32[]{:T(128)}, /*index=5*/s32[]{:T(128)}) %tuple.77), condition=%wide.region_16.17_spmd, body=%wide.region_14.16_spmd.sunk | while | flops 394498 | bytes 141941 | solution.py:33
  439.6 62.1 %while.27 = (s32[]{:T(128)}, f32[256,32]{0,1:T(8,128)S(1)}, f32[256,32]{0,1:T(8,128)S(1)}, s32[]{:T(128)}, f32[]{:T(128)}, /*index=5*/s32[]{:T(128)}) while((s32[]{:T(128)}, f32[256,32]{0,1:T(8,128)S(1)}, f32[256,32]{0,1:T(8,128)S(1)}, s32[]{:T(128)}, f32[]{:T(128)}, /*index=5*/s32[]{:T(128)}) %tuple.80), condition=%wide.region_22.23_spmd, body=%wide.region_20.22_spmd.sunk | while | flops 394498 | bytes 141941 | solution.py:33
  501.7 1.8 fusion.30
  505.3 1.7 copy.82
  507.0 2.1 add_convert_fusion
  509.2 101.8 %all-reduce.8.cloned.1.call-done = (f32[1536,32]{0,1:T(8,128)}, f32[512,32]{0,1:T(8,128)}) async-done(((f32[1536,32]{0,1:T(8,128)}, f32[512,32]{0,1:T(8,128)}), (f32[1536,32]{0,1:T(8,128)}, f32[512,32]{0,1:T(8,128)})) %all-reduce.8.cloned.1.call-update) | async-done | bytes 262160 | tf_op jit(solution)/shard_map/psum | solution.py:163
  611.0 2.4 fusion.36
  615.5 1.5 subtract_bitcast_fusion
  (496 shorter events, 96.0 us)
Async XLA Ops:
  7.2 265.0 %copy-start = (f32[1,1536,32]{1,2,0:T(8,128)S(1)}, f32[1,1536,32]{1,2,0:T(8,128)}, u32[]{:S(2)}) copy-start(f32[1,1536,32]{1,2,0:T(8,128)} %param.26) | copy-start | bytes 589828
  7.2 5.6 copy-start.15
  7.2 5.6 copy-start.16
  7.2 60.8 %all-gather.2.cloned.1.call-start = ((), (), s32[]{:S(2)}) async-start(), calls=%async_computation.2 | async-start | bytes 2359296 | tf_op jit(solution)/shard_map/all_gather | solution.py:136
  7.9 262.0 %reduce-scatter.5.cloned.1.call-start = ((), (), s32[]{:S(2)}) async-start(), calls=%async_computation.4 | async-start | bytes 786432 | tf_op jit(solution)/shard_map/reduce_scatter | solution.py:152
  12.8 2.1 copy-start.27
  54.1 11.5 %copy-start.29 = (s32[2,144]{1,0:T(2,128)S(1)}, s32[2,144]{1,0:T(2,128)}, u32[]{:S(2)}) copy-start(s32[2,144]{1,0:T(2,128)} %param.18) | copy-start | bytes 3460
  54.1 11.6 %copy-start.2 = (bf16[2,144,512]{2,1,0:T(8,128)(2,1)S(1)}, bf16[2,144,512]{2,1,0:T(8,128)(2,1)}, u32[]{:S(2)}) copy-start(bf16[2,144,512]{2,1,0:T(8,128)(2,1)} %param.16) | copy-start | bytes 884740
  54.1 11.6 %copy-start.28 = (f32[512]{0:T(512)S(1)}, f32[512]{0:T(512)}, u32[]{:S(2)}) copy-start(f32[512]{0:T(512)} %param.20) | copy-start | bytes 6148
  66.8 3.2 copy-start.20
  73.9 4.6 copy-start.10
  74.3 4.2 copy-start.12
  78.5 2.4 copy-start.6
  78.5 2.5 copy-start.22
  85.0 187.2 %reduce-scatter.3.cloned.1.call-start = ((), (), s32[]{:S(2)}) async-start(), calls=%async_computation.3 | async-start | bytes 2359296 | tf_op jit(solution)/shard_map/reduce_scatter | solution.py:149
  85.2 3.2 copy-start.13
  88.4 1.8 copy-start.7
  94.0 2.9 copy-start.24
  97.0 2.2 copy-start.17
  99.2 277.4 %all-reduce.6.cloned.1.call-start = ((), (), s32[]{:S(2)}) async-start(), calls=%async_computation.5 | async-start | bytes 131072 | tf_op jit(solution)/shard_map/psum | solution.py:158
  100.5 118.8 %copy-start.18 = (bf16[288,1536]{1,0:T(8,128)(2,1)S(1)}, bf16[288,1536]{1,0:T(8,128)(2,1)}, u32[]{:S(2)}) copy-start(bf16[288,1536]{1,0:T(8,128)(2,1)} %copy-done.17) | copy-start | bytes 2654212
  100.5 118.8 %copy-start.21 = (f32[288,512]{1,0:T(8,128)S(1)}, f32[288,512]{1,0:T(8,128)}, u32[]{:S(2)}) copy-start(f32[288,512]{1,0:T(8,128)} %copy-done.20) | copy-start | bytes 1769476
  219.3 50.7 %copy-start.5 = (f32[1,256,512]{2,1,0:T(8,128)S(1)}, f32[1,256,512]{2,1,0:T(8,128)}, u32[]{:S(2)}) copy-start(f32[1,256,512]{2,1,0:T(8,128)} %param.25) | copy-start | bytes 1572868
  219.3 50.7 %copy-start.26 = (f32[1,512,32]{1,2,0:T(8,128)S(1)}, f32[1,512,32]{1,2,0:T(8,128)}, u32[]{:S(2)}) copy-start(f32[1,512,32]{1,2,0:T(8,128)} %param.27) | copy-start | bytes 196612
  222.3 49.9 %copy-start.1 = (f32[1,256,1536]{2,1,0:T(8,128)S(1)}, f32[1,256,1536]{2,1,0:T(8,128)}, u32[]{:S(2)}) copy-start(f32[1,256,1536]{2,1,0:T(8,128)} %param.24) | copy-start | bytes 4718596
  272.1 229.6 %copy-start.3 = (bf16[256,1536]{1,0:T(8,128)(2,1)S(1)}, bf16[256,1536]{1,0:T(8,128)(2,1)}, u32[]{:S(2)}) copy-start(bf16[256,1536]{1,0:T(8,128)(2,1)} %reduce-scatter.3.cloned.1.call-done) | copy-start | bytes 2359300
  275.5 335.5 %all-reduce.8.cloned.1.call-start = ((), (), s32[]{:S(2)}) async-start(), calls=%async_computation.6 | async-start | bytes 524288 | tf_op jit(solution)/shard_map/psum | solution.py:163
  501.7 1.8 copy-start.8
  611.0 2.4 copy-start.19
  611.0 3.2 copy-start.25
  613.5 3.6 copy-start.4
  614.8 2.2 copy-start.14
  (3 other events, 3.8 us)
Sparse Core Ops, SparseCore 0:
  9.6 12.4 all-gather.1
  85.1 10.5 reduce-scatter.4
  99.3 11.6 reduce-scatter.2
  275.6 100.9 all-reduce.5
  504.8 106.1 all-reduce.7
where the time goes:
time: 626 us; the launch traced here: 624 us
  waiting for transfers between devices  203 us (32%)
  other arithmetic  129 us (21%)
  matrix products  105 us (17%)
  local copies, waits for them, and re-layouts  76.8 us (12%)
  blocking collectives  49.4 us (8%)
  loops' own time  46.1 us (7%)
  between operations  14.3 us (2%)
    scatter-add x1, other arithmetic, attention_backward(): jax.ops.segment_sum(score_sum.T, rel_bucket.reshape(-1), num_segments=tab...  113 us
    psum x1, waiting for transfers between devices, shards(): lax.psum((right_term(in_merged, in_ortho), right_term(out_merged, out_ort...  102 us
    psum x1, waiting for transfers between devices, shards(): lax.psum((left_term(in_merged, in_basis[0]), left_term(out_merged, out_ba...  101 us
    dot_general x128, matrix products, next_column(): jnp.dot(finished, jnp.dot(finished.T, column, precision=HIGH), precision=...  57.8 us
    gather x2, local copies, waits for them, and re-layouts, attention_forward(): pos_bias = jnp.take(bias_table, rel_bucket, axis=1)  50.2 us
    psum x1, blocking collectives, shards(): gain_total, table_total = lax.psum((gain_term, table_term), ('dp', 'mp'))  46.9 us
    another operation x2, loops' own time, orthonormal(): lax.fori_loop(0, left_factor.shape[1], next_column, jnp.zeros_like(left_f...  46.1 us
    dot_general x128, matrix products, next_column(): jnp.dot(finished.T, column, precision=HIGH)  17.3 us
  transfers between devices with their start and end apart: 5, of which 2 were waited for; matrix products, arithmetic and copies ran while one was open for 32% of the time, Pallas kernels for 0%

commit v1 on v0

v1 whole, which is shorter than its diff:
```python
import functools

import jax
import jax.numpy as jnp
from jax import lax
from jax.experimental import pallas as pl
from jax.experimental.pallas import tpu as pltpu
from jax.sharding import PartitionSpec as P

NORM_EPS = 1e-05
BASIS_EPS = 1e-06
MASKED = -1e30
LANES = 128
SUBLANES = 8
READY_HEADS = 2
F32 = jnp.float32
BF16 = jnp.bfloat16

VMEM = pl.BlockSpec(memory_space=pltpu.VMEM)
SMEM = pl.BlockSpec(memory_space=pltpu.SMEM)
HBM = pl.BlockSpec(memory_space=pltpu.HBM)
ANY = pl.BlockSpec(memory_space=pl.ANY)


def nn(a, b):
    return lax.dot_general(
        a, b, (((1,), (0,)), ((), ())), preferred_element_type=F32
    )


def nt(a, b):
    return lax.dot_general(
        a, b, (((1,), (1,)), ((), ())), preferred_element_type=F32
    )


def tn(a, b):
    return lax.dot_general(
        a, b, (((0,), (0,)), ((), ())), preferred_element_type=F32
    )


def block_columns(me, step, blocks, width):
    if blocks == 1:
        return pl.ds(0, width)
    index = me if step == 0 else 1 - me
    return pl.ds(pl.multiple_of(index * width, width), width)


def norm_forward(token_rows):
    tokens_wide = token_rows.astype(F32)
    mean_x = jnp.mean(tokens_wide, axis=-1, keepdims=True)
    centered = tokens_wide - mean_x
    variance = jnp.mean(centered * centered, axis=-1, keepdims=True)
    inv_sigma = lax.rsqrt(variance + NORM_EPS)
    return (centered * inv_sigma, inv_sigma)


def fetch(pairs, sems):
    copies = [
        pltpu.make_async_copy(source, target, sems.at[at])
        for at, (source, target) in enumerate(pairs)
    ]
    for copy in copies:
        copy.start()
    return copies


def halves(value):
    coarse = value.astype(BF16)
    return coarse, (value - coarse.astype(F32)).astype(BF16)


def stacked(value):
    return jnp.concatenate(halves(value), axis=0)


def folded(value):
    half = value.shape[0] // 2
    return value[:half] + value[half:]


def gather_bias(bias, heads, table_pad, index_t, index):
    span = index.shape[0]
    padded = table_pad.shape[1]
    even = span // LANES * LANES
    lookups = [(index_t[:, :even], False)] if even else []
    if even < span:
        lookups.append((index[even:, :], True))
    for places, flipped in lookups:
        rows, columns = places.shape
        for start in range(0, columns, LANES):
            stop = min(columns, start + LANES)
            part = places[:, start:stop]
            if stop - start < LANES:
                filler = jnp.zeros((rows, LANES - (stop - start)), jnp.int32)
                part = jnp.concatenate([part, filler], axis=1)
            high, low = part // LANES, part % LANES
            for head in heads:
                found = jnp.zeros((rows, LANES), F32)
                for level in range(padded // LANES):
                    row = table_pad[head : head + 1, level * LANES : (level + 1) * LANES]
                    row = jnp.broadcast_to(row, (rows, LANES))
                    picked = jnp.take_along_axis(row, low, axis=1, mode="promise_in_bounds")
                    found = jnp.where(high == level, picked, found)
                if flipped:
                    bias[head, start:stop, even:] = found[:, : stop - start].T
                else:
                    bias[head, :, start:stop] = found[:, : stop - start]


def prepare_kernel(blocks, ready, me_ref, *refs):
    sources, rest = refs[:12], refs[12:]
    normed, part, bias, index_t, table_pad, bucket, *kept = rest[:16]
    table, sems = rest[16:]
    copies = fetch(list(zip(sources, [bucket, table] + kept)), sems)
    tokens, gain, w_own = kept[:3]
    me = me_ref[0]
    width = w_own.shape[0]
    span = bucket.shape[0]
    head_count, padded = table_pad.shape
    for copy in copies[:2]:
        copy.wait()
    table_pad[...] = jnp.zeros_like(table_pad)
    table_pad[:, : table.shape[1]] = table[...]
    index_t[...] = bucket[...].T
    gather_bias(bias, range(ready), table_pad, index_t, bucket)
    for copy in copies[2:5]:
        copy.wait()
    x_hat, _ = norm_forward(tokens[...])
    normed[...] = (x_hat * gain[...]).astype(BF16)
    part[...] = nn(normed[:, block_columns(me, 0, blocks, width)], w_own[...])
    for copy in copies[5:]:
        copy.wait()


def attend_kernel(blocks, share, *refs):
    me_ref, normed, part, bias_ready, index_t, table_pad, bucket, gain, cot, region = refs[:10]
    own, arrived = refs[10:14], refs[14 : 10 + 4 * blocks]
    rest = refs[10 + 4 * blocks :]
    terms, lefts, rest = rest[:blocks], rest[blocks : 2 * blocks], rest[2 * blocks :]
    score_parts, (packed, gain_term), rest = rest[:blocks], rest[blocks : blocks + 2], rest[blocks + 2 :]
    proj, mixed_grad, mixed, score_sum, gain_row, bias = rest
    w_in, w_out, in_basis, out_basis = (
        [own[at]] + list(arrived[at : at + blocks - 1]) for at in range(4)
    )
    me = me_ref[0]
    window_count, span = region.shape
    features = normed.shape[1]
    ready, head_count = bias_ready.shape[0], bias.shape[0]
    head_size = features // head_count
    scale = head_size ** (-0.5)
    width = features // blocks
    if blocks == 1:
        proj[...] = part[...].astype(BF16)
    else:
        other = nn(normed[:, block_columns(me, 1, blocks, width)], w_in[1][...])
        proj[...] = (part[...] + other).astype(BF16)
    for step in range(blocks):
        mixed_grad[:, block_columns(me, step, blocks, width)] = nt(
            cot[...], w_out[step][...]
        ).astype(BF16)
    lane = lax.broadcasted_iota(jnp.int32, (span, LANES), 1)
    per_group = LANES // head_size
    for window in range(window_count):
        rows = pl.ds(window * span, span)
        ids_row = jnp.broadcast_to(region[window : window + 1, :], (span, span))
        allowed = ids_row == ids_row.T
        for group in range(features // LANES):
            start = group * LANES
            heads = slice(group * per_group, (group + 1) * per_group)
            if heads.stop <= ready:
                pair_bias = bias_ready[heads]
            else:
                if window == 0:
                    gather_bias(bias, range(heads.start, heads.stop), table_pad, index_t, bucket)
                pair_bias = bias[heads]
            q = proj[rows, start : start + LANES]
            k = proj[rows, features + start : features + start + LANES]
            v = proj[rows, 2 * features + start : 2 * features + start + LANES]
            g = mixed_grad[rows, start : start + LANES]
            pick = [lane // head_size == sub for sub in range(per_group)]
            k_split = jnp.concatenate([jnp.where(own, k, jnp.zeros_like(k)) for own in pick], 0)
            v_split = jnp.concatenate([jnp.where(own, v, jnp.zeros_like(v)) for own in pick], 0)
            scores = nt(k_split, q).reshape(per_group, span, span) * scale + pair_bias
            scores = jnp.where(allowed[None], scores, MASKED)
            top = jnp.max(scores, axis=1, keepdims=True)
            raised = jnp.exp(scores - top)
            prob = raised * (1.0 / jnp.sum(raised, axis=1, keepdims=True))
            prob_b = prob.astype(BF16)
            prob_grad = nt(v_split, g).reshape(per_group, span, span)
            inner = jnp.sum(prob * prob_grad, axis=1, keepdims=True)
            score_grad = prob * (prob_grad - inner)
            score_b = score_grad.astype(BF16)
            if window == 0:
                score_sum[heads] = score_grad
            else:
                score_sum[heads] += score_grad
            k_grads = nn(score_b.reshape(per_group * span, span), q)
            v_grads = nn(prob_b.reshape(per_group * span, span), g)

            def joined(parts):
                total = parts[0]
                for sub in range(1, per_group):
                    total = jnp.where(pick[sub], parts[sub], total)
                return total

            k_grad = joined([k_grads[at * span : (at + 1) * span] for at in range(per_group)])
            v_grad = joined([v_grads[at * span : (at + 1) * span] for at in range(per_group)])
            out = joined([tn(prob_b[at], v) for at in range(per_group)])
            q_grad = joined([tn(score_b[at], k) for at in range(per_group)])
            mixed[rows, start : start + LANES] = out.astype(BF16)
            packed[rows, start : start + LANES] = (q_grad * scale).astype(BF16)
            packed[rows, features + start : features + start + LANES] = (k_grad * scale).astype(
                BF16
            )
            packed[rows, 2 * features + start : 2 * features + start + LANES] = v_grad.astype(BF16)
    wide = 3 * features
    for step in range(blocks):
        columns = block_columns(me, step, blocks, width)
        product = tn(normed[:, columns], packed[...])
        terms[step][:, :wide] = product.astype(BF16)
        terms[step][:, wide:] = tn(mixed[:, columns], cot[...]).astype(BF16)
        weighted = product * w_in[step][...].astype(F32)
        folds = tree_add(
            [weighted[:, start : start + LANES] for start in range(0, wide, LANES)]
        )
        gain_row[:, columns] = jnp.sum(folds.T, axis=0, keepdims=True) / gain[:, columns]
        rank = in_basis[step].shape[0]
        for basis, at, place in (
            (in_basis[step], slice(None, wide), 0),
            (out_basis[step], slice(wide, None), rank),
        ):
            left = folded(nt(stacked(basis[...]), terms[step][:, at])) * share
            lefts[step][place : place + rank, :] = left
    gain_term[...] = jnp.zeros_like(gain_term)
    for piece in range(features // LANES):
        gain_term[piece : piece + 1, :] = gain_row[:, piece * LANES : (piece + 1) * LANES]
    rows = span // blocks
    for step in range(blocks):
        score_parts[step][...] = score_sum[:, block_columns(me, step, blocks, rows), :]


def token_kernel(blocks, me_ref, packed, *refs):
    w_in, (tokens, cot, gain, _, result, flag, normed_grad, token_grad, sems) = (
        refs[:blocks],
        refs[blocks:],
    )
    me = me_ref[0]
    width = tokens.shape[1] // blocks
    for step in range(blocks):
        normed_grad[:, block_columns(me, step, blocks, width)] = nt(packed[...], w_in[step][...])
    x_hat, inv_sigma = norm_forward(tokens[...])
    hat_grad = normed_grad[...] * gain[...]
    token_delta = inv_sigma * (
        hat_grad
        - jnp.mean(hat_grad, axis=-1, keepdims=True)
        - x_hat * jnp.mean(hat_grad * x_hat, axis=-1, keepdims=True)
    )
    token_grad[...] = (cot[...].astype(F32) + token_delta).astype(BF16)
    flag[...] = jnp.zeros_like(flag)
    for copy in fetch([(token_grad, result)], sems):
        copy.wait()


def table_kernel(blocks, me_ref, *refs):
    score_parts, (gain_term, index_t, stats) = refs[:blocks], refs[blocks:]
    head_count, rows, span = score_parts[0].shape
    padded = stats.shape[1] - 2 * LANES
    levels = padded // LANES
    indices = index_t[block_columns(me_ref[0], 0, blocks, rows), :]
    scores = tree_add([part[...] for part in score_parts])
    sublane = lax.broadcasted_iota(jnp.int32, (LANES, span), 0)
    total = jnp.zeros((2 * levels * head_count, LANES), F32)
    for row in range(rows):
        index = indices[row : row + 1, :]
        high = jnp.broadcast_to(index // LANES, (head_count, span))
        low = jnp.broadcast_to(index % LANES, (LANES, span))
        one_hot = jnp.where(low == sublane, 1.0, 0.0).astype(BF16)
        values = scores[:, row, :]
        coarse = values.astype(BF16).astype(F32)
        fine = values - coarse
        picked = [
            jnp.where(high == level, piece, 0.0)
            for piece in (coarse, fine)
            for level in range(levels)
        ]
        total += nt(jnp.concatenate(picked, axis=0).astype(BF16), one_hot)
    total = folded(total)
    for level in range(levels):
        stats[:, level * LANES : (level + 1) * LANES] = total[
            level * head_count : (level + 1) * head_count
        ]
    stats[:, padded : padded + LANES] = gain_term[...]
    stats[:, padded + LANES :] = jnp.zeros((head_count, LANES), F32)


def shard_kernel(share, shard, in_basis, out_basis, left):
    rank, split = in_basis.shape
    left[:rank, :] = folded(nt(stacked(in_basis[...]), shard[:, :split])) * share
    left[rank:, :] = folded(nt(stacked(out_basis[...]), shard[:, split:])) * share


def error_kernel(term_left, in_error, out_error, in_basis, out_basis, left):
    rank = in_basis.shape[0]
    for error, basis, at in ((in_error, in_basis, 0), (out_error, out_basis, rank)):
        coarse, fine = halves(error[...])
        pair = stacked(basis[...])
        left[at : at + rank, :] = term_left[at : at + rank, :] + folded(
            nt(pair, coarse) + nt(pair, fine)
        )


def merge_kernel(share, parts, *refs):
    shards, (in_error, out_error, merged) = refs[:parts], refs[parts:]
    split = in_error.shape[1]
    for columns, error in ((slice(None, split), in_error), (slice(split, None), out_error)):
        total = tree_add([shard[:, columns].astype(F32) for shard in shards])
        merged[:, columns] = total * share + error[...]


def tree_sum(values):
    while len(values) > 1:
        values = [values[at] + values[at + 1] for at in range(0, len(values), 2)]
    return values[0]


def tree_add(values):
    while len(values) > 1:
        odd = values[len(values) // 2 * 2 :]
        values = [values[at] + values[at + 1] for at in range(0, len(values) - 1, 2)] + odd
    return values[0]


def join_kernel(left_own, left_other, *refs):
    left = refs[len(refs) // 2]
    left[...] = left_own[...] + left_other[...]


def add_kernel(parts, *refs):
    refs[-1][...] = tree_sum([ref[...] for ref in refs[:parts]])


def stats_pieces(pair):
    pieces = []
    for at in range(2):
        tile = pair[:, at * LANES : (at + 1) * LANES]
        coarse, fine = halves(tile)
        pieces += [coarse.astype(F32), fine.astype(F32)]
    return jnp.concatenate(pieces, axis=0).astype(BF16)


def stats_pair(pieces):
    rows = pieces.shape[0] // 4
    return jnp.concatenate(
        [
            pieces[2 * at * rows : (2 * at + 1) * rows]
            + pieces[(2 * at + 1) * rows : (2 * at + 2) * rows]
            for at in range(2)
        ],
        axis=1,
    )


def orthonormal(problems):
    rank, rows = problems[0].shape
    tiles = rank // SUBLANES
    spread_shape = (SUBLANES, rows)
    place = lax.broadcasted_iota(jnp.int32, spread_shape, 0)

    def dots(rows_of, vector):
        return jnp.sum(rows_of * vector, axis=1, keepdims=True)

    def spread(tiled, row):
        tile, at = divmod(row, SUBLANES)
        return jnp.broadcast_to(tiled[tile][at : at + 1], spread_shape)

    states = []
    for first in problems:
        original = [first[at * SUBLANES : (at + 1) * SUBLANES] for at in range(tiles)]
        states.append((original, list(original), [jnp.zeros(spread_shape, F32)] * tiles))
    def project(finished, found):
        weighted = tree_add([found[q] * finished[q] for q in found])
        return jnp.sum(weighted, axis=0, keepdims=True)

    currents = [spread(original, 0) for original, _, _ in states]
    known = [None for _ in states]
    for column in range(rank):
        tile, at = divmod(column, SUBLANES)
        before = range((column - 1) // SUBLANES + 1)
        for which, (original, residual, finished) in enumerate(states):
            current = currents[which]
            square = dots(current, current)
            inverse = lax.rsqrt(square + BASIS_EPS)
            unit = current * inverse
            if column + 1 < rank:
                ahead = spread(residual, column + 1)
                step = dots(spread(original, column + 1), current) * inverse
                own = dots(ahead, current) * inverse
                following = ahead - unit * (step + own - step * (square * inverse * inverse))
                if column:
                    cross = project(finished, {q: dots(finished[q], current) for q in before})
                    following = following - known[which] + (step * inverse) * cross
            finished[tile] = jnp.where(place == at, unit, finished[tile])
            if column + 1 < rank:
                for q in range((column + 1) // SUBLANES, tiles):
                    residual[q] = residual[q] - (dots(original[q], current) * inverse) * unit
                currents[which] = following
            if column + 2 < rank:
                far = spread(residual, column + 2)
                known[which] = project(
                    finished, {q: dots(finished[q], far) for q in range(tile + 1)}
                )
    return [jnp.concatenate(finished, axis=0) for _, _, finished in states]


def ortho_kernel(share, parts, stat_parts, me_ref, *refs):
    lefts, stats = refs[:parts], refs[parts : parts + stat_parts]
    merged, ortho, *pieces, sums = refs[parts + stat_parts :]
    digit = me_ref[1]
    rank = ortho.shape[0] // 2
    quarter = merged.shape[1] // len(pieces)
    sums[...] = tree_sum([stat[...] for stat in stats])
    total = tree_sum([left[...] for left in lefts]) * share
    finished = orthonormal([total[:rank], total[rank:]])
    ortho[:rank, :], ortho[rank:, :] = finished
    for step, piece in enumerate(pieces):
        block = jnp.bitwise_xor(digit, step)
        columns = pl.ds(pl.multiple_of(block * quarter, quarter), quarter)
        pair = stacked(jnp.where(block < len(pieces) - 1, finished[0], finished[1]))
        coarse, fine = halves(merged[:, columns])
        piece[:, :quarter] = folded(nn(pair, coarse) + nn(pair, fine)).astype(BF16)
        stat_columns = pl.ds(pl.multiple_of(block * 2 * LANES, 2 * LANES), 2 * LANES)
        piece[:, quarter:] = stats_pieces(sums[:, stat_columns])


def reduce_kernel(*refs):
    pieces, total = refs[:-2], refs[-1]
    quarter = total.shape[1] - LANES
    summed = tree_sum([piece[...].astype(F32) for piece in pieces])
    total[:, :quarter] = summed[:, :quarter].astype(BF16)
    total[:, quarter:] = stats_pieces(stats_pair(summed[:, quarter:]))


def update_kernel(share, stat_share, parts, me_ref, *refs):
    pieces = refs[:parts]
    ortho, merged = refs[parts : parts + 2]
    in_update, out_update, in_new_error, out_new_error = refs[parts + 2 : parts + 6]
    small_results = refs[parts + 6 : parts + 10]
    rights, updates, errors, sems = refs[parts + 10 : parts + 14]
    small = refs[parts + 14 : parts + 18]
    in_basis, out_basis, table, gain = small
    digit = me_ref[1]
    rank = ortho.shape[0] // 2
    quarter = rights.shape[2] - LANES
    for step, piece in enumerate(pieces):
        rights[step] = piece[...].astype(F32)
    copies = []
    tiles = []
    for block in range(parts):
        here = rights[jnp.bitwise_xor(digit, block)]
        right = here[:, :quarter] * share
        tiles.append(stats_pair(here[:, quarter:]) * stat_share)
        is_in = block < parts - 1
        columns = slice(block * quarter, (block + 1) * quarter)
        own = ortho[:rank, :] if is_in else ortho[rank:, :]
        own_coarse, own_fine = halves(own)
        coarse, fine = halves(right)
        update = tn(
            jnp.concatenate([own_coarse, own_coarse, own_fine], axis=0),
            jnp.concatenate([coarse, fine, coarse], axis=0),
        )
        updates[block] = update
        errors[block] = merged[:, columns] - update
        if is_in:
            in_basis[:, columns] = right
            update_to, error_to = in_update.at[:, columns], in_new_error.at[:, columns]
        else:
            out_basis[...] = right
            update_to, error_to = out_update, out_new_error
        copies += fetch(
            [(updates.at[block], update_to), (errors.at[block], error_to)], sems.at[block]
        )
    stats = jnp.concatenate(tiles, axis=1)
    table[...] = stats[:, : table.shape[1]]
    padded = stats.shape[1] - 2 * LANES
    for at in range(gain.shape[1] // LANES):
        gain[:, at * LANES : (at + 1) * LANES] = stats[at : at + 1, padded : padded + LANES]
    copies += fetch(list(zip(small, small_results)), refs[parts + 18])
    for copy in copies:
        copy.wait()


def call(kernel, outs, scratch=(), flops=0, moved=0, vmem=16, **options):
    return pl.pallas_call(
        kernel,
        out_shape=outs,
        scratch_shapes=list(scratch),
        cost_estimate=pl.CostEstimate(flops=flops, bytes_accessed=moved, transcendentals=0),
        compiler_params=pltpu.CompilerParams(vmem_limit_bytes=vmem << 20),
        **options,
    )


def buffers(*arrays):
    return [pltpu.VMEM(array.shape, array.dtype) for array in arrays] + [
        pltpu.SemaphoreType.DMA((len(arrays),))
    ]


def in_hbm(*arrays):
    return [pltpu.with_memory_space_constraint(array, pltpu.HBM) for array in arrays]


def shape(dims, dtype):
    return jax.ShapeDtypeStruct(dims, dtype)


def exchange(value, axis, count, distance):
    return lax.ppermute(value, axis, [(at, at ^ distance) for at in range(count)])


def digits(count):
    groups, stride = [], 1
    while stride < count:
        size = 4 if count // stride % 4 == 0 else 2
        groups.append((stride, size))
        stride *= size
    return groups


def partners(value, axis, count, stride, size):
    return [value] + [exchange(value, axis, count, step * stride) for step in range(1, size)]


def sum_over(value, axis, count):
    for stride, size in digits(count):
        value = tree_sum(partners(value, axis, count, stride, size))
    return value


def shards(
    tokens,
    cotangent,
    region_ids,
    rel_bucket,
    norm_gain,
    in_weight,
    out_weight,
    bias_table,
    in_error,
    out_error,
    in_basis,
    out_basis,
):
    n_dp = lax.axis_size("dp")
    n_mp = lax.axis_size("mp")
    window_count, span, features = tokens.shape
    head_count, buckets = bias_table.shape
    rank = in_basis.shape[2]
    row_count = window_count * span
    row_block = in_weight.shape[0]
    wide = in_weight.shape[1]
    both = wide + features
    padded = -(-buckets // LANES) * LANES
    blocks = 2 if n_mp == 2 else 1
    me = jnp.stack([lax.axis_index("mp"), lax.axis_index("dp") & 3]).astype(jnp.int32)
    token_rows = tokens.reshape(row_count, features)
    cot_rows = cotangent.reshape(row_count, features)
    gain = norm_gain.reshape(1, features)

    in_basis_t = jnp.swapaxes(in_basis[0], 0, 1)
    out_basis_t = jnp.swapaxes(out_basis[0], 0, 1)
    if blocks == 2:
        own = (in_weight, out_weight, in_basis_t, out_basis_t)
        arrived = [exchange(array, "mp", n_mp, 1) for array in own]
    else:
        own = (
            lax.all_gather(in_weight, "mp", axis=0, tiled=True),
            lax.all_gather(out_weight, "mp", axis=0, tiled=True),
            in_basis_t,
            out_basis_t,
        )
        arrived = []
    width = features // blocks

    operands = (
        rel_bucket,
        bias_table,
        token_rows,
        gain,
        own[0],
        cot_rows,
        region_ids,
        *own[1:],
        in_error[0],
        out_error[0],
    )
    normed, part, bias, index_t, table_pad, bucket, *kept = call(
        functools.partial(prepare_kernel, blocks, READY_HEADS),
        (
            shape((row_count, features), BF16),
            shape((row_count, wide), F32),
            shape((READY_HEADS, span, span), F32),
            shape((span, span), jnp.int32),
            shape((head_count, padded), F32),
            shape((span, span), jnp.int32),
        )
        + tuple(shape(array.shape, array.dtype) for array in operands[2:]),
        [pltpu.VMEM(bias_table.shape, F32), pltpu.SemaphoreType.DMA((12,))],
        flops=2 * row_count * width * wide,
        moved=4 << 20,
        in_specs=[SMEM] + [HBM] * 12,
        out_specs=[VMEM] * 16,
    )(me, *in_hbm(*operands))
    token_rows, gain, w_in_own, cot_rows, region, *own, in_errors, out_errors = kept
    in_basis_t, out_basis_t = own[1:]

    left_shape = shape((2 * rank, width), F32)
    outputs = call(
        functools.partial(attend_kernel, blocks, 1.0 / n_mp),
        (shape((width, both), BF16),) * blocks
        + (left_shape,) * blocks
        + (shape((head_count, span // blocks, span), F32),) * blocks
        + (shape((row_count, wide), BF16), shape((SUBLANES, LANES), F32)),
        [
            pltpu.VMEM((row_count, wide), BF16),
            pltpu.VMEM((row_count, features), BF16),
            pltpu.VMEM((row_count, features), BF16),
            pltpu.VMEM((head_count, span, span), F32),
            pltpu.VMEM((1, features), F32),
            pltpu.VMEM((head_count, span, span), F32),
        ],
        flops=4 * row_count * features * both,
        moved=8 << 20,
        in_specs=[SMEM] + [VMEM] * (13 + len(arrived)),
        out_specs=[VMEM] * (3 * blocks + 2),
    )(me, normed, part, bias, index_t, table_pad, bucket, gain, cot_rows, region, w_in_own, *own, *arrived)
    terms, lefts, score_parts = (
        outputs[at * blocks : (at + 1) * blocks] for at in range(3)
    )
    packed, gain_term = outputs[3 * blocks :]

    if blocks == 2:
        left_other = exchange(lefts[1], "mp", n_mp, 1)
        left = lefts[0]
    else:
        term_parts = [lax.psum_scatter(terms[0], "mp", scatter_dimension=0, tiled=True)]
        left = call(
            functools.partial(shard_kernel, 1.0 / n_mp),
            shape((2 * rank, row_block), F32),
            in_specs=[VMEM] * 3,
            out_specs=VMEM,
        )(term_parts[0], in_basis_t, out_basis_t)

    left = call(
        error_kernel,
        shape((2 * rank, row_block), F32),
        flops=8 * row_block * both * rank,
        moved=3 << 20,
        in_specs=[VMEM] * 5,
        out_specs=VMEM,
    )(left, in_errors, out_errors, in_basis_t, out_basis_t)
    if blocks == 2:
        left, term_sent, score_sent = call(
            join_kernel,
            tuple(shape(array.shape, array.dtype) for array in (left, terms[1], score_parts[1])),
            in_specs=[VMEM] * 2 + [ANY] * 2,
            out_specs=[VMEM] + [ANY] * 2,
            input_output_aliases={2: 1, 3: 2},
        )(left, left_other, terms[1], score_parts[1])
        score_parts = [score_parts[0], exchange(score_sent, "mp", n_mp, 1)]
        term_parts = [terms[0], exchange(term_sent, "mp", n_mp, 1)]

    stats = call(
        functools.partial(table_kernel, blocks),
        shape((head_count, padded + 2 * LANES), F32),
        flops=2 * row_count * features * wide,
        moved=4 << 20,
        in_specs=[SMEM] + [VMEM] * (blocks + 2),
        out_specs=VMEM,
    )(me, *score_parts, gain_term, index_t)

    if blocks == 2:
        stats = [stats, exchange(stats, "mp", n_mp, 1)]
    else:
        stats = [sum_over(stats, "mp", n_mp)]

    groups = digits(n_dp)
    for group in groups[:0:-1]:
        left = call(
            functools.partial(add_kernel, group[1]),
            shape(left.shape, F32),
            in_specs=[VMEM] * (group[1] + 1),
            out_specs=VMEM,
        )(*partners(left, "dp", n_dp, *group), stats[-1])
    stride, parts = groups[0]
    lefts = partners(left, "dp", n_dp, stride, parts)
    merged = call(
        functools.partial(merge_kernel, 1.0 / n_mp, len(term_parts)),
        shape((row_block, both), F32),
        flops=4 * row_block * both,
        moved=6 << 20,
        in_specs=[VMEM] * (len(term_parts) + 2),
        out_specs=VMEM,
    )(*term_parts, in_errors, out_errors)

    quarter = both // parts
    piece = shape((rank, quarter + LANES), BF16)
    ortho, *pieces = call(
        functools.partial(ortho_kernel, 1.0 / n_dp, len(lefts), len(stats)),
        (shape((2 * rank, row_block), F32),) + (piece,) * parts,
        [pltpu.VMEM((head_count, padded + 2 * LANES), F32)],
        flops=12 * row_block * both * rank,
        moved=3 << 20,
        in_specs=[SMEM] + [VMEM] * (len(lefts) + len(stats) + 1),
        out_specs=[VMEM] * (1 + parts),
    )(me, *lefts, *stats, merged)

    token_grad, flag = call(
        functools.partial(token_kernel, blocks),
        (shape((row_count, features), BF16), shape((SUBLANES, LANES), F32)),
        [
            pltpu.VMEM((row_count, features), F32),
            pltpu.VMEM((row_count, features), BF16),
            pltpu.SemaphoreType.DMA((1,)),
        ],
        flops=2 * row_count * features * wide,
        moved=4 << 20,
        in_specs=[SMEM] + [VMEM] * (blocks + 5),
        out_specs=[HBM, VMEM],
    )(me, packed, w_in_own, *arrived[:1], token_rows, cot_rows, gain, ortho)

    def reduced(values):
        return call(
            reduce_kernel,
            piece,
            in_specs=[VMEM] * (len(values) + 1),
            out_specs=VMEM,
            moved=1 << 18,
        )(*values, flag)

    held = reduced(
        [pieces[0]]
        + [exchange(pieces[step], "dp", n_dp, step * stride) for step in range(1, parts)]
    )
    for group in groups[1:]:
        held = reduced(partners(held, "dp", n_dp, *group))
    pieces = partners(held, "dp", n_dp, stride, parts)

    small = (
        shape((rank, wide), F32),
        shape((rank, features), F32),
        shape((head_count, buckets), F32),
        shape((1, features), F32),
    )
    in_update, out_update, in_new_error, out_new_error, in_right, out_right, table, gain = call(
        functools.partial(update_kernel, 1.0 / n_dp, 1.0 / (n_dp * n_mp), parts),
        (
            shape((row_block, wide), F32),
            shape((row_block, features), F32),
            shape((row_block, wide), F32),
            shape((row_block, features), F32),
            *small,
        ),
        [
            pltpu.VMEM((parts, rank, quarter + LANES), F32),
            pltpu.VMEM((parts, row_block, quarter), F32),
            pltpu.VMEM((parts, row_block, quarter), F32),
            pltpu.SemaphoreType.DMA((parts, 2)),
        ]
        + buffers(*small),
        flops=12 * row_block * both * rank,
        moved=8 << 20,
        in_specs=[SMEM] + [VMEM] * (parts + 2),
        out_specs=[HBM] * 8,
    )(me, *pieces, ortho, merged)

    return (
        token_grad.reshape(tokens.shape),
        gain.reshape(features),
        table,
        in_update,
        out_update,
        in_new_error[None],
        out_new_error[None],
        jnp.swapaxes(in_right, 0, 1)[None],
        jnp.swapaxes(out_right, 0, 1)[None],
    )


def solution(mesh):
    placed = (
        P(("dp", "mp"), None, None),
        P(("dp", "mp"), None, None),
        P(("dp", "mp"), None),
        P(),
        P(),
        P("mp", None),
        P("mp", None),
        P(),
        P("dp", "mp", None),
        P("dp", "mp", None),
        P("mp", None, None),
        P("mp", None, None),
    )
    return jax.shard_map(
        shards,
        mesh=mesh,
        in_specs=placed,
        out_specs=(
            P(("dp", "mp"), None, None),
            P(),
            P(),
            P("mp", None),
            P("mp", None),
            P("dp", "mp", None),
            P("dp", "mp", None),
            P("mp", None, None),
            P("mp", None, None),
        ),
        check_vma=False,
    )
```

time: 626 us -> 62.4 us (0.10)
  waiting for transfers between devices: 203 us -> 13.7 us
  other arithmetic: 129 us -> 0.07 us
  matrix products: 105 us -> 0 us
  local copies, waits for them, and re-layouts: 76.8 us -> 0 us
  blocking collectives: 49.4 us -> 0 us
  loops' own time: 46.1 us -> 0 us
  Pallas kernels: 0 us -> 24.6 us
  starting transfers between devices: 0.6 us -> 22.8 us
  between operations: 14.3 us -> 0.93 us
    psum x2 -> x0, waiting for transfers between devices: 203 us -> none  [the longest x1 102 us: shards(): lax.psum((right_term(in_merged, in_ortho), right_term(out_merged, out_ort...]
    scatter-add x1 -> x0, other arithmetic: 113 us -> none  [attention_backward(): jax.ops.segment_sum(score_sum.T, rel_bucket.reshape(-1), num_segments=tab...]
    dot_general x272 -> x0, matrix products: 101 us -> none  [the longest x128 57.8 us: next_column(): jnp.dot(finished, jnp.dot(finished.T, column, precision=HIGH), precision=...]
    gather x2 -> x0, local copies, waits for them, and re-layouts: 50.2 us -> none  [attention_forward(): pos_bias = jnp.take(bias_table, rel_bucket, axis=1)]
    psum x1 -> x0, blocking collectives: 46.9 us -> none  [shards(): gain_total, table_total = lax.psum((gain_term, table_term), ('dp', 'mp'))]
    another operation x2 -> x0, loops' own time: 46.1 us -> none  [orthonormal(): lax.fori_loop(0, left_factor.shape[1], next_column, jnp.zeros_like(left_f...]
    pallas_call x0 -> x12, Pallas kernels: none -> 24.6 us  [the longest x1 7.78 us: shards(): call(functools.partial(attend_kernel, blocks, 1.0 / n_mp), (shape((width,...]
    ppermute x0 -> x23, starting transfers between devices: none -> 22.8 us  [exchange(): lax.ppermute(value, axis, [(at, at ^ distance) for at in range(count)])]
  transfers between devices with their start and end apart: 5 -> 23, of which waited for: 2 -> 11; matrix products, arithmetic and copies ran while one was open for 32% -> 0% of each run, Pallas kernels for 0% -> 15%
where the time goes in v1:
time: 62.4 us; the launch traced here: 62.2 us
  Pallas kernels  24.6 us (39%)
  starting transfers between devices  22.8 us (37%)
  waiting for transfers between devices  13.7 us (22%)
  between operations  0.93 us (1%)
    ppermute x23, starting transfers between devices, exchange(): lax.ppermute(value, axis, [(at, at ^ distance) for at in range(count)])  22.8 us
    ppermute x23, waiting for transfers between devices, exchange(): lax.ppermute(value, axis, [(at, at ^ distance) for at in range(count)])  13.7 us
    pallas_call x1, Pallas kernels, shards(): call(functools.partial(attend_kernel, blocks, 1.0 / n_mp), (shape((width,...  7.78 us
    pallas_call x1, Pallas kernels, shards(): call(functools.partial(ortho_kernel, 1.0 / n_dp, len(lefts), len(stats)),...  4.34 us
    pallas_call x1, Pallas kernels, shards(): call(functools.partial(prepare_kernel, blocks, READY_HEADS), (shape((row_...  3.12 us
    pallas_call x1, Pallas kernels, shards(): call(functools.partial(table_kernel, blocks), shape((head_count, padded +...  3.06 us
    pallas_call x1, Pallas kernels, shards(): call(functools.partial(update_kernel, 1.0 / n_dp, 1.0 / (n_dp * n_mp), pa...  2.94 us
    pallas_call x1, Pallas kernels, shards(): call(functools.partial(token_kernel, blocks), (shape((row_count, features...  2.22 us
  transfers between devices with their start and end apart: 23, of which 11 were waited for; matrix products, arithmetic and copies ran while one was open for 0% of the time, Pallas kernels for 15%

profile of v1, /device:TPU:0, one launch (start us, length us, event | category | flops | bytes accessed | tf_op | source)
XLA Modules:
  0.0 62.2 jit_solution(5417447549763514892)
XLA Ops:
  0.6 0.5 collective-permute-start
  1.2 0.4 collective-permute-start.2
  1.8 3.1 %shard_map.187 = (bf16[288,512]{1,0:T(8,128)(2,1)S(1)}, f32[288,1536]{1,0:T(8,128)S(1)}, f32[2,144,144]{2,1,0:T(8,128)S(1)}, s32[144,144]{1,0:T(8,128)S(1)}, f32...) custom-call(s32[2]{0:T(128)S(1)} %pad_add_fusion.me_ref.refs_0_, ...), custom_call_target="tpu_custom_call" | custom-call | flops 226492416 | bytes 4194304 | tf_op jit(solution)/shard_map/pallas_call | solution.py:599
  5.0 7.8 %shard_map.188 = (bf16[256,2048]{1,0:T(8,128)(2,1)S(1)}, bf16[256,2048]{1,0:T(8,128)(2,1)S(1)}, f32[64,256]{1,0:T(8,128)S(1)}, f32[64,256]{1,0:T(8,128)S(1)}, f3...) custom-call(s32[2]{0:T(128)S(1)} %pad_add_fusion.me_ref.refs_0_, ...), custom_call_target="tpu_custom_call" | custom-call | flops 1207959552 | bytes 8388608 | tf_op jit(solution)/shard_map/pallas_call | solution.py:620
  13.2 0.8 %shard_map.189.left_own = f32[64,256]{1,0:T(8,128)S(1)} custom-call(f32[64,256]{1,0:T(8,128)S(1)} %get-tuple-element.66.term_left, f32[256,1536]{1,0:T(8,128)S(1)} %get-tuple-element.67.in_error.refs_2_, f32[256,512]{1,0:T(8,128)S(1)} %get-tuple-element.68.out_error.refs_3_, f32[32,1536]{1,0:T(8,128)S(1)} %get-tuple-element.62.refs_12_.in_basis, ...), custom_call_target="tpu_custom_call" | custom-call | flops 134217728 | bytes 3145728 | tf_op jit(solution)/shard_map/pallas_call | solution.py:656
  14.7 5.0 %collective-permute-start.7 = (f32[64,256]{1,0:T(8,128)S(1)}, f32[64,256]{1,0:T(8,128)S(1)}, u32[]{:S(2)}, u32[]{:S(2)}) collective-permute-start(f32[64,256]{1,0:T(8,128)S(1)} %get-tuple-element.72.refs_0_), channel_id=1, source_target_pairs={{0,24},{2,26},{4,28},{6,30},{8,16},{10,18},{12,20},{14,22},{16,8},... | collective-permute-start | bytes 196616 | tf_op jit(solution)/shard_map/ppermute | solution.py:520
  19.7 0.6 collective-permute-start.5
  20.2 3.1 %shard_map.191.refs_4_ = f32[8,1024]{1,0:T(8,128)S(1)} custom-call(s32[2]{0:T(128)S(1)} %pad_add_fusion.me_ref.refs_0_, f32[8,72,144]{2,1,0:T(8,128)S(1)} %get-tuple-element.73.refs_0_, f32[8,72,144]{2,1,0:T(8,128)S(1)} %collective-permute-done.8.refs_1_, f32[8,128]{1,0:T(8,128)S(1)} %get-tuple-element.75.refs_2_, ...), custom_call_target="tpu_custom_call" | custom-call | flops 452984832 | bytes 4194304 | tf_op jit(solution)/shard_map/pallas_call | solution.py:675
  23.4 2.2 %collective-permute-done.6.refs_2_ = f32[64,256]{1,0:T(8,128)S(1)} collective-permute-done((f32[64,256]{1,0:T(8,128)S(1)}, f32[64,256]{1,0:T(8,128)S(1)}, u32[]{:S(2)}, u32[]{:S(2)}) %collective-permute-start.6) | collective-permute-done | bytes 65568 | tf_op jit(solution)/shard_map/ppermute | solution.py:520
  25.6 2.5 %collective-permute-start.12 = (f32[64,256]{1,0:T(8,128)S(1)}, f32[64,256]{1,0:T(8,128)S(1)}, u32[]{:S(2)}, u32[]{:S(2)}) collective-permute-start(f32[64,256]{1,0:T(8,128)S(1)} %shard_map.192.refs_0_), channel_id=1, source_target_pairs={{0,6},{2,4},{4,2},{6,0},{8,14},{10,12},{12,10},{14,8},{16,22},{18,... | collective-permute-start | bytes 196616 | tf_op jit(solution)/shard_map/ppermute | solution.py:520
  28.1 0.5 collective-permute-start.11
  28.6 0.5 collective-permute-start.10
  29.5 1.4 %collective-permute-done.12.refs_3_ = f32[64,256]{1,0:T(8,128)S(1)} collective-permute-done((f32[64,256]{1,0:T(8,128)S(1)}, f32[64,256]{1,0:T(8,128)S(1)}, u32[]{:S(2)}, u32[]{:S(2)}) %collective-permute-start.12) | collective-permute-done | bytes 65568 | tf_op jit(solution)/shard_map/ppermute | solution.py:520
  30.9 1.4 %collective-permute-done.11.refs_2_ = f32[64,256]{1,0:T(8,128)S(1)} collective-permute-done((f32[64,256]{1,0:T(8,128)S(1)}, f32[64,256]{1,0:T(8,128)S(1)}, u32[]{:S(2)}, u32[]{:S(2)}) %collective-permute-start.11) | collective-permute-done | bytes 65568 | tf_op jit(solution)/shard_map/ppermute | solution.py:520
  32.4 0.5 collective-permute-done.10.refs_1_
  32.9 4.3 %shard_map.194 = (f32[64,256]{1,0:T(8,128)S(1)}, bf16[32,640]{1,0:T(8,128)(2,1)S(1)}, bf16[32,640]{1,0:T(8,128)(2,1)S(1)}, bf16[32,640]{1,0:T(8,128)(2,1)S(1)}, bf16[32,640]{1,0:T(8,128)(2,1)S(1)}) custom-call(s32[2]{0:T(128)S(1)} %pad_add_fusion.me_ref.refs_0_, f32[64,256]{1,0:T(8,128)S(1)} %shard_map.192.refs_0_, ...), custom_call_target="tpu_custom_call" | custom-call | flops 201326592 | bytes 3145728 | tf_op jit(solution)/shard_map/pallas_call | solution.py:710
  37.2 0.6 collective-permute-start.14
  37.8 1.5 %collective-permute-start.15 = (bf16[32,640]{1,0:T(8,128)(2,1)S(1)}, bf16[32,640]{1,0:T(8,128)(2,1)S(1)}, u32[]{:S(2)}, u32[]{:S(2)}) collective-permute-start(bf16[32,640]{1,0:T(8,128)(2,1)S(1)} %get-tuple-element.82), channel_id=1, source_target_pairs={{0,4},{2,6},{4,0},{6,2},{8,12},{10,14},{12,8},{14,10},{16,20},{18,... | collective-permute-start | bytes 122888 | tf_op jit(solution)/shard_map/ppermute | solution.py:520
  39.3 1.4 %collective-permute-start.16 = (bf16[32,640]{1,0:T(8,128)(2,1)S(1)}, bf16[32,640]{1,0:T(8,128)(2,1)S(1)}, u32[]{:S(2)}, u32[]{:S(2)}) collective-permute-start(bf16[32,640]{1,0:T(8,128)(2,1)S(1)} %get-tuple-element.83), channel_id=1, source_target_pairs={{0,6},{2,4},{4,2},{6,0},{8,14},{10,12},{12,10},{14,8},{16,22},{18,... | collective-permute-start | bytes 122888 | tf_op jit(solution)/shard_map/ppermute | solution.py:520
  40.7 2.2 %shard_map.195 = (bf16[288,512]{1,0:T(8,128)(2,1)}, f32[8,128]{1,0:T(8,128)S(1)}) custom-call(s32[2]{0:T(128)S(1)} %pad_add_fusion.me_ref.refs_0_, bf16[288,1536]{1,0:T(8,128)(2,1)S(1)} %get-tuple-element.64.packed, bf16[256,1536]{1,0:T(8,128)(2,1)S(1)} %get-tuple-element.60.refs_10_.refs_0_, bf16[256,1536]{1,0:T(8,128)(2,1)S(1)} %collective-permute-done.refs_14_.refs_1_, ...), custom_call_target="tpu_custom_call" | custom-call | flops 452984832 | bytes 4194304 | tf_op jit(solution)/shard_map/pallas_call | solution.py:720
  43.0 1.2 %collective-permute-done.16.refs_3_ = bf16[32,640]{1,0:T(8,128)(2,1)S(1)} collective-permute-done((bf16[32,640]{1,0:T(8,128)(2,1)S(1)}, bf16[32,640]{1,0:T(8,128)(2,1)S(1)}, u32[]{:S(2)}, u32[]{:S(2)}) %collective-permute-start.16) | collective-permute-done | bytes 40992 | tf_op jit(solution)/shard_map/ppermute | solution.py:520
  44.2 2.9 %collective-permute-start.19 = (bf16[32,640]{1,0:T(8,128)(2,1)S(1)}, bf16[32,640]{1,0:T(8,128)(2,1)S(1)}, u32[]{:S(2)}, u32[]{:S(2)}) collective-permute-start(bf16[32,640]{1,0:T(8,128)(2,1)S(1)} %shard_map.196.refs_0_), channel_id=1, source_target_pairs={{0,24},{2,26},{4,28},{6,30},{8,16},{10,18},{12,20},{14,22},{16,8},... | collective-permute-start | bytes 122888 | tf_op jit(solution)/shard_map/ppermute | solution.py:520
  47.2 1.5 %collective-permute-start.17 = (bf16[32,640]{1,0:T(8,128)(2,1)S(1)}, bf16[32,640]{1,0:T(8,128)(2,1)S(1)}, u32[]{:S(2)}, u32[]{:S(2)}) collective-permute-start(bf16[32,640]{1,0:T(8,128)(2,1)S(1)} %shard_map.196.refs_0_), channel_id=1, source_target_pairs={{0,8},{2,10},{4,12},{6,14},{8,0},{10,2},{12,4},{14,6},{16,24},{18,... | collective-permute-start | bytes 122888 | tf_op jit(solution)/shard_map/ppermute | solution.py:520
  48.7 1.4 %collective-permute-done.19.refs_3_ = bf16[32,640]{1,0:T(8,128)(2,1)S(1)} collective-permute-done((bf16[32,640]{1,0:T(8,128)(2,1)S(1)}, bf16[32,640]{1,0:T(8,128)(2,1)S(1)}, u32[]{:S(2)}, u32[]{:S(2)}) %collective-permute-start.19) | collective-permute-done | bytes 40992 | tf_op jit(solution)/shard_map/ppermute | solution.py:520
  50.1 1.9 %collective-permute-done.18.refs_2_ = bf16[32,640]{1,0:T(8,128)(2,1)S(1)} collective-permute-done((bf16[32,640]{1,0:T(8,128)(2,1)S(1)}, bf16[32,640]{1,0:T(8,128)(2,1)S(1)}, u32[]{:S(2)}, u32[]{:S(2)}) %collective-permute-start.18) | collective-permute-done | bytes 40992 | tf_op jit(solution)/shard_map/ppermute | solution.py:520
  52.1 1.5 %collective-permute-start.22 = (bf16[32,640]{1,0:T(8,128)(2,1)S(1)}, bf16[32,640]{1,0:T(8,128)(2,1)S(1)}, u32[]{:S(2)}, u32[]{:S(2)}) collective-permute-start(bf16[32,640]{1,0:T(8,128)(2,1)S(1)} %shard_map.197.refs_0_), channel_id=1, source_target_pairs={{0,6},{2,4},{4,2},{6,0},{8,14},{10,12},{12,10},{14,8},{16,22},{18,... | collective-permute-start | bytes 122888 | tf_op jit(solution)/shard_map/ppermute | solution.py:520
  53.6 1.5 %collective-permute-start.21 = (bf16[32,640]{1,0:T(8,128)(2,1)S(1)}, bf16[32,640]{1,0:T(8,128)(2,1)S(1)}, u32[]{:S(2)}, u32[]{:S(2)}) collective-permute-start(bf16[32,640]{1,0:T(8,128)(2,1)S(1)} %shard_map.197.refs_0_), channel_id=1, source_target_pairs={{0,4},{2,6},{4,0},{6,2},{8,12},{10,14},{12,8},{14,10},{16,20},{18,... | collective-permute-start | bytes 122888 | tf_op jit(solution)/shard_map/ppermute | solution.py:520
  55.1 0.5 collective-permute-start.20
  55.6 1.4 %collective-permute-done.22.refs_3_ = bf16[32,640]{1,0:T(8,128)(2,1)S(1)} collective-permute-done((bf16[32,640]{1,0:T(8,128)(2,1)S(1)}, bf16[32,640]{1,0:T(8,128)(2,1)S(1)}, u32[]{:S(2)}, u32[]{:S(2)}) %collective-permute-start.22) | collective-permute-done | bytes 40992 | tf_op jit(solution)/shard_map/ppermute | solution.py:520
  57.1 0.5 collective-permute-done.21.refs_2_
  57.6 1.5 %collective-permute-done.20.refs_1_ = bf16[32,640]{1,0:T(8,128)(2,1)S(1)} collective-permute-done((bf16[32,640]{1,0:T(8,128)(2,1)S(1)}, bf16[32,640]{1,0:T(8,128)(2,1)S(1)}, u32[]{:S(2)}, u32[]{:S(2)}) %collective-permute-start.20) | collective-permute-done | bytes 40992 | tf_op jit(solution)/shard_map/ppermute | solution.py:520
  59.1 2.9 %shard_map.198 = (f32[256,1536]{1,0:T(8,128)}, f32[256,512]{1,0:T(8,128)}, f32[256,1536]{1,0:T(8,128)}, f32[256,512]{1,0:T(8,128)}, f32[32,1536]{1,0:T(8,128)}, ...) custom-call(s32[2]{0:T(128)S(1)} %pad_add_fusion.me_ref.refs_0_, bf16[32,640]{1,0:T(8,128)(2,1)S(1)} %shard_map.197.refs_0_, ...), custom_call_target="tpu_custom_call" | custom-call | flops 201326592 | bytes 8388608 | tf_op jit(solution)/shard_map/pallas_call | solution.py:757
  (27 shorter events, 1.9 us)
Async XLA Ops:
  0.6 4.4 %collective-permute-start = (bf16[256,1536]{1,0:T(8,128)(2,1)}, bf16[256,1536]{1,0:T(8,128)(2,1)S(1)}, u32[]{:S(2)}, u32[]{:S(2)}) collective-permute-start(bf16[256,1536]{1,0:T(8,128)(2,1)} %refs_4_.1), channel_id=1, source_target_pairs={{0,1},{1,0},{2,3},{3,2},{4,5},{5,4},{6,7},{7,6},{8,9},{9,8},{10,11... | collective-permute-start | bytes 2359304 | tf_op jit(solution)/shard_map/ppermute | solution.py:520
  1.2 3.8 %collective-permute-start.1 = (bf16[256,512]{1,0:T(8,128)(2,1)}, bf16[256,512]{1,0:T(8,128)(2,1)S(1)}, u32[]{:S(2)}, u32[]{:S(2)}) collective-permute-start(bf16[256,512]{1,0:T(8,128)(2,1)} %refs_7_.1), channel_id=1, source_target_pairs={{0,1},{1,0},{2,3},{3,2},{4,5},{5,4},{6,7},{7,6},{8,9},{9,8},{10,11... | collective-permute-start | bytes 786440 | tf_op jit(solution)/shard_map/ppermute | solution.py:520
  1.2 3.7 %collective-permute-start.2 = (f32[32,1536]{1,0:T(8,128)}, f32[32,1536]{1,0:T(8,128)S(1)}, u32[]{:S(2)}, u32[]{:S(2)}) collective-permute-start(f32[32,1536]{1,0:T(8,128)} %bitcast.27), channel_id=1, source_target_pairs={{0,1},{1,0},{2,3},{3,2},{4,5},{5,4},{6,7},{7,6},{8,9},{9,8},{10,11... | collective-permute-start | bytes 589832 | tf_op jit(solution)/shard_map/ppermute | solution.py:520
  1.7 3.3 %collective-permute-start.3 = (f32[32,512]{1,0:T(8,128)}, f32[32,512]{1,0:T(8,128)S(1)}, u32[]{:S(2)}, u32[]{:S(2)}) collective-permute-start(f32[32,512]{1,0:T(8,128)} %bitcast.29), channel_id=1, source_target_pairs={{0,1},{1,0},{2,3},{3,2},{4,5},{5,4},{6,7},{7,6},{8,9},{9,8},{10,11... | collective-permute-start | bytes 196616 | tf_op jit(solution)/shard_map/ppermute | solution.py:520
  12.8 1.3 %collective-permute-start.4 = (f32[64,256]{1,0:T(8,128)S(1)}, f32[64,256]{1,0:T(8,128)S(1)}, u32[]{:S(2)}, u32[]{:S(2)}) collective-permute-start(f32[64,256]{1,0:T(8,128)S(1)} %get-tuple-element.69), channel_id=1, source_target_pairs={{0,1},{1,0},{2,3},{3,2},{4,5},{5,4},{6,7},{7,6},{8,9},{9,8},{10,11... | collective-permute-start | bytes 196616 | tf_op jit(solution)/shard_map/ppermute | solution.py:520
  14.1 15.0 %collective-permute-start.13 = (bf16[256,2048]{1,0:T(8,128)(2,1)S(1)}, bf16[256,2048]{1,0:T(8,128)(2,1)S(1)}, u32[]{:S(2)}, u32[]{:S(2)}) collective-permute-start(bf16[256,2048]{1,0:T(8,128)(2,1)S(1)} %get-tuple-element.77), channel_id=1, source_target_pairs={{0,1},{1,0},{2,3},{3,2},{4,5},{5,4},{6,7},{7,6},{8,9},{9,8},{10,11... | collective-permute-start | bytes 3145736 | tf_op jit(solution)/shard_map/ppermute | solution.py:520
  14.5 5.7 %collective-permute-start.8 = (f32[8,72,144]{2,1,0:T(8,128)S(1)}, f32[8,72,144]{2,1,0:T(8,128)S(1)}, u32[]{:S(2)}, u32[]{:S(2)}) collective-permute-start(f32[8,72,144]{2,1,0:T(8,128)S(1)} %get-tuple-element.74), channel_id=1, source_target_pairs={{0,1},{1,0},{2,3},{3,2},{4,5},{5,4},{6,7},{7,6},{8,9},{9,8},{10,11... | collective-permute-start | bytes 995336 | tf_op jit(solution)/shard_map/ppermute | solution.py:520
  14.7 8.7 %collective-permute-start.7 = (f32[64,256]{1,0:T(8,128)S(1)}, f32[64,256]{1,0:T(8,128)S(1)}, u32[]{:S(2)}, u32[]{:S(2)}) collective-permute-start(f32[64,256]{1,0:T(8,128)S(1)} %get-tuple-element.72.refs_0_), channel_id=1, source_target_pairs={{0,24},{2,26},{4,28},{6,30},{8,16},{10,18},{12,20},{14,22},{16,8},... | collective-permute-start | bytes 196616 | tf_op jit(solution)/shard_map/ppermute | solution.py:520
  19.7 5.9 %collective-permute-start.6 = (f32[64,256]{1,0:T(8,128)S(1)}, f32[64,256]{1,0:T(8,128)S(1)}, u32[]{:S(2)}, u32[]{:S(2)}) collective-permute-start(f32[64,256]{1,0:T(8,128)S(1)} %get-tuple-element.72.refs_0_), channel_id=1, source_target_pairs={{0,16},{2,18},{4,20},{6,22},{8,24},{10,26},{12,28},{14,30},{16,0},... | collective-permute-start | bytes 196616 | tf_op jit(solution)/shard_map/ppermute | solution.py:520
  19.7 5.9 %collective-permute-start.5 = (f32[64,256]{1,0:T(8,128)S(1)}, f32[64,256]{1,0:T(8,128)S(1)}, u32[]{:S(2)}, u32[]{:S(2)}) collective-permute-start(f32[64,256]{1,0:T(8,128)S(1)} %get-tuple-element.72.refs_0_), channel_id=1, source_target_pairs={{0,8},{2,10},{4,12},{6,14},{8,0},{10,2},{12,4},{14,6},{16,24},{18,... | collective-permute-start | bytes 196616 | tf_op jit(solution)/shard_map/ppermute | solution.py:520
  23.3 2.3 %collective-permute-start.9 = (f32[8,1024]{1,0:T(8,128)S(1)}, f32[8,1024]{1,0:T(8,128)S(1)}, u32[]{:S(2)}, u32[]{:S(2)}) collective-permute-start(f32[8,1024]{1,0:T(8,128)S(1)} %shard_map.191.refs_4_), channel_id=1, source_target_pairs={{0,1},{1,0},{2,3},{3,2},{4,5},{5,4},{6,7},{7,6},{8,9},{9,8},{10,11... | collective-permute-start | bytes 98312 | tf_op jit(solution)/shard_map/ppermute | solution.py:520
  25.6 5.3 %collective-permute-start.12 = (f32[64,256]{1,0:T(8,128)S(1)}, f32[64,256]{1,0:T(8,128)S(1)}, u32[]{:S(2)}, u32[]{:S(2)}) collective-permute-start(f32[64,256]{1,0:T(8,128)S(1)} %shard_map.192.refs_0_), channel_id=1, source_target_pairs={{0,6},{2,4},{4,2},{6,0},{8,14},{10,12},{12,10},{14,8},{16,22},{18,... | collective-permute-start | bytes 196616 | tf_op jit(solution)/shard_map/ppermute | solution.py:520
  28.1 4.3 %collective-permute-start.11 = (f32[64,256]{1,0:T(8,128)S(1)}, f32[64,256]{1,0:T(8,128)S(1)}, u32[]{:S(2)}, u32[]{:S(2)}) collective-permute-start(f32[64,256]{1,0:T(8,128)S(1)} %shard_map.192.refs_0_), channel_id=1, source_target_pairs={{0,4},{2,6},{4,0},{6,2},{8,12},{10,14},{12,8},{14,10},{16,20},{18,... | collective-permute-start | bytes 196616 | tf_op jit(solution)/shard_map/ppermute | solution.py:520
  28.6 4.3 %collective-permute-start.10 = (f32[64,256]{1,0:T(8,128)S(1)}, f32[64,256]{1,0:T(8,128)S(1)}, u32[]{:S(2)}, u32[]{:S(2)}) collective-permute-start(f32[64,256]{1,0:T(8,128)S(1)} %shard_map.192.refs_0_), channel_id=1, source_target_pairs={{0,2},{2,0},{4,6},{6,4},{8,10},{10,8},{12,14},{14,12},{16,18},{18,... | collective-permute-start | bytes 196616 | tf_op jit(solution)/shard_map/ppermute | solution.py:520
  37.2 5.8 %collective-permute-start.14 = (bf16[32,640]{1,0:T(8,128)(2,1)S(1)}, bf16[32,640]{1,0:T(8,128)(2,1)S(1)}, u32[]{:S(2)}, u32[]{:S(2)}) collective-permute-start(bf16[32,640]{1,0:T(8,128)(2,1)S(1)} %get-tuple-element.81), channel_id=1, source_target_pairs={{0,2},{2,0},{4,6},{6,4},{8,10},{10,8},{12,14},{14,12},{16,18},{18,... | collective-permute-start | bytes 122888 | tf_op jit(solution)/shard_map/ppermute | solution.py:520
  37.8 5.2 %collective-permute-start.15 = (bf16[32,640]{1,0:T(8,128)(2,1)S(1)}, bf16[32,640]{1,0:T(8,128)(2,1)S(1)}, u32[]{:S(2)}, u32[]{:S(2)}) collective-permute-start(bf16[32,640]{1,0:T(8,128)(2,1)S(1)} %get-tuple-element.82), channel_id=1, source_target_pairs={{0,4},{2,6},{4,0},{6,2},{8,12},{10,14},{12,8},{14,10},{16,20},{18,... | collective-permute-start | bytes 122888 | tf_op jit(solution)/shard_map/ppermute | solution.py:520
  39.3 4.9 %collective-permute-start.16 = (bf16[32,640]{1,0:T(8,128)(2,1)S(1)}, bf16[32,640]{1,0:T(8,128)(2,1)S(1)}, u32[]{:S(2)}, u32[]{:S(2)}) collective-permute-start(bf16[32,640]{1,0:T(8,128)(2,1)S(1)} %get-tuple-element.83), channel_id=1, source_target_pairs={{0,6},{2,4},{4,2},{6,0},{8,14},{10,12},{12,10},{14,8},{16,22},{18,... | collective-permute-start | bytes 122888 | tf_op jit(solution)/shard_map/ppermute | solution.py:520
  44.2 5.9 %collective-permute-start.19 = (bf16[32,640]{1,0:T(8,128)(2,1)S(1)}, bf16[32,640]{1,0:T(8,128)(2,1)S(1)}, u32[]{:S(2)}, u32[]{:S(2)}) collective-permute-start(bf16[32,640]{1,0:T(8,128)(2,1)S(1)} %shard_map.196.refs_0_), channel_id=1, source_target_pairs={{0,24},{2,26},{4,28},{6,30},{8,16},{10,18},{12,20},{14,22},{16,8},... | collective-permute-start | bytes 122888 | tf_op jit(solution)/shard_map/ppermute | solution.py:520
  47.2 4.9 %collective-permute-start.18 = (bf16[32,640]{1,0:T(8,128)(2,1)S(1)}, bf16[32,640]{1,0:T(8,128)(2,1)S(1)}, u32[]{:S(2)}, u32[]{:S(2)}) collective-permute-start(bf16[32,640]{1,0:T(8,128)(2,1)S(1)} %shard_map.196.refs_0_), channel_id=1, source_target_pairs={{0,16},{2,18},{4,20},{6,22},{8,24},{10,26},{12,28},{14,30},{16,0},... | collective-permute-start | bytes 122888 | tf_op jit(solution)/shard_map/ppermute | solution.py:520
  47.2 4.9 %collective-permute-start.17 = (bf16[32,640]{1,0:T(8,128)(2,1)S(1)}, bf16[32,640]{1,0:T(8,128)(2,1)S(1)}, u32[]{:S(2)}, u32[]{:S(2)}) collective-permute-start(bf16[32,640]{1,0:T(8,128)(2,1)S(1)} %shard_map.196.refs_0_), channel_id=1, source_target_pairs={{0,8},{2,10},{4,12},{6,14},{8,0},{10,2},{12,4},{14,6},{16,24},{18,... | collective-permute-start | bytes 122888 | tf_op jit(solution)/shard_map/ppermute | solution.py:520
  52.1 5.0 %collective-permute-start.22 = (bf16[32,640]{1,0:T(8,128)(2,1)S(1)}, bf16[32,640]{1,0:T(8,128)(2,1)S(1)}, u32[]{:S(2)}, u32[]{:S(2)}) collective-permute-start(bf16[32,640]{1,0:T(8,128)(2,1)S(1)} %shard_map.197.refs_0_), channel_id=1, source_target_pairs={{0,6},{2,4},{4,2},{6,0},{8,14},{10,12},{12,10},{14,8},{16,22},{18,... | collective-permute-start | bytes 122888 | tf_op jit(solution)/shard_map/ppermute | solution.py:520
  53.6 4.0 %collective-permute-start.21 = (bf16[32,640]{1,0:T(8,128)(2,1)S(1)}, bf16[32,640]{1,0:T(8,128)(2,1)S(1)}, u32[]{:S(2)}, u32[]{:S(2)}) collective-permute-start(bf16[32,640]{1,0:T(8,128)(2,1)S(1)} %shard_map.197.refs_0_), channel_id=1, source_target_pairs={{0,4},{2,6},{4,0},{6,2},{8,12},{10,14},{12,8},{14,10},{16,20},{18,... | collective-permute-start | bytes 122888 | tf_op jit(solution)/shard_map/ppermute | solution.py:520
  55.1 4.0 %collective-permute-start.20 = (bf16[32,640]{1,0:T(8,128)(2,1)S(1)}, bf16[32,640]{1,0:T(8,128)(2,1)S(1)}, u32[]{:S(2)}, u32[]{:S(2)}) collective-permute-start(bf16[32,640]{1,0:T(8,128)(2,1)S(1)} %shard_map.197.refs_0_), channel_id=1, source_target_pairs={{0,2},{2,0},{4,6},{6,4},{8,10},{10,8},{12,14},{14,12},{16,18},{18,... | collective-permute-start | bytes 122888 | tf_op jit(solution)/shard_map/ppermute | solution.py:520

commit v2 on v1

--- a/solution.py
+++ b/solution.py
@@ -17,7 +17,6 @@
 BF16 = jnp.bfloat16
 
 VMEM = pl.BlockSpec(memory_space=pltpu.VMEM)
-SMEM = pl.BlockSpec(memory_space=pltpu.SMEM)
 HBM = pl.BlockSpec(memory_space=pltpu.HBM)
 ANY = pl.BlockSpec(memory_space=pl.ANY)
 
@@ -109,13 +108,13 @@
                     bias[head, :, start:stop] = found[:, : stop - start]
 
 
-def prepare_kernel(blocks, ready, me_ref, *refs):
+def prepare_kernel(blocks, ready, *refs):
     sources, rest = refs[:12], refs[12:]
     normed, part, bias, index_t, table_pad, bucket, *kept = rest[:16]
     table, sems = rest[16:]
     copies = fetch(list(zip(sources, [bucket, table] + kept)), sems)
     tokens, gain, w_own = kept[:3]
-    me = me_ref[0]
+    me = lax.axis_index("mp")
     width = w_own.shape[0]
     span = bucket.shape[0]
     head_count, padded = table_pad.shape
@@ -135,16 +134,16 @@
 
 
 def attend_kernel(blocks, share, *refs):
-    me_ref, normed, part, bias_ready, index_t, table_pad, bucket, gain, cot, region = refs[:10]
-    own, arrived = refs[10:14], refs[14 : 10 + 4 * blocks]
-    rest = refs[10 + 4 * blocks :]
+    normed, part, bias_ready, index_t, table_pad, bucket, gain, cot, region = refs[:9]
+    own, arrived = refs[9:13], refs[13 : 9 + 4 * blocks]
+    rest = refs[9 + 4 * blocks :]
     terms, lefts, rest = rest[:blocks], rest[blocks : 2 * blocks], rest[2 * blocks :]
     score_parts, (packed, gain_term), rest = rest[:blocks], rest[blocks : blocks + 2], rest[blocks + 2 :]
     proj, mixed_grad, mixed, score_sum, gain_row, bias = rest
     w_in, w_out, in_basis, out_basis = (
         [own[at]] + list(arrived[at : at + blocks - 1]) for at in range(4)
     )
-    me = me_ref[0]
+    me = lax.axis_index("mp")
     window_count, span = region.shape
     features = normed.shape[1]
     ready, head_count = bias_ready.shape[0], bias.shape[0]
@@ -241,12 +240,12 @@
         score_parts[step][...] = score_sum[:, block_columns(me, step, blocks, rows), :]
 
 
-def token_kernel(blocks, me_ref, packed, *refs):
+def token_kernel(blocks, packed, *refs):
     w_in, (tokens, cot, gain, _, result, flag, normed_grad, token_grad, sems) = (
         refs[:blocks],
         refs[blocks:],
     )
-    me = me_ref[0]
+    me = lax.axis_index("mp")
     width = tokens.shape[1] // blocks
     for step in range(blocks):
         normed_grad[:, block_columns(me, step, blocks, width)] = nt(packed[...], w_in[step][...])
@@ -263,12 +262,12 @@
         copy.wait()
 
 
-def table_kernel(blocks, me_ref, *refs):
+def table_kernel(blocks, *refs):
     score_parts, (gain_term, index_t, stats) = refs[:blocks], refs[blocks:]
     head_count, rows, span = score_parts[0].shape
     padded = stats.shape[1] - 2 * LANES
     levels = padded // LANES
-    indices = index_t[block_columns(me_ref[0], 0, blocks, rows), :]
+    indices = index_t[block_columns(lax.axis_index("mp"), 0, blocks, rows), :]
     scores = tree_add([part[...] for part in score_parts])
     sublane = lax.broadcasted_iota(jnp.int32, (LANES, span), 0)
     total = jnp.zeros((2 * levels * head_count, LANES), F32)
@@ -414,10 +413,10 @@
     return [jnp.concatenate(finished, axis=0) for _, _, finished in states]
 
 
-def ortho_kernel(share, parts, stat_parts, me_ref, *refs):
+def ortho_kernel(share, parts, stat_parts, *refs):
     lefts, stats = refs[:parts], refs[parts : parts + stat_parts]
     merged, ortho, *pieces, sums = refs[parts + stat_parts :]
-    digit = me_ref[1]
+    digit = lax.axis_index("dp") % 4
     rank = ortho.shape[0] // 2
     quarter = merged.shape[1] // len(pieces)
     sums[...] = tree_sum([stat[...] for stat in stats])
@@ -428,8 +427,7 @@
         block = jnp.bitwise_xor(digit, step)
         columns = pl.ds(pl.multiple_of(block * quarter, quarter), quarter)
         pair = stacked(jnp.where(block < len(pieces) - 1, finished[0], finished[1]))
-        coarse, fine = halves(merged[:, columns])
-        piece[:, :quarter] = folded(nn(pair, coarse) + nn(pair, fine)).astype(BF16)
+        piece[:, :quarter] = folded(nn(pair, merged[:, columns].astype(BF16))).astype(BF16)
         stat_columns = pl.ds(pl.multiple_of(block * 2 * LANES, 2 * LANES), 2 * LANES)
         piece[:, quarter:] = stats_pieces(sums[:, stat_columns])
 
@@ -442,7 +440,7 @@
     total[:, quarter:] = stats_pieces(stats_pair(summed[:, quarter:]))
 
 
-def update_kernel(share, stat_share, parts, me_ref, *refs):
+def update_kernel(share, stat_share, parts, *refs):
     pieces = refs[:parts]
     ortho, merged = refs[parts : parts + 2]
     in_update, out_update, in_new_error, out_new_error = refs[parts + 2 : parts + 6]
@@ -450,7 +448,7 @@
     rights, updates, errors, sems = refs[parts + 10 : parts + 14]
     small = refs[parts + 14 : parts + 18]
     in_basis, out_basis, table, gain = small
-    digit = me_ref[1]
+    digit = lax.axis_index("dp") % 4
     rank = ortho.shape[0] // 2
     quarter = rights.shape[2] - LANES
     for step, piece in enumerate(pieces):
@@ -564,7 +562,6 @@
     both = wide + features
     padded = -(-buckets // LANES) * LANES
     blocks = 2 if n_mp == 2 else 1
-    me = jnp.stack([lax.axis_index("mp"), lax.axis_index("dp") & 3]).astype(jnp.int32)
     token_rows = tokens.reshape(row_count, features)
     cot_rows = cotangent.reshape(row_count, features)
     gain = norm_gain.reshape(1, features)
@@ -610,9 +607,9 @@
         [pltpu.VMEM(bias_table.shape, F32), pltpu.SemaphoreType.DMA((12,))],
         flops=2 * row_count * width * wide,
         moved=4 << 20,
-        in_specs=[SMEM] + [HBM] * 12,
+        in_specs=[HBM] * 12,
         out_specs=[VMEM] * 16,
-    )(me, *in_hbm(*operands))
+    )(*in_hbm(*operands))
     token_rows, gain, w_in_own, cot_rows, region, *own, in_errors, out_errors = kept
     in_basis_t, out_basis_t = own[1:]
 
@@ -633,9 +630,9 @@
         ],
         flops=4 * row_count * features * both,
         moved=8 << 20,
-        in_specs=[SMEM] + [VMEM] * (13 + len(arrived)),
+        in_specs=[VMEM] * (13 + len(arrived)),
         out_specs=[VMEM] * (3 * blocks + 2),
-    )(me, normed, part, bias, index_t, table_pad, bucket, gain, cot_rows, region, w_in_own, *own, *arrived)
+    )(normed, part, bias, index_t, table_pad, bucket, gain, cot_rows, region, w_in_own, *own, *arrived)
     terms, lefts, score_parts = (
         outputs[at * blocks : (at + 1) * blocks] for at in range(3)
     )
@@ -677,9 +674,9 @@
         shape((head_count, padded + 2 * LANES), F32),
         flops=2 * row_count * features * wide,
         moved=4 << 20,
-        in_specs=[SMEM] + [VMEM] * (blocks + 2),
+        in_specs=[VMEM] * (blocks + 2),
         out_specs=VMEM,
-    )(me, *score_parts, gain_term, index_t)
+    )(*score_parts, gain_term, index_t)
 
     if blocks == 2:
         stats = [stats, exchange(stats, "mp", n_mp, 1)]
@@ -713,9 +710,9 @@
         [pltpu.VMEM((head_count, padded + 2 * LANES), F32)],
         flops=12 * row_block * both * rank,
         moved=3 << 20,
-        in_specs=[SMEM] + [VMEM] * (len(lefts) + len(stats) + 1),
+        in_specs=[VMEM] * (len(lefts) + len(stats) + 1),
         out_specs=[VMEM] * (1 + parts),
-    )(me, *lefts, *stats, merged)
+    )(*lefts, *stats, merged)
 
     token_grad, flag = call(
         functools.partial(token_kernel, blocks),
@@ -727,9 +724,9 @@
         ],
         flops=2 * row_count * features * wide,
         moved=4 << 20,
-        in_specs=[SMEM] + [VMEM] * (blocks + 5),
+        in_specs=[VMEM] * (blocks + 5),
         out_specs=[HBM, VMEM],
-    )(me, packed, w_in_own, *arrived[:1], token_rows, cot_rows, gain, ortho)
+    )(packed, w_in_own, *arrived[:1], token_rows, cot_rows, gain, ortho)
 
     def reduced(values):
         return call(
@@ -772,9 +769,9 @@
         + buffers(*small),
         flops=12 * row_block * both * rank,
         moved=8 << 20,
-        in_specs=[SMEM] + [VMEM] * (parts + 2),
+        in_specs=[VMEM] * (parts + 2),
         out_specs=[HBM] * 8,
-    )(me, *pieces, ortho, merged)
+    )(*pieces, ortho, merged)
 
     return (
         token_grad.reshape(tokens.shape),

time: 62.4 us -> 59.7 us (0.957)
  Pallas kernels: 24.6 us -> 21.5 us
    pallas_call x1, Pallas kernels: 4.34 us -> 3.54 us  [shards(): call(functools.partial(ortho_kernel, 1.0 / n_dp, len(lefts), len(stats)),...]
  transfers between devices with their start and end apart: 23 -> 23, of which waited for: 11 -> 11; matrix products, arithmetic and copies ran while one was open for 0% -> 0% of each run, Pallas kernels for 15% -> 14%
where the time goes in v2:
time: 59.7 us; the launch traced here: 59.5 us
  starting transfers between devices  22.8 us (38%)
  Pallas kernels  21.5 us (36%)
  waiting for transfers between devices  14.2 us (24%)
  between operations  0.94 us (2%)
    ppermute x23, starting transfers between devices, exchange(): lax.ppermute(value, axis, [(at, at ^ distance) for at in range(count)])  22.8 us
    ppermute x23, waiting for transfers between devices, exchange(): lax.ppermute(value, axis, [(at, at ^ distance) for at in range(count)])  14.2 us
    pallas_call x1, Pallas kernels, shards(): call(functools.partial(attend_kernel, blocks, 1.0 / n_mp), (shape((width,...  7.4 us
    pallas_call x1, Pallas kernels, shards(): call(functools.partial(ortho_kernel, 1.0 / n_dp, len(lefts), len(stats)),...  3.54 us
    pallas_call x1, Pallas kernels, shards(): call(functools.partial(table_kernel, blocks), shape((head_count, padded +...  2.67 us
    pallas_call x1, Pallas kernels, shards(): call(functools.partial(prepare_kernel, blocks, READY_HEADS), (shape((row_...  2.58 us
    pallas_call x1, Pallas kernels, shards(): call(functools.partial(update_kernel, 1.0 / n_dp, 1.0 / (n_dp * n_mp), pa...  2.47 us
    pallas_call x1, Pallas kernels, shards(): call(functools.partial(token_kernel, blocks), (shape((row_count, features...  1.71 us
  transfers between devices with their start and end apart: 23, of which 11 were waited for; matrix products, arithmetic and copies ran while one was open for 0% of the time, Pallas kernels for 14%

profile of v2, /device:TPU:0, one launch (start us, length us, event | category | flops | bytes accessed | tf_op | source)
XLA Modules:
  0.0 59.5 jit_solution(18342689097258003156)
XLA Ops:
  0.6 0.5 collective-permute-start
  1.8 2.6 %shard_map.187 = (bf16[288,512]{1,0:T(8,128)(2,1)S(1)}, f32[288,1536]{1,0:T(8,128)S(1)}, f32[2,144,144]{2,1,0:T(8,128)S(1)}, s32[144,144]{1,0:T(8,128)S(1)}, f32...) custom-call(s32[144,144]{1,0:T(8,128)} %refs_0_.1, ...), custom_call_target="tpu_custom_call" | custom-call | flops 226492416 | bytes 4194304 | tf_op jit(solution)/shard_map/pallas_call | solution.py:596
  4.4 7.4 %shard_map.188 = (bf16[256,2048]{1,0:T(8,128)(2,1)S(1)}, bf16[256,2048]{1,0:T(8,128)(2,1)S(1)}, f32[64,256]{1,0:T(8,128)S(1)}, f32[64,256]{1,0:T(8,128)S(1)}, f3...) custom-call(bf16[288,512]{1,0:T(8,128)(2,1)S(1)} %get-tuple-element.5, ...), custom_call_target="tpu_custom_call" | custom-call | flops 1207959552 | bytes 8388608 | tf_op jit(solution)/shard_map/pallas_call | solution.py:617
  11.8 0.4 collective-permute-start.4
  12.2 0.8 %shard_map.189.left_own = f32[64,256]{1,0:T(8,128)S(1)} custom-call(f32[64,256]{1,0:T(8,128)S(1)} %get-tuple-element.66.term_left, f32[256,1536]{1,0:T(8,128)S(1)} %get-tuple-element.67.in_error.refs_2_, f32[256,512]{1,0:T(8,128)S(1)} %get-tuple-element.68.out_error.refs_3_, f32[32,1536]{1,0:T(8,128)S(1)} %get-tuple-element.62.refs_11_.in_basis, ...), custom_call_target="tpu_custom_call" | custom-call | flops 134217728 | bytes 3145728 | tf_op jit(solution)/shard_map/pallas_call | solution.py:653
  13.7 4.9 %collective-permute-start.7 = (f32[64,256]{1,0:T(8,128)S(1)}, f32[64,256]{1,0:T(8,128)S(1)}, u32[]{:S(2)}, u32[]{:S(2)}) collective-permute-start(f32[64,256]{1,0:T(8,128)S(1)} %get-tuple-element.72.refs_0_), channel_id=1, source_target_pairs={{0,24},{2,26},{4,28},{6,30},{8,16},{10,18},{12,20},{14,22},{16,8},... | collective-permute-start | bytes 196616 | tf_op jit(solution)/shard_map/ppermute | solution.py:518
  18.7 0.6 collective-permute-start.5
  19.2 2.7 %shard_map.191.refs_4_ = f32[8,1024]{1,0:T(8,128)S(1)} custom-call(f32[8,72,144]{2,1,0:T(8,128)S(1)} %get-tuple-element.73.refs_0_, f32[8,72,144]{2,1,0:T(8,128)S(1)} %collective-permute-done.8.refs_1_, f32[8,128]{1,0:T(8,128)S(1)} %get-tuple-element.75.refs_2_, s32[144,144]{1,0:T(8,128)S(1)} %get-tuple-element.54.refs_3_), custom_call_target="tpu_custom_call" | custom-call | flops 452984832 | bytes 4194304 | tf_op jit(solution)/shard_map/pallas_call | solution.py:672
  22.0 2.6 %collective-permute-done.6.refs_2_ = f32[64,256]{1,0:T(8,128)S(1)} collective-permute-done((f32[64,256]{1,0:T(8,128)S(1)}, f32[64,256]{1,0:T(8,128)S(1)}, u32[]{:S(2)}, u32[]{:S(2)}) %collective-permute-start.6) | collective-permute-done | bytes 65568 | tf_op jit(solution)/shard_map/ppermute | solution.py:518
  24.6 2.5 %collective-permute-start.12 = (f32[64,256]{1,0:T(8,128)S(1)}, f32[64,256]{1,0:T(8,128)S(1)}, u32[]{:S(2)}, u32[]{:S(2)}) collective-permute-start(f32[64,256]{1,0:T(8,128)S(1)} %shard_map.192.refs_0_), channel_id=1, source_target_pairs={{0,6},{2,4},{4,2},{6,0},{8,14},{10,12},{12,10},{14,8},{16,22},{18,... | collective-permute-start | bytes 196616 | tf_op jit(solution)/shard_map/ppermute | solution.py:518
  27.1 0.5 collective-permute-start.11
  27.6 0.6 collective-permute-start.10
  28.5 1.4 %collective-permute-done.12.refs_3_ = f32[64,256]{1,0:T(8,128)S(1)} collective-permute-done((f32[64,256]{1,0:T(8,128)S(1)}, f32[64,256]{1,0:T(8,128)S(1)}, u32[]{:S(2)}, u32[]{:S(2)}) %collective-permute-start.12) | collective-permute-done | bytes 65568 | tf_op jit(solution)/shard_map/ppermute | solution.py:518
  29.9 1.4 %collective-permute-done.11.refs_2_ = f32[64,256]{1,0:T(8,128)S(1)} collective-permute-done((f32[64,256]{1,0:T(8,128)S(1)}, f32[64,256]{1,0:T(8,128)S(1)}, u32[]{:S(2)}, u32[]{:S(2)}) %collective-permute-start.11) | collective-permute-done | bytes 65568 | tf_op jit(solution)/shard_map/ppermute | solution.py:518
  31.3 0.5 collective-permute-done.10.refs_1_
  31.8 3.5 %shard_map.194 = (f32[64,256]{1,0:T(8,128)S(1)}, bf16[32,640]{1,0:T(8,128)(2,1)S(1)}, bf16[32,640]{1,0:T(8,128)(2,1)S(1)}, bf16[32,640]{1,0:T(8,128)(2,1)S(1)}, bf16[32,640]{1,0:T(8,128)(2,1)S(1)}) custom-call(f32[64,256]{1,0:T(8,128)S(1)} %shard_map.192.refs_0_, f32[64,256]{1,0:T(8,128)S(1)} %collective-permute-done.10.refs_1_, ...), custom_call_target="tpu_custom_call" | custom-call | flops 201326592 | bytes 3145728 | tf_op jit(solution)/shard_map/pallas_call | solution.py:707
  35.4 0.6 %collective-permute-start.14 = (bf16[32,640]{1,0:T(8,128)(2,1)S(1)}, bf16[32,640]{1,0:T(8,128)(2,1)S(1)}, u32[]{:S(2)}, u32[]{:S(2)}) collective-permute-start(bf16[32,640]{1,0:T(8,128)(2,1)S(1)} %get-tuple-element.81), channel_id=1, source_target_pairs={{0,2},{2,0},{4,6},{6,4},{8,10},{10,8},{12,14},{14,12},{16,18},{18,... | collective-permute-start | bytes 122888 | tf_op jit(solution)/shard_map/ppermute | solution.py:518
  36.0 1.5 %collective-permute-start.15 = (bf16[32,640]{1,0:T(8,128)(2,1)S(1)}, bf16[32,640]{1,0:T(8,128)(2,1)S(1)}, u32[]{:S(2)}, u32[]{:S(2)}) collective-permute-start(bf16[32,640]{1,0:T(8,128)(2,1)S(1)} %get-tuple-element.82), channel_id=1, source_target_pairs={{0,4},{2,6},{4,0},{6,2},{8,12},{10,14},{12,8},{14,10},{16,20},{18,... | collective-permute-start | bytes 122888 | tf_op jit(solution)/shard_map/ppermute | solution.py:518
  37.5 1.4 %collective-permute-start.16 = (bf16[32,640]{1,0:T(8,128)(2,1)S(1)}, bf16[32,640]{1,0:T(8,128)(2,1)S(1)}, u32[]{:S(2)}, u32[]{:S(2)}) collective-permute-start(bf16[32,640]{1,0:T(8,128)(2,1)S(1)} %get-tuple-element.83), channel_id=1, source_target_pairs={{0,6},{2,4},{4,2},{6,0},{8,14},{10,12},{12,10},{14,8},{16,22},{18,... | collective-permute-start | bytes 122888 | tf_op jit(solution)/shard_map/ppermute | solution.py:518
  38.9 1.7 %shard_map.195 = (bf16[288,512]{1,0:T(8,128)(2,1)}, f32[8,128]{1,0:T(8,128)S(1)}) custom-call(bf16[288,1536]{1,0:T(8,128)(2,1)S(1)} %get-tuple-element.64.packed, bf16[256,1536]{1,0:T(8,128)(2,1)S(1)} %get-tuple-element.60.refs_9_.refs_0_, bf16[256,1536]{1,0:T(8,128)(2,1)S(1)} %collective-permute-done.refs_13_.refs_1_, ...), custom_call_target="tpu_custom_call" | custom-call | flops 452984832 | bytes 4194304 | tf_op jit(solution)/shard_map/pallas_call | solution.py:717
  40.6 1.7 %collective-permute-done.16.refs_3_ = bf16[32,640]{1,0:T(8,128)(2,1)S(1)} collective-permute-done((bf16[32,640]{1,0:T(8,128)(2,1)S(1)}, bf16[32,640]{1,0:T(8,128)(2,1)S(1)}, u32[]{:S(2)}, u32[]{:S(2)}) %collective-permute-start.16) | collective-permute-done | bytes 40992 | tf_op jit(solution)/shard_map/ppermute | solution.py:518
  42.4 2.6 %collective-permute-start.19 = (bf16[32,640]{1,0:T(8,128)(2,1)S(1)}, bf16[32,640]{1,0:T(8,128)(2,1)S(1)}, u32[]{:S(2)}, u32[]{:S(2)}) collective-permute-start(bf16[32,640]{1,0:T(8,128)(2,1)S(1)} %shard_map.196.refs_0_), channel_id=1, source_target_pairs={{0,24},{2,26},{4,28},{6,30},{8,16},{10,18},{12,20},{14,22},{16,8},... | collective-permute-start | bytes 122888 | tf_op jit(solution)/shard_map/ppermute | solution.py:518
  45.1 1.8 %collective-permute-start.17 = (bf16[32,640]{1,0:T(8,128)(2,1)S(1)}, bf16[32,640]{1,0:T(8,128)(2,1)S(1)}, u32[]{:S(2)}, u32[]{:S(2)}) collective-permute-start(bf16[32,640]{1,0:T(8,128)(2,1)S(1)} %shard_map.196.refs_0_), channel_id=1, source_target_pairs={{0,8},{2,10},{4,12},{6,14},{8,0},{10,2},{12,4},{14,6},{16,24},{18,... | collective-permute-start | bytes 122888 | tf_op jit(solution)/shard_map/ppermute | solution.py:518
  46.9 1.4 %collective-permute-done.19.refs_3_ = bf16[32,640]{1,0:T(8,128)(2,1)S(1)} collective-permute-done((bf16[32,640]{1,0:T(8,128)(2,1)S(1)}, bf16[32,640]{1,0:T(8,128)(2,1)S(1)}, u32[]{:S(2)}, u32[]{:S(2)}) %collective-permute-start.19) | collective-permute-done | bytes 40992 | tf_op jit(solution)/shard_map/ppermute | solution.py:518
  48.3 1.6 %collective-permute-done.18.refs_2_ = bf16[32,640]{1,0:T(8,128)(2,1)S(1)} collective-permute-done((bf16[32,640]{1,0:T(8,128)(2,1)S(1)}, bf16[32,640]{1,0:T(8,128)(2,1)S(1)}, u32[]{:S(2)}, u32[]{:S(2)}) %collective-permute-start.18) | collective-permute-done | bytes 40992 | tf_op jit(solution)/shard_map/ppermute | solution.py:518
  49.9 1.5 %collective-permute-start.22 = (bf16[32,640]{1,0:T(8,128)(2,1)S(1)}, bf16[32,640]{1,0:T(8,128)(2,1)S(1)}, u32[]{:S(2)}, u32[]{:S(2)}) collective-permute-start(bf16[32,640]{1,0:T(8,128)(2,1)S(1)} %shard_map.197.refs_0_), channel_id=1, source_target_pairs={{0,6},{2,4},{4,2},{6,0},{8,14},{10,12},{12,10},{14,8},{16,22},{18,... | collective-permute-start | bytes 122888 | tf_op jit(solution)/shard_map/ppermute | solution.py:518
  51.4 1.5 %collective-permute-start.21 = (bf16[32,640]{1,0:T(8,128)(2,1)S(1)}, bf16[32,640]{1,0:T(8,128)(2,1)S(1)}, u32[]{:S(2)}, u32[]{:S(2)}) collective-permute-start(bf16[32,640]{1,0:T(8,128)(2,1)S(1)} %shard_map.197.refs_0_), channel_id=1, source_target_pairs={{0,4},{2,6},{4,0},{6,2},{8,12},{10,14},{12,8},{14,10},{16,20},{18,... | collective-permute-start | bytes 122888 | tf_op jit(solution)/shard_map/ppermute | solution.py:518
  52.9 0.6 collective-permute-start.20
  53.5 1.4 %collective-permute-done.22.refs_3_ = bf16[32,640]{1,0:T(8,128)(2,1)S(1)} collective-permute-done((bf16[32,640]{1,0:T(8,128)(2,1)S(1)}, bf16[32,640]{1,0:T(8,128)(2,1)S(1)}, u32[]{:S(2)}, u32[]{:S(2)}) %collective-permute-start.22) | collective-permute-done | bytes 40992 | tf_op jit(solution)/shard_map/ppermute | solution.py:518
  54.9 0.5 collective-permute-done.21.refs_2_
  55.4 1.5 %collective-permute-done.20.refs_1_ = bf16[32,640]{1,0:T(8,128)(2,1)S(1)} collective-permute-done((bf16[32,640]{1,0:T(8,128)(2,1)S(1)}, bf16[32,640]{1,0:T(8,128)(2,1)S(1)}, u32[]{:S(2)}, u32[]{:S(2)}) %collective-permute-start.20) | collective-permute-done | bytes 40992 | tf_op jit(solution)/shard_map/ppermute | solution.py:518
  56.9 2.5 %shard_map.198 = (f32[256,1536]{1,0:T(8,128)}, f32[256,512]{1,0:T(8,128)}, f32[256,1536]{1,0:T(8,128)}, f32[256,512]{1,0:T(8,128)}, f32[32,1536]{1,0:T(8,128)}, ...) custom-call(bf16[32,640]{1,0:T(8,128)(2,1)S(1)} %shard_map.197.refs_0_, ...), custom_call_target="tpu_custom_call" | custom-call | flops 201326592 | bytes 8388608 | tf_op jit(solution)/shard_map/pallas_call | solution.py:754
  (26 shorter events, 1.9 us)
Async XLA Ops:
  0.6 3.7 %collective-permute-start = (bf16[256,1536]{1,0:T(8,128)(2,1)}, bf16[256,1536]{1,0:T(8,128)(2,1)S(1)}, u32[]{:S(2)}, u32[]{:S(2)}) collective-permute-start(bf16[256,1536]{1,0:T(8,128)(2,1)} %refs_4_.1), channel_id=1, source_target_pairs={{0,1},{1,0},{2,3},{3,2},{4,5},{5,4},{6,7},{7,6},{8,9},{9,8},{10,11... | collective-permute-start | bytes 2359304 | tf_op jit(solution)/shard_map/ppermute | solution.py:518
  1.2 3.2 %collective-permute-start.1 = (bf16[256,512]{1,0:T(8,128)(2,1)}, bf16[256,512]{1,0:T(8,128)(2,1)S(1)}, u32[]{:S(2)}, u32[]{:S(2)}) collective-permute-start(bf16[256,512]{1,0:T(8,128)(2,1)} %refs_7_.1), channel_id=1, source_target_pairs={{0,1},{1,0},{2,3},{3,2},{4,5},{5,4},{6,7},{7,6},{8,9},{9,8},{10,11... | collective-permute-start | bytes 786440 | tf_op jit(solution)/shard_map/ppermute | solution.py:518
  1.2 3.1 %collective-permute-start.2 = (f32[32,1536]{1,0:T(8,128)}, f32[32,1536]{1,0:T(8,128)S(1)}, u32[]{:S(2)}, u32[]{:S(2)}) collective-permute-start(f32[32,1536]{1,0:T(8,128)} %bitcast.25), channel_id=1, source_target_pairs={{0,1},{1,0},{2,3},{3,2},{4,5},{5,4},{6,7},{7,6},{8,9},{9,8},{10,11... | collective-permute-start | bytes 589832 | tf_op jit(solution)/shard_map/ppermute | solution.py:518
  1.7 2.7 %collective-permute-start.3 = (f32[32,512]{1,0:T(8,128)}, f32[32,512]{1,0:T(8,128)S(1)}, u32[]{:S(2)}, u32[]{:S(2)}) collective-permute-start(f32[32,512]{1,0:T(8,128)} %bitcast.27), channel_id=1, source_target_pairs={{0,1},{1,0},{2,3},{3,2},{4,5},{5,4},{6,7},{7,6},{8,9},{9,8},{10,11... | collective-permute-start | bytes 196616 | tf_op jit(solution)/shard_map/ppermute | solution.py:518
  11.8 1.4 %collective-permute-start.4 = (f32[64,256]{1,0:T(8,128)S(1)}, f32[64,256]{1,0:T(8,128)S(1)}, u32[]{:S(2)}, u32[]{:S(2)}) collective-permute-start(f32[64,256]{1,0:T(8,128)S(1)} %get-tuple-element.69), channel_id=1, source_target_pairs={{0,1},{1,0},{2,3},{3,2},{4,5},{5,4},{6,7},{7,6},{8,9},{9,8},{10,11... | collective-permute-start | bytes 196616 | tf_op jit(solution)/shard_map/ppermute | solution.py:518
  13.2 15.0 %collective-permute-start.13 = (bf16[256,2048]{1,0:T(8,128)(2,1)S(1)}, bf16[256,2048]{1,0:T(8,128)(2,1)S(1)}, u32[]{:S(2)}, u32[]{:S(2)}) collective-permute-start(bf16[256,2048]{1,0:T(8,128)(2,1)S(1)} %get-tuple-element.77), channel_id=1, source_target_pairs={{0,1},{1,0},{2,3},{3,2},{4,5},{5,4},{6,7},{7,6},{8,9},{9,8},{10,11... | collective-permute-start | bytes 3145736 | tf_op jit(solution)/shard_map/ppermute | solution.py:518
  13.6 5.7 %collective-permute-start.8 = (f32[8,72,144]{2,1,0:T(8,128)S(1)}, f32[8,72,144]{2,1,0:T(8,128)S(1)}, u32[]{:S(2)}, u32[]{:S(2)}) collective-permute-start(f32[8,72,144]{2,1,0:T(8,128)S(1)} %get-tuple-element.74), channel_id=1, source_target_pairs={{0,1},{1,0},{2,3},{3,2},{4,5},{5,4},{6,7},{7,6},{8,9},{9,8},{10,11... | collective-permute-start | bytes 995336 | tf_op jit(solution)/shard_map/ppermute | solution.py:518
  13.7 8.3 %collective-permute-start.7 = (f32[64,256]{1,0:T(8,128)S(1)}, f32[64,256]{1,0:T(8,128)S(1)}, u32[]{:S(2)}, u32[]{:S(2)}) collective-permute-start(f32[64,256]{1,0:T(8,128)S(1)} %get-tuple-element.72.refs_0_), channel_id=1, source_target_pairs={{0,24},{2,26},{4,28},{6,30},{8,16},{10,18},{12,20},{14,22},{16,8},... | collective-permute-start | bytes 196616 | tf_op jit(solution)/shard_map/ppermute | solution.py:518
  18.7 5.9 %collective-permute-start.6 = (f32[64,256]{1,0:T(8,128)S(1)}, f32[64,256]{1,0:T(8,128)S(1)}, u32[]{:S(2)}, u32[]{:S(2)}) collective-permute-start(f32[64,256]{1,0:T(8,128)S(1)} %get-tuple-element.72.refs_0_), channel_id=1, source_target_pairs={{0,16},{2,18},{4,20},{6,22},{8,24},{10,26},{12,28},{14,30},{16,0},... | collective-permute-start | bytes 196616 | tf_op jit(solution)/shard_map/ppermute | solution.py:518
  18.7 5.9 %collective-permute-start.5 = (f32[64,256]{1,0:T(8,128)S(1)}, f32[64,256]{1,0:T(8,128)S(1)}, u32[]{:S(2)}, u32[]{:S(2)}) collective-permute-start(f32[64,256]{1,0:T(8,128)S(1)} %get-tuple-element.72.refs_0_), channel_id=1, source_target_pairs={{0,8},{2,10},{4,12},{6,14},{8,0},{10,2},{12,4},{14,6},{16,24},{18,... | collective-permute-start | bytes 196616 | tf_op jit(solution)/shard_map/ppermute | solution.py:518
  21.9 2.6 %collective-permute-start.9 = (f32[8,1024]{1,0:T(8,128)S(1)}, f32[8,1024]{1,0:T(8,128)S(1)}, u32[]{:S(2)}, u32[]{:S(2)}) collective-permute-start(f32[8,1024]{1,0:T(8,128)S(1)} %shard_map.191.refs_4_), channel_id=1, source_target_pairs={{0,1},{1,0},{2,3},{3,2},{4,5},{5,4},{6,7},{7,6},{8,9},{9,8},{10,11... | collective-permute-start | bytes 98312 | tf_op jit(solution)/shard_map/ppermute | solution.py:518
  24.6 5.3 %collective-permute-start.12 = (f32[64,256]{1,0:T(8,128)S(1)}, f32[64,256]{1,0:T(8,128)S(1)}, u32[]{:S(2)}, u32[]{:S(2)}) collective-permute-start(f32[64,256]{1,0:T(8,128)S(1)} %shard_map.192.refs_0_), channel_id=1, source_target_pairs={{0,6},{2,4},{4,2},{6,0},{8,14},{10,12},{12,10},{14,8},{16,22},{18,... | collective-permute-start | bytes 196616 | tf_op jit(solution)/shard_map/ppermute | solution.py:518
  27.1 4.3 %collective-permute-start.11 = (f32[64,256]{1,0:T(8,128)S(1)}, f32[64,256]{1,0:T(8,128)S(1)}, u32[]{:S(2)}, u32[]{:S(2)}) collective-permute-start(f32[64,256]{1,0:T(8,128)S(1)} %shard_map.192.refs_0_), channel_id=1, source_target_pairs={{0,4},{2,6},{4,0},{6,2},{8,12},{10,14},{12,8},{14,10},{16,20},{18,... | collective-permute-start | bytes 196616 | tf_op jit(solution)/shard_map/ppermute | solution.py:518
  27.6 4.3 %collective-permute-start.10 = (f32[64,256]{1,0:T(8,128)S(1)}, f32[64,256]{1,0:T(8,128)S(1)}, u32[]{:S(2)}, u32[]{:S(2)}) collective-permute-start(f32[64,256]{1,0:T(8,128)S(1)} %shard_map.192.refs_0_), channel_id=1, source_target_pairs={{0,2},{2,0},{4,6},{6,4},{8,10},{10,8},{12,14},{14,12},{16,18},{18,... | collective-permute-start | bytes 196616 | tf_op jit(solution)/shard_map/ppermute | solution.py:518
  35.4 5.3 %collective-permute-start.14 = (bf16[32,640]{1,0:T(8,128)(2,1)S(1)}, bf16[32,640]{1,0:T(8,128)(2,1)S(1)}, u32[]{:S(2)}, u32[]{:S(2)}) collective-permute-start(bf16[32,640]{1,0:T(8,128)(2,1)S(1)} %get-tuple-element.81), channel_id=1, source_target_pairs={{0,2},{2,0},{4,6},{6,4},{8,10},{10,8},{12,14},{14,12},{16,18},{18,... | collective-permute-start | bytes 122888 | tf_op jit(solution)/shard_map/ppermute | solution.py:518
  36.0 4.6 %collective-permute-start.15 = (bf16[32,640]{1,0:T(8,128)(2,1)S(1)}, bf16[32,640]{1,0:T(8,128)(2,1)S(1)}, u32[]{:S(2)}, u32[]{:S(2)}) collective-permute-start(bf16[32,640]{1,0:T(8,128)(2,1)S(1)} %get-tuple-element.82), channel_id=1, source_target_pairs={{0,4},{2,6},{4,0},{6,2},{8,12},{10,14},{12,8},{14,10},{16,20},{18,... | collective-permute-start | bytes 122888 | tf_op jit(solution)/shard_map/ppermute | solution.py:518
  37.5 4.9 %collective-permute-start.16 = (bf16[32,640]{1,0:T(8,128)(2,1)S(1)}, bf16[32,640]{1,0:T(8,128)(2,1)S(1)}, u32[]{:S(2)}, u32[]{:S(2)}) collective-permute-start(bf16[32,640]{1,0:T(8,128)(2,1)S(1)} %get-tuple-element.83), channel_id=1, source_target_pairs={{0,6},{2,4},{4,2},{6,0},{8,14},{10,12},{12,10},{14,8},{16,22},{18,... | collective-permute-start | bytes 122888 | tf_op jit(solution)/shard_map/ppermute | solution.py:518
  42.4 5.9 %collective-permute-start.19 = (bf16[32,640]{1,0:T(8,128)(2,1)S(1)}, bf16[32,640]{1,0:T(8,128)(2,1)S(1)}, u32[]{:S(2)}, u32[]{:S(2)}) collective-permute-start(bf16[32,640]{1,0:T(8,128)(2,1)S(1)} %shard_map.196.refs_0_), channel_id=1, source_target_pairs={{0,24},{2,26},{4,28},{6,30},{8,16},{10,18},{12,20},{14,22},{16,8},... | collective-permute-start | bytes 122888 | tf_op jit(solution)/shard_map/ppermute | solution.py:518
  45.0 4.9 %collective-permute-start.18 = (bf16[32,640]{1,0:T(8,128)(2,1)S(1)}, bf16[32,640]{1,0:T(8,128)(2,1)S(1)}, u32[]{:S(2)}, u32[]{:S(2)}) collective-permute-start(bf16[32,640]{1,0:T(8,128)(2,1)S(1)} %shard_map.196.refs_0_), channel_id=1, source_target_pairs={{0,16},{2,18},{4,20},{6,22},{8,24},{10,26},{12,28},{14,30},{16,0},... | collective-permute-start | bytes 122888 | tf_op jit(solution)/shard_map/ppermute | solution.py:518
  45.1 4.8 %collective-permute-start.17 = (bf16[32,640]{1,0:T(8,128)(2,1)S(1)}, bf16[32,640]{1,0:T(8,128)(2,1)S(1)}, u32[]{:S(2)}, u32[]{:S(2)}) collective-permute-start(bf16[32,640]{1,0:T(8,128)(2,1)S(1)} %shard_map.196.refs_0_), channel_id=1, source_target_pairs={{0,8},{2,10},{4,12},{6,14},{8,0},{10,2},{12,4},{14,6},{16,24},{18,... | collective-permute-start | bytes 122888 | tf_op jit(solution)/shard_map/ppermute | solution.py:518
  49.9 5.0 %collective-permute-start.22 = (bf16[32,640]{1,0:T(8,128)(2,1)S(1)}, bf16[32,640]{1,0:T(8,128)(2,1)S(1)}, u32[]{:S(2)}, u32[]{:S(2)}) collective-permute-start(bf16[32,640]{1,0:T(8,128)(2,1)S(1)} %shard_map.197.refs_0_), channel_id=1, source_target_pairs={{0,6},{2,4},{4,2},{6,0},{8,14},{10,12},{12,10},{14,8},{16,22},{18,... | collective-permute-start | bytes 122888 | tf_op jit(solution)/shard_map/ppermute | solution.py:518
  51.4 4.0 %collective-permute-start.21 = (bf16[32,640]{1,0:T(8,128)(2,1)S(1)}, bf16[32,640]{1,0:T(8,128)(2,1)S(1)}, u32[]{:S(2)}, u32[]{:S(2)}) collective-permute-start(bf16[32,640]{1,0:T(8,128)(2,1)S(1)} %shard_map.197.refs_0_), channel_id=1, source_target_pairs={{0,4},{2,6},{4,0},{6,2},{8,12},{10,14},{12,8},{14,10},{16,20},{18,... | collective-permute-start | bytes 122888 | tf_op jit(solution)/shard_map/ppermute | solution.py:518
  52.9 4.0 %collective-permute-start.20 = (bf16[32,640]{1,0:T(8,128)(2,1)S(1)}, bf16[32,640]{1,0:T(8,128)(2,1)S(1)}, u32[]{:S(2)}, u32[]{:S(2)}) collective-permute-start(bf16[32,640]{1,0:T(8,128)(2,1)S(1)} %shard_map.197.refs_0_), channel_id=1, source_target_pairs={{0,2},{2,0},{4,6},{6,4},{8,10},{10,8},{12,14},{14,12},{16,18},{18,... | collective-permute-start | bytes 122888 | tf_op jit(solution)/shard_map/ppermute | solution.py:518

commit v3 on v2

--- a/solution.py
+++ b/solution.py
@@ -134,12 +134,11 @@
 
 
 def attend_kernel(blocks, share, *refs):
-    normed, part, bias_ready, index_t, table_pad, bucket, gain, cot, region = refs[:9]
-    own, arrived = refs[9:13], refs[13 : 9 + 4 * blocks]
-    rest = refs[9 + 4 * blocks :]
+    normed, part, bias_ready, index_t, table_pad, bucket, cot, region = refs[:8]
+    own, arrived = refs[8:12], refs[12 : 8 + 4 * blocks]
+    rest = refs[8 + 4 * blocks :]
     terms, lefts, rest = rest[:blocks], rest[blocks : 2 * blocks], rest[2 * blocks :]
-    score_parts, (packed, gain_term), rest = rest[:blocks], rest[blocks : blocks + 2], rest[blocks + 2 :]
-    proj, mixed_grad, mixed, score_sum, gain_row, bias = rest
+    score_sum, packed, proj, mixed_grad, mixed, bias = rest
     w_in, w_out, in_basis, out_basis = (
         [own[at]] + list(arrived[at : at + blocks - 1]) for at in range(4)
     )
@@ -217,14 +216,8 @@
     wide = 3 * features
     for step in range(blocks):
         columns = block_columns(me, step, blocks, width)
-        product = tn(normed[:, columns], packed[...])
-        terms[step][:, :wide] = product.astype(BF16)
+        terms[step][:, :wide] = tn(normed[:, columns], packed[...]).astype(BF16)
         terms[step][:, wide:] = tn(mixed[:, columns], cot[...]).astype(BF16)
-        weighted = product * w_in[step][...].astype(F32)
-        folds = tree_add(
-            [weighted[:, start : start + LANES] for start in range(0, wide, LANES)]
-        )
-        gain_row[:, columns] = jnp.sum(folds.T, axis=0, keepdims=True) / gain[:, columns]
         rank = in_basis[step].shape[0]
         for basis, at, place in (
             (in_basis[step], slice(None, wide), 0),
@@ -232,12 +225,6 @@
         ):
             left = folded(nt(stacked(basis[...]), terms[step][:, at])) * share
             lefts[step][place : place + rank, :] = left
-    gain_term[...] = jnp.zeros_like(gain_term)
-    for piece in range(features // LANES):
-        gain_term[piece : piece + 1, :] = gain_row[:, piece * LANES : (piece + 1) * LANES]
-    rows = span // blocks
-    for step in range(blocks):
-        score_parts[step][...] = score_sum[:, block_columns(me, step, blocks, rows), :]
 
 
 def token_kernel(blocks, packed, *refs):
@@ -263,12 +250,28 @@
 
 
 def table_kernel(blocks, *refs):
-    score_parts, (gain_term, index_t, stats) = refs[:blocks], refs[blocks:]
-    head_count, rows, span = score_parts[0].shape
+    scores_of, terms = refs[:blocks], refs[blocks : 2 * blocks]
+    w_in, rest = refs[2 * blocks : 3 * blocks], refs[3 * blocks :]
+    gain, index_t, stats, gain_row = rest
+    me = lax.axis_index("mp")
+    features = gain.shape[1]
+    for step in range(blocks):
+        columns = block_columns(me, step, blocks, features // blocks)
+        folds = tree_add(
+            [
+                terms[step][:, at : at + LANES].astype(F32)
+                * w_in[step][:, at : at + LANES].astype(F32)
+                for at in range(0, w_in[step].shape[1], LANES)
+            ]
+        )
+        gain_row[:, columns] = jnp.sum(folds.T, axis=0, keepdims=True) / gain[:, columns]
+    head_count, span, _ = scores_of[0].shape
+    rows = span // blocks
+    mine = block_columns(me, 0, blocks, rows)
     padded = stats.shape[1] - 2 * LANES
     levels = padded // LANES
-    indices = index_t[block_columns(lax.axis_index("mp"), 0, blocks, rows), :]
-    scores = tree_add([part[...] for part in score_parts])
+    indices = index_t[mine, :]
+    scores = tree_add([part[:, mine, :] for part in scores_of])
     sublane = lax.broadcasted_iota(jnp.int32, (LANES, span), 0)
     total = jnp.zeros((2 * levels * head_count, LANES), F32)
     for row in range(rows):
@@ -290,8 +293,11 @@
         stats[:, level * LANES : (level + 1) * LANES] = total[
             level * head_count : (level + 1) * head_count
         ]
-    stats[:, padded : padded + LANES] = gain_term[...]
-    stats[:, padded + LANES :] = jnp.zeros((head_count, LANES), F32)
+    stats[:, padded:] = jnp.zeros((head_count, 2 * LANES), F32)
+    for piece in range(features // LANES):
+        stats[piece : piece + 1, padded : padded + LANES] = gain_row[
+            :, piece * LANES : (piece + 1) * LANES
+        ]
 
 
 def shard_kernel(share, shard, in_basis, out_basis, left):
@@ -440,51 +446,83 @@
     total[:, quarter:] = stats_pieces(stats_pair(summed[:, quarter:]))
 
 
-def update_kernel(share, stat_share, parts, *refs):
-    pieces = refs[:parts]
-    ortho, merged = refs[parts : parts + 2]
-    in_update, out_update, in_new_error, out_new_error = refs[parts + 2 : parts + 6]
-    small_results = refs[parts + 6 : parts + 10]
-    rights, updates, errors, sems = refs[parts + 10 : parts + 14]
-    small = refs[parts + 14 : parts + 18]
-    in_basis, out_basis, table, gain = small
-    digit = lax.axis_index("dp") % 4
+def update_blocks(share, steps, pieces, ortho, merged, results, updates, errors, sems, small):
+    in_update, out_update, in_new_error, out_new_error = results
     rank = ortho.shape[0] // 2
-    quarter = rights.shape[2] - LANES
-    for step, piece in enumerate(pieces):
-        rights[step] = piece[...].astype(F32)
-    copies = []
-    tiles = []
-    for block in range(parts):
-        here = rights[jnp.bitwise_xor(digit, block)]
-        right = here[:, :quarter] * share
-        tiles.append(stats_pair(here[:, quarter:]) * stat_share)
-        is_in = block < parts - 1
-        columns = slice(block * quarter, (block + 1) * quarter)
-        own = ortho[:rank, :] if is_in else ortho[rank:, :]
-        own_coarse, own_fine = halves(own)
+    quarter = updates.shape[2]
+    count = merged.shape[1] // quarter
+    places = []
+    for at, step in enumerate(steps):
+        block = jnp.bitwise_xor(lax.axis_index("dp") % 4, step)
+        columns = pl.ds(pl.multiple_of(block * quarter, quarter), quarter)
+        right = pieces[step][:, :quarter].astype(F32) * share
+        own_coarse, own_fine = halves(
+            jnp.where(block < count - 1, ortho[:rank, :], ortho[rank:, :])
+        )
         coarse, fine = halves(right)
         update = tn(
             jnp.concatenate([own_coarse, own_coarse, own_fine], axis=0),
             jnp.concatenate([coarse, fine, coarse], axis=0),
         )
-        updates[block] = update
-        errors[block] = merged[:, columns] - update
-        if is_in:
-            in_basis[:, columns] = right
-            update_to, error_to = in_update.at[:, columns], in_new_error.at[:, columns]
-        else:
-            out_basis[...] = right
-            update_to, error_to = out_update, out_new_error
-        copies += fetch(
-            [(updates.at[block], update_to), (errors.at[block], error_to)], sems.at[block]
-        )
-    stats = jnp.concatenate(tiles, axis=1)
-    table[...] = stats[:, : table.shape[1]]
-    padded = stats.shape[1] - 2 * LANES
-    for at in range(gain.shape[1] // LANES):
-        gain[:, at * LANES : (at + 1) * LANES] = stats[at : at + 1, padded : padded + LANES]
-    copies += fetch(list(zip(small, small_results)), refs[parts + 18])
+        updates[at] = update
+        errors[at] = merged[:, columns] - update
+        places.append((block, columns))
+
+        @pl.when(block < count - 1)
+        def _():
+            targets = in_update.at[:, columns], in_new_error.at[:, columns]
+            fetch(list(zip((updates.at[at], errors.at[at]), targets)), sems.at[at])
+
+        @pl.when(block == count - 1)
+        def _():
+            targets = out_update, out_new_error
+            fetch(list(zip((updates.at[at], errors.at[at]), targets)), sems.at[at])
+
+    small()
+    for at, (block, columns) in enumerate(places):
+        pltpu.make_async_copy(updates.at[at], out_update, sems.at[at, 0]).wait()
+        pltpu.make_async_copy(errors.at[at], out_new_error, sems.at[at, 1]).wait()
+
+
+def first_kernel(share, steps, *refs):
+    count = len(steps)
+    pieces = dict(zip(steps, refs[:count]))
+    ortho, merged = refs[count : count + 2]
+    results, (updates, errors, sems) = refs[count + 2 : count + 6], refs[count + 6 :]
+    update_blocks(share, steps, pieces, ortho, merged, results, updates, errors, sems, lambda: None)
+
+
+def last_kernel(share, stat_share, steps, parts, *refs):
+    pieces, (ortho, merged) = refs[:parts], refs[parts : parts + 2]
+    results, small_results = refs[parts + 6 : parts + 10], refs[parts + 10 : parts + 14]
+    rights, *small = refs[parts + 14 : parts + 19]
+    small_sems, updates, errors, sems = refs[parts + 19 :]
+    in_basis, out_basis, table, gain = small
+    quarter = rights.shape[2] - LANES
+    copies = []
+
+    def small_outputs():
+        for step, piece in enumerate(pieces):
+            rights[step] = piece[...].astype(F32)
+        tiles = []
+        for block in range(parts):
+            here = rights[jnp.bitwise_xor(lax.axis_index("dp") % 4, block)]
+            right = here[:, :quarter] * share
+            tiles.append(stats_pair(here[:, quarter:]) * stat_share)
+            if block < parts - 1:
+                in_basis[:, block * quarter : (block + 1) * quarter] = right
+            else:
+                out_basis[...] = right
+        stats = jnp.concatenate(tiles, axis=1)
+        table[...] = stats[:, : table.shape[1]]
+        padded = stats.shape[1] - 2 * LANES
+        for at in range(gain.shape[1] // LANES):
+            gain[:, at * LANES : (at + 1) * LANES] = stats[at : at + 1, padded : padded + LANES]
+        copies.extend(fetch(list(zip(small, small_results)), small_sems))
+
+    update_blocks(
+        share, steps, pieces, ortho, merged, results, updates, errors, sems, small_outputs
+    )
     for copy in copies:
         copy.wait()
 
@@ -618,25 +656,21 @@
         functools.partial(attend_kernel, blocks, 1.0 / n_mp),
         (shape((width, both), BF16),) * blocks
         + (left_shape,) * blocks
-        + (shape((head_count, span // blocks, span), F32),) * blocks
-        + (shape((row_count, wide), BF16), shape((SUBLANES, LANES), F32)),
+        + (shape((head_count, span, span), F32), shape((row_count, wide), BF16)),
         [
             pltpu.VMEM((row_count, wide), BF16),
             pltpu.VMEM((row_count, features), BF16),
             pltpu.VMEM((row_count, features), BF16),
             pltpu.VMEM((head_count, span, span), F32),
-            pltpu.VMEM((1, features), F32),
-            pltpu.VMEM((head_count, span, span), F32),
         ],
         flops=4 * row_count * features * both,
         moved=8 << 20,
-        in_specs=[VMEM] * (13 + len(arrived)),
-        out_specs=[VMEM] * (3 * blocks + 2),
-    )(normed, part, bias, index_t, table_pad, bucket, gain, cot_rows, region, w_in_own, *own, *arrived)
-    terms, lefts, score_parts = (
-        outputs[at * blocks : (at + 1) * blocks] for at in range(3)
-    )
-    packed, gain_term = outputs[3 * blocks :]
+        in_specs=[VMEM] * (12 + len(arrived)),
+        out_specs=[VMEM] * (2 * blocks + 2),
+    )(normed, part, bias, index_t, table_pad, bucket, cot_rows, region, w_in_own, *own, *arrived)
+    *outputs, score_sum, packed = outputs
+    terms, lefts = outputs[:blocks], outputs[blocks:]
+    scores_of = [score_sum]
 
     if blocks == 2:
         left_other = exchange(lefts[1], "mp", n_mp, 1)
@@ -661,23 +695,24 @@
     if blocks == 2:
         left, term_sent, score_sent = call(
             join_kernel,
-            tuple(shape(array.shape, array.dtype) for array in (left, terms[1], score_parts[1])),
+            tuple(shape(array.shape, array.dtype) for array in (left, terms[1], score_sum)),
             in_specs=[VMEM] * 2 + [ANY] * 2,
             out_specs=[VMEM] + [ANY] * 2,
             input_output_aliases={2: 1, 3: 2},
-        )(left, left_other, terms[1], score_parts[1])
-        score_parts = [score_parts[0], exchange(score_sent, "mp", n_mp, 1)]
+        )(left, left_other, terms[1], score_sum)
+        scores_of = [score_sent, exchange(score_sent, "mp", n_mp, 1)]
+        terms = [terms[0], term_sent]
         term_parts = [terms[0], exchange(term_sent, "mp", n_mp, 1)]
 
     stats = call(
         functools.partial(table_kernel, blocks),
         shape((head_count, padded + 2 * LANES), F32),
+        [pltpu.VMEM((1, features), F32)],
         flops=2 * row_count * features * wide,
         moved=4 << 20,
-        in_specs=[VMEM] * (blocks + 2),
+        in_specs=[VMEM] * (3 * blocks + 2),
         out_specs=VMEM,
-    )(*score_parts, gain_term, index_t)
-
+    )(*scores_of, *terms, w_in_own, *arrived[:1], gain, index_t)
     if blocks == 2:
         stats = [stats, exchange(stats, "mp", n_mp, 1)]
     else:
@@ -745,33 +780,44 @@
         held = reduced(partners(held, "dp", n_dp, *group))
     pieces = partners(held, "dp", n_dp, stride, parts)
 
+    big = (
+        shape((row_block, wide), F32),
+        shape((row_block, features), F32),
+        shape((row_block, wide), F32),
+        shape((row_block, features), F32),
+    )
     small = (
         shape((rank, wide), F32),
         shape((rank, features), F32),
         shape((head_count, buckets), F32),
         shape((1, features), F32),
     )
+    early, late = (0, parts - 1), tuple(range(parts - 2, 0, -1))
+
+    def staging(steps):
+        return [pltpu.VMEM((len(steps), row_block, quarter), F32)] * 2 + [
+            pltpu.SemaphoreType.DMA((len(steps), 2))
+        ]
+
+    results = call(
+        functools.partial(first_kernel, 1.0 / n_dp, early),
+        big,
+        staging(early),
+        flops=24 * row_block * quarter * rank,
+        moved=1 << 20,
+        in_specs=[VMEM] * (len(early) + 2),
+        out_specs=[HBM] * 4,
+    )(*(pieces[step] for step in early), ortho, merged)
     in_update, out_update, in_new_error, out_new_error, in_right, out_right, table, gain = call(
-        functools.partial(update_kernel, 1.0 / n_dp, 1.0 / (n_dp * n_mp), parts),
-        (
-            shape((row_block, wide), F32),
-            shape((row_block, features), F32),
-            shape((row_block, wide), F32),
-            shape((row_block, features), F32),
-            *small,
-        ),
-        [
-            pltpu.VMEM((parts, rank, quarter + LANES), F32),
-            pltpu.VMEM((parts, row_block, quarter), F32),
-            pltpu.VMEM((parts, row_block, quarter), F32),
-            pltpu.SemaphoreType.DMA((parts, 2)),
-        ]
-        + buffers(*small),
-        flops=12 * row_block * both * rank,
-        moved=8 << 20,
-        in_specs=[VMEM] * (parts + 2),
+        functools.partial(last_kernel, 1.0 / n_dp, 1.0 / (n_dp * n_mp), late, parts),
+        big + small,
+        [pltpu.VMEM((parts, rank, quarter + LANES), F32)] + buffers(*small) + staging(late),
+        flops=24 * row_block * quarter * rank,
+        moved=1 << 20,
+        in_specs=[VMEM] * (parts + 2) + [HBM] * 4,
         out_specs=[HBM] * 8,
-    )(*pieces, ortho, merged)
+        input_output_aliases={2 + parts + at: at for at in range(4)},
+    )(*pieces, ortho, merged, *in_hbm(*results))
 
     return (
         token_grad.reshape(tokens.shape),

time: 59.7 us -> 58.8 us (0.985)
  waiting for transfers between devices: 14.2 us -> 12.4 us
  Pallas kernels: 21.5 us -> 22.5 us
    ppermute x23, waiting for transfers between devices: 14.2 us -> 12.4 us  [exchange(): lax.ppermute(value, axis, [(at, at ^ distance) for at in range(count)])]
    pallas_call x1 -> x2, Pallas kernels: 2.47 us -> 3.38 us  [the longest x1 1.77 us: shards(): call(functools.partial(last_kernel, 1.0 / n_dp, 1.0 / (n_dp * n_mp), late...]
  transfers between devices with their start and end apart: 23 -> 23, of which waited for: 11 -> 10; matrix products, arithmetic and copies ran while one was open for 0% -> 0% of each run, Pallas kernels for 14% -> 17%
where the time goes in v3:
time: 58.8 us; the launch traced here: 58.7 us
  starting transfers between devices  22.8 us (39%)
  Pallas kernels  22.5 us (38%)
  waiting for transfers between devices  12.4 us (21%)
  between operations  0.95 us (2%)
    ppermute x23, starting transfers between devices, exchange(): lax.ppermute(value, axis, [(at, at ^ distance) for at in range(count)])  22.8 us
    ppermute x23, waiting for transfers between devices, exchange(): lax.ppermute(value, axis, [(at, at ^ distance) for at in range(count)])  12.4 us
    pallas_call x1, Pallas kernels, shards(): call(functools.partial(attend_kernel, blocks, 1.0 / n_mp), (shape((width,...  7.04 us
    pallas_call x1, Pallas kernels, shards(): call(functools.partial(ortho_kernel, 1.0 / n_dp, len(lefts), len(stats)),...  3.43 us
    pallas_call x1, Pallas kernels, shards(): call(functools.partial(table_kernel, blocks), shape((head_count, padded +...  2.98 us
    pallas_call x1, Pallas kernels, shards(): call(functools.partial(prepare_kernel, blocks, READY_HEADS), (shape((row_...  2.58 us
    pallas_call x1, Pallas kernels, shards(): call(functools.partial(last_kernel, 1.0 / n_dp, 1.0 / (n_dp * n_mp), late...  1.77 us
    pallas_call x1, Pallas kernels, shards(): call(functools.partial(token_kernel, blocks), (shape((row_count, features...  1.71 us
  transfers between devices with their start and end apart: 23, of which 10 were waited for; matrix products, arithmetic and copies ran while one was open for 0% of the time, Pallas kernels for 17%

profile of v3, /device:TPU:0, one launch (start us, length us, event | category | flops | bytes accessed | tf_op | source)
XLA Modules:
  0.0 58.7 jit_solution(1317731996219191024)
XLA Ops:
  0.6 0.5 collective-permute-start
  1.8 2.6 %shard_map.187 = (bf16[288,512]{1,0:T(8,128)(2,1)S(1)}, f32[288,1536]{1,0:T(8,128)S(1)}, f32[2,144,144]{2,1,0:T(8,128)S(1)}, s32[144,144]{1,0:T(8,128)S(1)}, f32...) custom-call(s32[144,144]{1,0:T(8,128)} %refs_0_.1, ...), custom_call_target="tpu_custom_call" | custom-call | flops 226492416 | bytes 4194304 | tf_op jit(solution)/shard_map/pallas_call | solution.py:634
  4.4 7.0 %shard_map.188 = (bf16[256,2048]{1,0:T(8,128)(2,1)S(1)}, bf16[256,2048]{1,0:T(8,128)(2,1)S(1)}, f32[64,256]{1,0:T(8,128)S(1)}, f32[64,256]{1,0:T(8,128)S(1)}, f3...) custom-call(bf16[288,512]{1,0:T(8,128)(2,1)S(1)} %get-tuple-element.53.refs_0_, ...), custom_call_target="tpu_custom_call" | custom-call | flops 1207959552 | bytes 8388608 | tf_op jit(solution)/shard_map/pallas_call | solution.py:655
  11.4 0.5 collective-permute-start.4
  11.9 0.7 %shard_map.189.left_own = f32[64,256]{1,0:T(8,128)S(1)} custom-call(f32[64,256]{1,0:T(8,128)S(1)} %get-tuple-element.68.term_left, f32[256,1536]{1,0:T(8,128)S(1)} %get-tuple-element.69.in_error.refs_2_, f32[256,512]{1,0:T(8,128)S(1)} %get-tuple-element.70.out_error.refs_3_, f32[32,1536]{1,0:T(8,128)S(1)} %get-tuple-element.63.refs_10_.in_basis, ...), custom_call_target="tpu_custom_call" | custom-call | flops 134217728 | bytes 3145728 | tf_op jit(solution)/shard_map/pallas_call | solution.py:687
  13.4 4.9 %collective-permute-start.7 = (f32[64,256]{1,0:T(8,128)S(1)}, f32[64,256]{1,0:T(8,128)S(1)}, u32[]{:S(2)}, u32[]{:S(2)}) collective-permute-start(f32[64,256]{1,0:T(8,128)S(1)} %get-tuple-element.74.refs_0_), channel_id=1, source_target_pairs={{0,24},{2,26},{4,28},{6,30},{8,16},{10,18},{12,20},{14,22},{16,8},... | collective-permute-start | bytes 196616 | tf_op jit(solution)/shard_map/ppermute | solution.py:556
  18.3 0.6 collective-permute-start.5
  18.9 3.0 %shard_map.191.refs_4_ = f32[8,1024]{1,0:T(8,128)S(1)} custom-call(f32[8,144,144]{2,1,0:T(8,128)S(1)} %get-tuple-element.75.refs_0_, f32[8,144,144]{2,1,0:T(8,128)S(1)} %collective-permute-done.8.refs_1_, bf16[256,2048]{1,0:T(8,128)(2,1)S(1)} %get-tuple-element.76.refs_2_.refs_0_, bf16[256,2048]{1,0:T(8,128)(2,1)S(1)} %get-tuple-element.77.refs_3_, ...), custom_call_target="tpu_custom_call" | custom-call | flops 452984832 | bytes 4194304 | tf_op jit(solution)/shard_map/pallas_call | solution.py:707
  21.9 2.3 %collective-permute-done.6.refs_2_ = f32[64,256]{1,0:T(8,128)S(1)} collective-permute-done((f32[64,256]{1,0:T(8,128)S(1)}, f32[64,256]{1,0:T(8,128)S(1)}, u32[]{:S(2)}, u32[]{:S(2)}) %collective-permute-start.6) | collective-permute-done | bytes 65568 | tf_op jit(solution)/shard_map/ppermute | solution.py:556
  24.2 2.5 %collective-permute-start.12 = (f32[64,256]{1,0:T(8,128)S(1)}, f32[64,256]{1,0:T(8,128)S(1)}, u32[]{:S(2)}, u32[]{:S(2)}) collective-permute-start(f32[64,256]{1,0:T(8,128)S(1)} %shard_map.192.refs_0_), channel_id=1, source_target_pairs={{0,6},{2,4},{4,2},{6,0},{8,14},{10,12},{12,10},{14,8},{16,22},{18,... | collective-permute-start | bytes 196616 | tf_op jit(solution)/shard_map/ppermute | solution.py:556
  26.7 0.5 collective-permute-start.11
  27.2 0.5 collective-permute-start.10
  27.8 0.6 shard_map.193.refs_6_.refs_3_.refs_5_
  28.3 1.2 %collective-permute-done.12.refs_3_ = f32[64,256]{1,0:T(8,128)S(1)} collective-permute-done((f32[64,256]{1,0:T(8,128)S(1)}, f32[64,256]{1,0:T(8,128)S(1)}, u32[]{:S(2)}, u32[]{:S(2)}) %collective-permute-start.12) | collective-permute-done | bytes 65568 | tf_op jit(solution)/shard_map/ppermute | solution.py:556
  29.6 1.4 %collective-permute-done.11.refs_2_ = f32[64,256]{1,0:T(8,128)S(1)} collective-permute-done((f32[64,256]{1,0:T(8,128)S(1)}, f32[64,256]{1,0:T(8,128)S(1)}, u32[]{:S(2)}, u32[]{:S(2)}) %collective-permute-start.11) | collective-permute-done | bytes 65568 | tf_op jit(solution)/shard_map/ppermute | solution.py:556
  31.0 0.5 collective-permute-done.10.refs_1_
  31.5 3.4 %shard_map.194 = (f32[64,256]{1,0:T(8,128)S(1)}, bf16[32,640]{1,0:T(8,128)(2,1)S(1)}, bf16[32,640]{1,0:T(8,128)(2,1)S(1)}, bf16[32,640]{1,0:T(8,128)(2,1)S(1)}, bf16[32,640]{1,0:T(8,128)(2,1)S(1)}) custom-call(f32[64,256]{1,0:T(8,128)S(1)} %shard_map.192.refs_0_, f32[64,256]{1,0:T(8,128)S(1)} %collective-permute-done.10.refs_1_, ...), custom_call_target="tpu_custom_call" | custom-call | flops 201326592 | bytes 3145728 | tf_op jit(solution)/shard_map/pallas_call | solution.py:742
  34.9 0.6 collective-permute-start.14
  35.5 1.5 %collective-permute-start.15 = (bf16[32,640]{1,0:T(8,128)(2,1)S(1)}, bf16[32,640]{1,0:T(8,128)(2,1)S(1)}, u32[]{:S(2)}, u32[]{:S(2)}) collective-permute-start(bf16[32,640]{1,0:T(8,128)(2,1)S(1)} %get-tuple-element.82), channel_id=1, source_target_pairs={{0,4},{2,6},{4,0},{6,2},{8,12},{10,14},{12,8},{14,10},{16,20},{18,... | collective-permute-start | bytes 122888 | tf_op jit(solution)/shard_map/ppermute | solution.py:556
  37.0 1.4 %collective-permute-start.16 = (bf16[32,640]{1,0:T(8,128)(2,1)S(1)}, bf16[32,640]{1,0:T(8,128)(2,1)S(1)}, u32[]{:S(2)}, u32[]{:S(2)}) collective-permute-start(bf16[32,640]{1,0:T(8,128)(2,1)S(1)} %get-tuple-element.83), channel_id=1, source_target_pairs={{0,6},{2,4},{4,2},{6,0},{8,14},{10,12},{12,10},{14,8},{16,22},{18,... | collective-permute-start | bytes 122888 | tf_op jit(solution)/shard_map/ppermute | solution.py:556
  38.5 1.7 %shard_map.195 = (bf16[288,512]{1,0:T(8,128)(2,1)}, f32[8,128]{1,0:T(8,128)S(1)}) custom-call(bf16[288,1536]{1,0:T(8,128)(2,1)S(1)} %get-tuple-element.65.packed, bf16[256,1536]{1,0:T(8,128)(2,1)S(1)} %get-tuple-element.61.refs_8_.refs_4_.refs_0_, bf16[256,1536]{1,0:T(8,128)(2,1)S(1)} %collective-permute-done.refs_12_.refs_5_.refs_1_, ...), custom_call_target="tpu_custom_call" | custom-call | flops 452984832 | bytes 4194304 | tf_op jit(solution)/shard_map/pallas_call | solution.py:752
  40.2 1.7 %collective-permute-done.16.refs_3_ = bf16[32,640]{1,0:T(8,128)(2,1)S(1)} collective-permute-done((bf16[32,640]{1,0:T(8,128)(2,1)S(1)}, bf16[32,640]{1,0:T(8,128)(2,1)S(1)}, u32[]{:S(2)}, u32[]{:S(2)}) %collective-permute-start.16) | collective-permute-done | bytes 40992 | tf_op jit(solution)/shard_map/ppermute | solution.py:556
  42.0 2.8 %collective-permute-start.19 = (bf16[32,640]{1,0:T(8,128)(2,1)S(1)}, bf16[32,640]{1,0:T(8,128)(2,1)S(1)}, u32[]{:S(2)}, u32[]{:S(2)}) collective-permute-start(bf16[32,640]{1,0:T(8,128)(2,1)S(1)} %shard_map.196.refs_0_), channel_id=1, source_target_pairs={{0,24},{2,26},{4,28},{6,30},{8,16},{10,18},{12,20},{14,22},{16,8},... | collective-permute-start | bytes 122888 | tf_op jit(solution)/shard_map/ppermute | solution.py:556
  44.8 1.7 %collective-permute-start.17 = (bf16[32,640]{1,0:T(8,128)(2,1)S(1)}, bf16[32,640]{1,0:T(8,128)(2,1)S(1)}, u32[]{:S(2)}, u32[]{:S(2)}) collective-permute-start(bf16[32,640]{1,0:T(8,128)(2,1)S(1)} %shard_map.196.refs_0_), channel_id=1, source_target_pairs={{0,8},{2,10},{4,12},{6,14},{8,0},{10,2},{12,4},{14,6},{16,24},{18,... | collective-permute-start | bytes 122888 | tf_op jit(solution)/shard_map/ppermute | solution.py:556
  46.4 1.4 %collective-permute-done.19.refs_3_ = bf16[32,640]{1,0:T(8,128)(2,1)S(1)} collective-permute-done((bf16[32,640]{1,0:T(8,128)(2,1)S(1)}, bf16[32,640]{1,0:T(8,128)(2,1)S(1)}, u32[]{:S(2)}, u32[]{:S(2)}) %collective-permute-start.19) | collective-permute-done | bytes 40992 | tf_op jit(solution)/shard_map/ppermute | solution.py:556
  47.8 1.8 %collective-permute-done.18.refs_2_ = bf16[32,640]{1,0:T(8,128)(2,1)S(1)} collective-permute-done((bf16[32,640]{1,0:T(8,128)(2,1)S(1)}, bf16[32,640]{1,0:T(8,128)(2,1)S(1)}, u32[]{:S(2)}, u32[]{:S(2)}) %collective-permute-start.18) | collective-permute-done | bytes 40992 | tf_op jit(solution)/shard_map/ppermute | solution.py:556
  49.7 1.5 %collective-permute-start.22 = (bf16[32,640]{1,0:T(8,128)(2,1)S(1)}, bf16[32,640]{1,0:T(8,128)(2,1)S(1)}, u32[]{:S(2)}, u32[]{:S(2)}) collective-permute-start(bf16[32,640]{1,0:T(8,128)(2,1)S(1)} %shard_map.197.refs_0_), channel_id=1, source_target_pairs={{0,6},{2,4},{4,2},{6,0},{8,14},{10,12},{12,10},{14,8},{16,22},{18,... | collective-permute-start | bytes 122888 | tf_op jit(solution)/shard_map/ppermute | solution.py:556
  51.2 1.5 %collective-permute-start.21 = (bf16[32,640]{1,0:T(8,128)(2,1)S(1)}, bf16[32,640]{1,0:T(8,128)(2,1)S(1)}, u32[]{:S(2)}, u32[]{:S(2)}) collective-permute-start(bf16[32,640]{1,0:T(8,128)(2,1)S(1)} %shard_map.197.refs_0_), channel_id=1, source_target_pairs={{0,4},{2,6},{4,0},{6,2},{8,12},{10,14},{12,8},{14,10},{16,20},{18,... | collective-permute-start | bytes 122888 | tf_op jit(solution)/shard_map/ppermute | solution.py:556
  52.7 0.5 collective-permute-start.20
  53.2 1.4 %collective-permute-done.22.refs_1_.refs_3_ = bf16[32,640]{1,0:T(8,128)(2,1)S(1)} collective-permute-done((bf16[32,640]{1,0:T(8,128)(2,1)S(1)}, bf16[32,640]{1,0:T(8,128)(2,1)S(1)}, u32[]{:S(2)}, u32[]{:S(2)}) %collective-permute-start.22) | collective-permute-done | bytes 40992 | tf_op jit(solution)/shard_map/ppermute | solution.py:556
  54.7 1.6 %shard_map.198 = (f32[256,1536]{1,0:T(8,128)}, f32[256,512]{1,0:T(8,128)}, f32[256,1536]{1,0:T(8,128)}, f32[256,512]{1,0:T(8,128)}) custom-call(bf16[32,640]{1,0:T(8,128)(2,1)S(1)} %shard_map.197.refs_0_, bf16[32,640]{1,0:T(8,128)(2,1)S(1)} %collective-permute-done.22.refs_1_.refs_3_, f32[64,256]{1,0:T(8,128)S(1)} %get-tuple-element.78.refs_5_.refs_2_.refs_4_, ...), custom_call_target="tpu_custom_call" | custom-call | flops 100663296 | bytes 1048576 | tf_op jit(solution)/shard_map/pallas_call | solution.py:802
  56.7 1.8 %shard_map.199 = (f32[256,1536]{1,0:T(8,128)}, f32[256,512]{1,0:T(8,128)}, f32[256,1536]{1,0:T(8,128)}, f32[256,512]{1,0:T(8,128)}, f32[32,1536]{1,0:T(8,128)}, ...) custom-call(bf16[32,640]{1,0:T(8,128)(2,1)S(1)} %shard_map.197.refs_, ...), custom_call_target="tpu_custom_call", output_to_operand_aliasing={{0}: (6, {}), {1}: (7, {}), {2}: (8, {}), {3}: (9, {})} | custom-call | flops 100663296 | bytes 1048576 | tf_op jit(solution)/shard_map/pallas_call | solution.py:811
  (27 shorter events, 1.9 us)
Async XLA Ops:
  0.6 3.7 %collective-permute-start = (bf16[256,1536]{1,0:T(8,128)(2,1)}, bf16[256,1536]{1,0:T(8,128)(2,1)S(1)}, u32[]{:S(2)}, u32[]{:S(2)}) collective-permute-start(bf16[256,1536]{1,0:T(8,128)(2,1)} %refs_4_.1), channel_id=1, source_target_pairs={{0,1},{1,0},{2,3},{3,2},{4,5},{5,4},{6,7},{7,6},{8,9},{9,8},{10,11... | collective-permute-start | bytes 2359304 | tf_op jit(solution)/shard_map/ppermute | solution.py:556
  1.2 3.2 %collective-permute-start.1 = (bf16[256,512]{1,0:T(8,128)(2,1)}, bf16[256,512]{1,0:T(8,128)(2,1)S(1)}, u32[]{:S(2)}, u32[]{:S(2)}) collective-permute-start(bf16[256,512]{1,0:T(8,128)(2,1)} %refs_7_.1), channel_id=1, source_target_pairs={{0,1},{1,0},{2,3},{3,2},{4,5},{5,4},{6,7},{7,6},{8,9},{9,8},{10,11... | collective-permute-start | bytes 786440 | tf_op jit(solution)/shard_map/ppermute | solution.py:556
  1.2 3.1 %collective-permute-start.2 = (f32[32,1536]{1,0:T(8,128)}, f32[32,1536]{1,0:T(8,128)S(1)}, u32[]{:S(2)}, u32[]{:S(2)}) collective-permute-start(f32[32,1536]{1,0:T(8,128)} %bitcast.27), channel_id=1, source_target_pairs={{0,1},{1,0},{2,3},{3,2},{4,5},{5,4},{6,7},{7,6},{8,9},{9,8},{10,11... | collective-permute-start | bytes 589832 | tf_op jit(solution)/shard_map/ppermute | solution.py:556
  1.7 2.7 %collective-permute-start.3 = (f32[32,512]{1,0:T(8,128)}, f32[32,512]{1,0:T(8,128)S(1)}, u32[]{:S(2)}, u32[]{:S(2)}) collective-permute-start(f32[32,512]{1,0:T(8,128)} %bitcast.29), channel_id=1, source_target_pairs={{0,1},{1,0},{2,3},{3,2},{4,5},{5,4},{6,7},{7,6},{8,9},{9,8},{10,11... | collective-permute-start | bytes 196616 | tf_op jit(solution)/shard_map/ppermute | solution.py:556
  11.4 1.4 %collective-permute-start.4 = (f32[64,256]{1,0:T(8,128)S(1)}, f32[64,256]{1,0:T(8,128)S(1)}, u32[]{:S(2)}, u32[]{:S(2)}) collective-permute-start(f32[64,256]{1,0:T(8,128)S(1)} %get-tuple-element.71), channel_id=1, source_target_pairs={{0,1},{1,0},{2,3},{3,2},{4,5},{5,4},{6,7},{7,6},{8,9},{9,8},{10,11... | collective-permute-start | bytes 196616 | tf_op jit(solution)/shard_map/ppermute | solution.py:556
  12.8 15.0 %collective-permute-start.13 = (bf16[256,2048]{1,0:T(8,128)(2,1)S(1)}, bf16[256,2048]{1,0:T(8,128)(2,1)S(1)}, u32[]{:S(2)}, u32[]{:S(2)}) collective-permute-start(bf16[256,2048]{1,0:T(8,128)(2,1)S(1)} %get-tuple-element.77.refs_3_), channel_id=1, source_target_pairs={{0,1},{1,0},{2,3},{3,2},{4,5},{5,4},{6,7},{7,6},{8,9},{9,8},{10,11... | collective-permute-start | bytes 3145736 | tf_op jit(solution)/shard_map/ppermute | solution.py:556
  13.2 5.6 %collective-permute-start.8 = (f32[8,144,144]{2,1,0:T(8,128)S(1)}, f32[8,144,144]{2,1,0:T(8,128)S(1)}, u32[]{:S(2)}, u32[]{:S(2)}) collective-permute-start(f32[8,144,144]{2,1,0:T(8,128)S(1)} %get-tuple-element.75.refs_0_), channel_id=1, source_target_pairs={{0,1},{1,0},{2,3},{3,2},{4,5},{5,4},{6,7},{7,6},{8,9},{9,8},{10,11... | collective-permute-start | bytes 1990664 | tf_op jit(solution)/shard_map/ppermute | solution.py:556
  13.4 8.5 %collective-permute-start.7 = (f32[64,256]{1,0:T(8,128)S(1)}, f32[64,256]{1,0:T(8,128)S(1)}, u32[]{:S(2)}, u32[]{:S(2)}) collective-permute-start(f32[64,256]{1,0:T(8,128)S(1)} %get-tuple-element.74.refs_0_), channel_id=1, source_target_pairs={{0,24},{2,26},{4,28},{6,30},{8,16},{10,18},{12,20},{14,22},{16,8},... | collective-permute-start | bytes 196616 | tf_op jit(solution)/shard_map/ppermute | solution.py:556
  18.3 5.9 %collective-permute-start.6 = (f32[64,256]{1,0:T(8,128)S(1)}, f32[64,256]{1,0:T(8,128)S(1)}, u32[]{:S(2)}, u32[]{:S(2)}) collective-permute-start(f32[64,256]{1,0:T(8,128)S(1)} %get-tuple-element.74.refs_0_), channel_id=1, source_target_pairs={{0,16},{2,18},{4,20},{6,22},{8,24},{10,26},{12,28},{14,30},{16,0},... | collective-permute-start | bytes 196616 | tf_op jit(solution)/shard_map/ppermute | solution.py:556
  18.3 5.9 %collective-permute-start.5 = (f32[64,256]{1,0:T(8,128)S(1)}, f32[64,256]{1,0:T(8,128)S(1)}, u32[]{:S(2)}, u32[]{:S(2)}) collective-permute-start(f32[64,256]{1,0:T(8,128)S(1)} %get-tuple-element.74.refs_0_), channel_id=1, source_target_pairs={{0,8},{2,10},{4,12},{6,14},{8,0},{10,2},{12,4},{14,6},{16,24},{18,... | collective-permute-start | bytes 196616 | tf_op jit(solution)/shard_map/ppermute | solution.py:556
  21.8 2.4 %collective-permute-start.9 = (f32[8,1024]{1,0:T(8,128)S(1)}, f32[8,1024]{1,0:T(8,128)S(1)}, u32[]{:S(2)}, u32[]{:S(2)}) collective-permute-start(f32[8,1024]{1,0:T(8,128)S(1)} %shard_map.191.refs_4_), channel_id=1, source_target_pairs={{0,1},{1,0},{2,3},{3,2},{4,5},{5,4},{6,7},{7,6},{8,9},{9,8},{10,11... | collective-permute-start | bytes 98312 | tf_op jit(solution)/shard_map/ppermute | solution.py:556
  24.2 5.3 %collective-permute-start.12 = (f32[64,256]{1,0:T(8,128)S(1)}, f32[64,256]{1,0:T(8,128)S(1)}, u32[]{:S(2)}, u32[]{:S(2)}) collective-permute-start(f32[64,256]{1,0:T(8,128)S(1)} %shard_map.192.refs_0_), channel_id=1, source_target_pairs={{0,6},{2,4},{4,2},{6,0},{8,14},{10,12},{12,10},{14,8},{16,22},{18,... | collective-permute-start | bytes 196616 | tf_op jit(solution)/shard_map/ppermute | solution.py:556
  26.7 4.3 %collective-permute-start.11 = (f32[64,256]{1,0:T(8,128)S(1)}, f32[64,256]{1,0:T(8,128)S(1)}, u32[]{:S(2)}, u32[]{:S(2)}) collective-permute-start(f32[64,256]{1,0:T(8,128)S(1)} %shard_map.192.refs_0_), channel_id=1, source_target_pairs={{0,4},{2,6},{4,0},{6,2},{8,12},{10,14},{12,8},{14,10},{16,20},{18,... | collective-permute-start | bytes 196616 | tf_op jit(solution)/shard_map/ppermute | solution.py:556
  27.2 4.3 %collective-permute-start.10 = (f32[64,256]{1,0:T(8,128)S(1)}, f32[64,256]{1,0:T(8,128)S(1)}, u32[]{:S(2)}, u32[]{:S(2)}) collective-permute-start(f32[64,256]{1,0:T(8,128)S(1)} %shard_map.192.refs_0_), channel_id=1, source_target_pairs={{0,2},{2,0},{4,6},{6,4},{8,10},{10,8},{12,14},{14,12},{16,18},{18,... | collective-permute-start | bytes 196616 | tf_op jit(solution)/shard_map/ppermute | solution.py:556
  34.9 5.2 %collective-permute-start.14 = (bf16[32,640]{1,0:T(8,128)(2,1)S(1)}, bf16[32,640]{1,0:T(8,128)(2,1)S(1)}, u32[]{:S(2)}, u32[]{:S(2)}) collective-permute-start(bf16[32,640]{1,0:T(8,128)(2,1)S(1)} %get-tuple-element.81), channel_id=1, source_target_pairs={{0,2},{2,0},{4,6},{6,4},{8,10},{10,8},{12,14},{14,12},{16,18},{18,... | collective-permute-start | bytes 122888 | tf_op jit(solution)/shard_map/ppermute | solution.py:556
  35.5 4.7 %collective-permute-start.15 = (bf16[32,640]{1,0:T(8,128)(2,1)S(1)}, bf16[32,640]{1,0:T(8,128)(2,1)S(1)}, u32[]{:S(2)}, u32[]{:S(2)}) collective-permute-start(bf16[32,640]{1,0:T(8,128)(2,1)S(1)} %get-tuple-element.82), channel_id=1, source_target_pairs={{0,4},{2,6},{4,0},{6,2},{8,12},{10,14},{12,8},{14,10},{16,20},{18,... | collective-permute-start | bytes 122888 | tf_op jit(solution)/shard_map/ppermute | solution.py:556
  37.0 4.9 %collective-permute-start.16 = (bf16[32,640]{1,0:T(8,128)(2,1)S(1)}, bf16[32,640]{1,0:T(8,128)(2,1)S(1)}, u32[]{:S(2)}, u32[]{:S(2)}) collective-permute-start(bf16[32,640]{1,0:T(8,128)(2,1)S(1)} %get-tuple-element.83), channel_id=1, source_target_pairs={{0,6},{2,4},{4,2},{6,0},{8,14},{10,12},{12,10},{14,8},{16,22},{18,... | collective-permute-start | bytes 122888 | tf_op jit(solution)/shard_map/ppermute | solution.py:556
  42.0 5.9 %collective-permute-start.19 = (bf16[32,640]{1,0:T(8,128)(2,1)S(1)}, bf16[32,640]{1,0:T(8,128)(2,1)S(1)}, u32[]{:S(2)}, u32[]{:S(2)}) collective-permute-start(bf16[32,640]{1,0:T(8,128)(2,1)S(1)} %shard_map.196.refs_0_), channel_id=1, source_target_pairs={{0,24},{2,26},{4,28},{6,30},{8,16},{10,18},{12,20},{14,22},{16,8},... | collective-permute-start | bytes 122888 | tf_op jit(solution)/shard_map/ppermute | solution.py:556
  44.8 4.9 %collective-permute-start.18 = (bf16[32,640]{1,0:T(8,128)(2,1)S(1)}, bf16[32,640]{1,0:T(8,128)(2,1)S(1)}, u32[]{:S(2)}, u32[]{:S(2)}) collective-permute-start(bf16[32,640]{1,0:T(8,128)(2,1)S(1)} %shard_map.196.refs_0_), channel_id=1, source_target_pairs={{0,16},{2,18},{4,20},{6,22},{8,24},{10,26},{12,28},{14,30},{16,0},... | collective-permute-start | bytes 122888 | tf_op jit(solution)/shard_map/ppermute | solution.py:556
  44.8 4.9 %collective-permute-start.17 = (bf16[32,640]{1,0:T(8,128)(2,1)S(1)}, bf16[32,640]{1,0:T(8,128)(2,1)S(1)}, u32[]{:S(2)}, u32[]{:S(2)}) collective-permute-start(bf16[32,640]{1,0:T(8,128)(2,1)S(1)} %shard_map.196.refs_0_), channel_id=1, source_target_pairs={{0,8},{2,10},{4,12},{6,14},{8,0},{10,2},{12,4},{14,6},{16,24},{18,... | collective-permute-start | bytes 122888 | tf_op jit(solution)/shard_map/ppermute | solution.py:556
  49.7 5.0 %collective-permute-start.22 = (bf16[32,640]{1,0:T(8,128)(2,1)S(1)}, bf16[32,640]{1,0:T(8,128)(2,1)S(1)}, u32[]{:S(2)}, u32[]{:S(2)}) collective-permute-start(bf16[32,640]{1,0:T(8,128)(2,1)S(1)} %shard_map.197.refs_0_), channel_id=1, source_target_pairs={{0,6},{2,4},{4,2},{6,0},{8,14},{10,12},{12,10},{14,8},{16,22},{18,... | collective-permute-start | bytes 122888 | tf_op jit(solution)/shard_map/ppermute | solution.py:556
  51.2 5.1 %collective-permute-start.21 = (bf16[32,640]{1,0:T(8,128)(2,1)S(1)}, bf16[32,640]{1,0:T(8,128)(2,1)S(1)}, u32[]{:S(2)}, u32[]{:S(2)}) collective-permute-start(bf16[32,640]{1,0:T(8,128)(2,1)S(1)} %shard_map.197.refs_0_), channel_id=1, source_target_pairs={{0,4},{2,6},{4,0},{6,2},{8,12},{10,14},{12,8},{14,10},{16,20},{18,... | collective-permute-start | bytes 122888 | tf_op jit(solution)/shard_map/ppermute | solution.py:556
  52.7 4.0 %collective-permute-start.20 = (bf16[32,640]{1,0:T(8,128)(2,1)S(1)}, bf16[32,640]{1,0:T(8,128)(2,1)S(1)}, u32[]{:S(2)}, u32[]{:S(2)}) collective-permute-start(bf16[32,640]{1,0:T(8,128)(2,1)S(1)} %shard_map.197.refs_0_), channel_id=1, source_target_pairs={{0,2},{2,0},{4,6},{6,4},{8,10},{10,8},{12,14},{14,12},{16,18},{18,... | collective-permute-start | bytes 122888 | tf_op jit(solution)/shard_map/ppermute | solution.py:556

commit v4 on v3

--- a/solution.py
+++ b/solution.py
@@ -110,8 +110,8 @@
 
 def prepare_kernel(blocks, ready, *refs):
     sources, rest = refs[:12], refs[12:]
-    normed, part, bias, index_t, table_pad, bucket, *kept = rest[:16]
-    table, sems = rest[16:]
+    normed, normed_t, part, bias, index_t, table_pad, bucket, *kept = rest[:17]
+    table, sems = rest[17:]
     copies = fetch(list(zip(sources, [bucket, table] + kept)), sems)
     tokens, gain, w_own = kept[:3]
     me = lax.axis_index("mp")
@@ -128,15 +128,16 @@
         copy.wait()
     x_hat, _ = norm_forward(tokens[...])
     normed[...] = (x_hat * gain[...]).astype(BF16)
+    normed_t[...] = normed[...].T
     part[...] = nn(normed[:, block_columns(me, 0, blocks, width)], w_own[...])
     for copy in copies[5:]:
         copy.wait()
 
 
 def attend_kernel(blocks, share, *refs):
-    normed, part, bias_ready, index_t, table_pad, bucket, cot, region = refs[:8]
-    own, arrived = refs[8:12], refs[12 : 8 + 4 * blocks]
-    rest = refs[8 + 4 * blocks :]
+    normed, normed_t, part, bias_ready, index_t, table_pad, bucket, cot, region = refs[:9]
+    own, arrived = refs[9:13], refs[13 : 9 + 4 * blocks]
+    rest = refs[9 + 4 * blocks :]
     terms, lefts, rest = rest[:blocks], rest[blocks : 2 * blocks], rest[2 * blocks :]
     score_sum, packed, proj, mixed_grad, mixed, bias = rest
     w_in, w_out, in_basis, out_basis = (
@@ -160,19 +161,25 @@
         ).astype(BF16)
     lane = lax.broadcasted_iota(jnp.int32, (span, LANES), 1)
     per_group = LANES // head_size
+    allowed_in = []
     for window in range(window_count):
-        rows = pl.ds(window * span, span)
         ids_row = jnp.broadcast_to(region[window : window + 1, :], (span, span))
-        allowed = ids_row == ids_row.T
-        for group in range(features // LANES):
-            start = group * LANES
-            heads = slice(group * per_group, (group + 1) * per_group)
-            if heads.stop <= ready:
-                pair_bias = bias_ready[heads]
-            else:
-                if window == 0:
-                    gather_bias(bias, range(heads.start, heads.stop), table_pad, index_t, bucket)
-                pair_bias = bias[heads]
+        allowed_in.append(ids_row == ids_row.T)
+    wide = 3 * features
+    rank = in_basis[0].shape[0]
+    left_sums = [[] for _ in range(blocks)]
+    span_columns = 2 * LANES
+    for group in range(features // LANES):
+        start = group * LANES
+        heads = slice(group * per_group, (group + 1) * per_group)
+        if heads.stop <= ready:
+            pair_bias = bias_ready[heads]
+        else:
+            gather_bias(bias, range(heads.start, heads.stop), table_pad, index_t, bucket)
+            pair_bias = bias[heads]
+        for window in range(window_count):
+            rows = pl.ds(window * span, span)
+            allowed = allowed_in[window]
             q = proj[rows, start : start + LANES]
             k = proj[rows, features + start : features + start + LANES]
             v = proj[rows, 2 * features + start : 2 * features + start + LANES]
@@ -213,18 +220,22 @@
                 BF16
             )
             packed[rows, 2 * features + start : 2 * features + start + LANES] = v_grad.astype(BF16)
-    wide = 3 * features
+        if (start + LANES) % span_columns:
+            continue
+        for third in range(3):
+            first = third * features + start + LANES - span_columns
+            columns = slice(first, first + span_columns)
+            for step in range(blocks):
+                rows = block_columns(me, step, blocks, width)
+                term = nn(normed_t[rows, :], packed[:, columns]).astype(BF16)
+                terms[step][:, columns] = term
+                left_sums[step].append(nt(stacked(in_basis[step][:, columns]), term))
     for step in range(blocks):
         columns = block_columns(me, step, blocks, width)
-        terms[step][:, :wide] = tn(normed[:, columns], packed[...]).astype(BF16)
-        terms[step][:, wide:] = tn(mixed[:, columns], cot[...]).astype(BF16)
-        rank = in_basis[step].shape[0]
-        for basis, at, place in (
-            (in_basis[step], slice(None, wide), 0),
-            (out_basis[step], slice(wide, None), rank),
-        ):
-            left = folded(nt(stacked(basis[...]), terms[step][:, at])) * share
-            lefts[step][place : place + rank, :] = left
+        term = tn(mixed[:, columns], cot[...]).astype(BF16)
+        terms[step][:, wide:] = term
+        lefts[step][:rank, :] = folded(tree_add(left_sums[step])) * share
+        lefts[step][rank:, :] = folded(nt(stacked(out_basis[step][...]), term)) * share
 
 
 def token_kernel(blocks, packed, *refs):
@@ -631,10 +642,11 @@
         in_error[0],
         out_error[0],
     )
-    normed, part, bias, index_t, table_pad, bucket, *kept = call(
+    normed, normed_t, part, bias, index_t, table_pad, bucket, *kept = call(
         functools.partial(prepare_kernel, blocks, READY_HEADS),
         (
             shape((row_count, features), BF16),
+            shape((features, row_count), BF16),
             shape((row_count, wide), F32),
             shape((READY_HEADS, span, span), F32),
             shape((span, span), jnp.int32),
@@ -646,7 +658,7 @@
         flops=2 * row_count * width * wide,
         moved=4 << 20,
         in_specs=[HBM] * 12,
-        out_specs=[VMEM] * 16,
+        out_specs=[VMEM] * 17,
     )(*in_hbm(*operands))
     token_rows, gain, w_in_own, cot_rows, region, *own, in_errors, out_errors = kept
     in_basis_t, out_basis_t = own[1:]
@@ -665,9 +677,9 @@
         ],
         flops=4 * row_count * features * both,
         moved=8 << 20,
-        in_specs=[VMEM] * (12 + len(arrived)),
+        in_specs=[VMEM] * (13 + len(arrived)),
         out_specs=[VMEM] * (2 * blocks + 2),
-    )(normed, part, bias, index_t, table_pad, bucket, cot_rows, region, w_in_own, *own, *arrived)
+    )(normed, normed_t, part, bias, index_t, table_pad, bucket, cot_rows, region, w_in_own, *own, *arrived)
     *outputs, score_sum, packed = outputs
     terms, lefts = outputs[:blocks], outputs[blocks:]
     scores_of = [score_sum]

time: 58.8 us -> 60 us (1.020)
  Pallas kernels: 22.5 us -> 23.4 us
    pallas_call x1, Pallas kernels: 7.04 us -> 8.13 us  [shards(): call(functools.partial(attend_kernel, blocks, 1.0 / n_mp), (shape((width,...]
where the time goes in v4:
time: 60 us; the launch traced here: 59.8 us
  Pallas kernels  23.4 us (39%)
  starting transfers between devices  22.9 us (38%)
  waiting for transfers between devices  12.6 us (21%)
  between operations  0.94 us (2%)
    ppermute x23, starting transfers between devices, exchange(): lax.ppermute(value, axis, [(at, at ^ distance) for at in range(count)])  22.9 us
    ppermute x23, waiting for transfers between devices, exchange(): lax.ppermute(value, axis, [(at, at ^ distance) for at in range(count)])  12.6 us
    pallas_call x1, Pallas kernels, shards(): call(functools.partial(attend_kernel, blocks, 1.0 / n_mp), (shape((width,...  8.13 us
    pallas_call x1, Pallas kernels, shards(): call(functools.partial(ortho_kernel, 1.0 / n_dp, len(lefts), len(stats)),...  3.43 us
    pallas_call x1, Pallas kernels, shards(): call(functools.partial(table_kernel, blocks), shape((head_count, padded +...  2.98 us
    pallas_call x1, Pallas kernels, shards(): call(functools.partial(prepare_kernel, blocks, READY_HEADS), (shape((row_...  2.58 us
    pallas_call x1, Pallas kernels, shards(): call(functools.partial(last_kernel, 1.0 / n_dp, 1.0 / (n_dp * n_mp), late...  1.77 us
    pallas_call x1, Pallas kernels, shards(): call(functools.partial(token_kernel, blocks), (shape((row_count, features...  1.7 us
  transfers between devices with their start and end apart: 23, of which 10 were waited for; matrix products, arithmetic and copies ran while one was open for 0% of the time, Pallas kernels for 17%

profile of v4, /device:TPU:0, one launch (start us, length us, event | category | flops | bytes accessed | tf_op | source)
XLA Modules:
  0.0 59.8 jit_solution(11009389737685091364)
XLA Ops:
  0.6 0.5 collective-permute-start
  1.2 0.4 collective-permute-start.2
  1.8 2.6 %shard_map.187 = (bf16[288,512]{1,0:T(8,128)(2,1)S(1)}, bf16[512,288]{1,0:T(8,128)(2,1)S(1)}, f32[288,1536]{1,0:T(8,128)S(1)}, f32[2,144,144]{2,1,0:T(8,128)S(1)...) custom-call(s32[144,144]{1,0:T(8,128)} %refs_0_.1, ...), custom_call_target="tpu_custom_call" | custom-call | flops 226492416 | bytes 4194304 | tf_op jit(solution)/shard_map/pallas_call | solution.py:645
  4.4 8.1 %shard_map.188 = (bf16[256,2048]{1,0:T(8,128)(2,1)S(1)}, bf16[256,2048]{1,0:T(8,128)(2,1)S(1)}, f32[64,256]{1,0:T(8,128)S(1)}, f32[64,256]{1,0:T(8,128)S(1)}, f3...) custom-call(bf16[288,512]{1,0:T(8,128)(2,1)S(1)} %get-tuple-element.54.refs_0_, ...), custom_call_target="tpu_custom_call" | custom-call | flops 1207959552 | bytes 8388608 | tf_op jit(solution)/shard_map/pallas_call | solution.py:667
  12.5 0.5 collective-permute-start.4
  13.0 0.8 %shard_map.189.left_own = f32[64,256]{1,0:T(8,128)S(1)} custom-call(f32[64,256]{1,0:T(8,128)S(1)} %get-tuple-element.70.term_left, f32[256,1536]{1,0:T(8,128)S(1)} %get-tuple-element.71.in_error.refs_2_, f32[256,512]{1,0:T(8,128)S(1)} %get-tuple-element.72.out_error.refs_3_, f32[32,1536]{1,0:T(8,128)S(1)} %get-tuple-element.65.refs_11_.in_basis, ...), custom_call_target="tpu_custom_call" | custom-call | flops 134217728 | bytes 3145728 | tf_op jit(solution)/shard_map/pallas_call | solution.py:699
  14.5 4.9 %collective-permute-start.7 = (f32[64,256]{1,0:T(8,128)S(1)}, f32[64,256]{1,0:T(8,128)S(1)}, u32[]{:S(2)}, u32[]{:S(2)}) collective-permute-start(f32[64,256]{1,0:T(8,128)S(1)} %get-tuple-element.76.refs_0_), channel_id=1, source_target_pairs={{0,24},{2,26},{4,28},{6,30},{8,16},{10,18},{12,20},{14,22},{16,8},... | collective-permute-start | bytes 196616 | tf_op jit(solution)/shard_map/ppermute | solution.py:567
  19.5 0.6 collective-permute-start.5
  20.0 3.0 %shard_map.191.refs_4_ = f32[8,1024]{1,0:T(8,128)S(1)} custom-call(f32[8,144,144]{2,1,0:T(8,128)S(1)} %get-tuple-element.77.refs_0_, f32[8,144,144]{2,1,0:T(8,128)S(1)} %collective-permute-done.8.refs_1_, bf16[256,2048]{1,0:T(8,128)(2,1)S(1)} %get-tuple-element.78.refs_2_.refs_0_, bf16[256,2048]{1,0:T(8,128)(2,1)S(1)} %get-tuple-element.79.refs_3_, ...), custom_call_target="tpu_custom_call" | custom-call | flops 452984832 | bytes 4194304 | tf_op jit(solution)/shard_map/pallas_call | solution.py:719
  23.1 2.3 %collective-permute-done.6.refs_2_ = f32[64,256]{1,0:T(8,128)S(1)} collective-permute-done((f32[64,256]{1,0:T(8,128)S(1)}, f32[64,256]{1,0:T(8,128)S(1)}, u32[]{:S(2)}, u32[]{:S(2)}) %collective-permute-start.6) | collective-permute-done | bytes 65568 | tf_op jit(solution)/shard_map/ppermute | solution.py:567
  25.4 2.5 %collective-permute-start.12 = (f32[64,256]{1,0:T(8,128)S(1)}, f32[64,256]{1,0:T(8,128)S(1)}, u32[]{:S(2)}, u32[]{:S(2)}) collective-permute-start(f32[64,256]{1,0:T(8,128)S(1)} %shard_map.192.refs_0_), channel_id=1, source_target_pairs={{0,6},{2,4},{4,2},{6,0},{8,14},{10,12},{12,10},{14,8},{16,22},{18,... | collective-permute-start | bytes 196616 | tf_op jit(solution)/shard_map/ppermute | solution.py:567
  27.9 0.5 collective-permute-start.11
  28.4 0.5 collective-permute-start.10
  29.3 1.4 %collective-permute-done.12.refs_3_ = f32[64,256]{1,0:T(8,128)S(1)} collective-permute-done((f32[64,256]{1,0:T(8,128)S(1)}, f32[64,256]{1,0:T(8,128)S(1)}, u32[]{:S(2)}, u32[]{:S(2)}) %collective-permute-start.12) | collective-permute-done | bytes 65568 | tf_op jit(solution)/shard_map/ppermute | solution.py:567
  30.7 1.4 %collective-permute-done.11.refs_2_ = f32[64,256]{1,0:T(8,128)S(1)} collective-permute-done((f32[64,256]{1,0:T(8,128)S(1)}, f32[64,256]{1,0:T(8,128)S(1)}, u32[]{:S(2)}, u32[]{:S(2)}) %collective-permute-start.11) | collective-permute-done | bytes 65568 | tf_op jit(solution)/shard_map/ppermute | solution.py:567
  32.2 0.5 collective-permute-done.10.refs_1_
  32.7 3.4 %shard_map.194 = (f32[64,256]{1,0:T(8,128)S(1)}, bf16[32,640]{1,0:T(8,128)(2,1)S(1)}, bf16[32,640]{1,0:T(8,128)(2,1)S(1)}, bf16[32,640]{1,0:T(8,128)(2,1)S(1)}, bf16[32,640]{1,0:T(8,128)(2,1)S(1)}) custom-call(f32[64,256]{1,0:T(8,128)S(1)} %shard_map.192.refs_0_, f32[64,256]{1,0:T(8,128)S(1)} %collective-permute-done.10.refs_1_, ...), custom_call_target="tpu_custom_call" | custom-call | flops 201326592 | bytes 3145728 | tf_op jit(solution)/shard_map/pallas_call | solution.py:754
  36.1 0.6 collective-permute-start.14
  36.7 1.5 %collective-permute-start.15 = (bf16[32,640]{1,0:T(8,128)(2,1)S(1)}, bf16[32,640]{1,0:T(8,128)(2,1)S(1)}, u32[]{:S(2)}, u32[]{:S(2)}) collective-permute-start(bf16[32,640]{1,0:T(8,128)(2,1)S(1)} %get-tuple-element.84), channel_id=1, source_target_pairs={{0,4},{2,6},{4,0},{6,2},{8,12},{10,14},{12,8},{14,10},{16,20},{18,... | collective-permute-start | bytes 122888 | tf_op jit(solution)/shard_map/ppermute | solution.py:567
  38.2 1.4 %collective-permute-start.16 = (bf16[32,640]{1,0:T(8,128)(2,1)S(1)}, bf16[32,640]{1,0:T(8,128)(2,1)S(1)}, u32[]{:S(2)}, u32[]{:S(2)}) collective-permute-start(bf16[32,640]{1,0:T(8,128)(2,1)S(1)} %get-tuple-element.85), channel_id=1, source_target_pairs={{0,6},{2,4},{4,2},{6,0},{8,14},{10,12},{12,10},{14,8},{16,22},{18,... | collective-permute-start | bytes 122888 | tf_op jit(solution)/shard_map/ppermute | solution.py:567
  39.6 1.7 %shard_map.195 = (bf16[288,512]{1,0:T(8,128)(2,1)}, f32[8,128]{1,0:T(8,128)S(1)}) custom-call(bf16[288,1536]{1,0:T(8,128)(2,1)S(1)} %get-tuple-element.67.packed, bf16[256,1536]{1,0:T(8,128)(2,1)S(1)} %get-tuple-element.63.refs_9_.refs_4_.refs_0_, bf16[256,1536]{1,0:T(8,128)(2,1)S(1)} %collective-permute-done.refs_13_.refs_5_.refs_1_, ...), custom_call_target="tpu_custom_call" | custom-call | flops 452984832 | bytes 4194304 | tf_op jit(solution)/shard_map/pallas_call | solution.py:764
  41.3 1.7 %collective-permute-done.16.refs_3_ = bf16[32,640]{1,0:T(8,128)(2,1)S(1)} collective-permute-done((bf16[32,640]{1,0:T(8,128)(2,1)S(1)}, bf16[32,640]{1,0:T(8,128)(2,1)S(1)}, u32[]{:S(2)}, u32[]{:S(2)}) %collective-permute-start.16) | collective-permute-done | bytes 40992 | tf_op jit(solution)/shard_map/ppermute | solution.py:567
  43.1 2.8 %collective-permute-start.19 = (bf16[32,640]{1,0:T(8,128)(2,1)S(1)}, bf16[32,640]{1,0:T(8,128)(2,1)S(1)}, u32[]{:S(2)}, u32[]{:S(2)}) collective-permute-start(bf16[32,640]{1,0:T(8,128)(2,1)S(1)} %shard_map.196.refs_0_), channel_id=1, source_target_pairs={{0,24},{2,26},{4,28},{6,30},{8,16},{10,18},{12,20},{14,22},{16,8},... | collective-permute-start | bytes 122888 | tf_op jit(solution)/shard_map/ppermute | solution.py:567
  45.9 1.6 %collective-permute-start.17 = (bf16[32,640]{1,0:T(8,128)(2,1)S(1)}, bf16[32,640]{1,0:T(8,128)(2,1)S(1)}, u32[]{:S(2)}, u32[]{:S(2)}) collective-permute-start(bf16[32,640]{1,0:T(8,128)(2,1)S(1)} %shard_map.196.refs_0_), channel_id=1, source_target_pairs={{0,8},{2,10},{4,12},{6,14},{8,0},{10,2},{12,4},{14,6},{16,24},{18,... | collective-permute-start | bytes 122888 | tf_op jit(solution)/shard_map/ppermute | solution.py:567
  47.6 1.4 %collective-permute-done.19.refs_3_ = bf16[32,640]{1,0:T(8,128)(2,1)S(1)} collective-permute-done((bf16[32,640]{1,0:T(8,128)(2,1)S(1)}, bf16[32,640]{1,0:T(8,128)(2,1)S(1)}, u32[]{:S(2)}, u32[]{:S(2)}) %collective-permute-start.19) | collective-permute-done | bytes 40992 | tf_op jit(solution)/shard_map/ppermute | solution.py:567
  49.0 1.9 %collective-permute-done.18.refs_2_ = bf16[32,640]{1,0:T(8,128)(2,1)S(1)} collective-permute-done((bf16[32,640]{1,0:T(8,128)(2,1)S(1)}, bf16[32,640]{1,0:T(8,128)(2,1)S(1)}, u32[]{:S(2)}, u32[]{:S(2)}) %collective-permute-start.18) | collective-permute-done | bytes 40992 | tf_op jit(solution)/shard_map/ppermute | solution.py:567
  50.9 1.5 %collective-permute-start.22 = (bf16[32,640]{1,0:T(8,128)(2,1)S(1)}, bf16[32,640]{1,0:T(8,128)(2,1)S(1)}, u32[]{:S(2)}, u32[]{:S(2)}) collective-permute-start(bf16[32,640]{1,0:T(8,128)(2,1)S(1)} %shard_map.197.refs_0_), channel_id=1, source_target_pairs={{0,6},{2,4},{4,2},{6,0},{8,14},{10,12},{12,10},{14,8},{16,22},{18,... | collective-permute-start | bytes 122888 | tf_op jit(solution)/shard_map/ppermute | solution.py:567
  52.4 1.5 %collective-permute-start.21 = (bf16[32,640]{1,0:T(8,128)(2,1)S(1)}, bf16[32,640]{1,0:T(8,128)(2,1)S(1)}, u32[]{:S(2)}, u32[]{:S(2)}) collective-permute-start(bf16[32,640]{1,0:T(8,128)(2,1)S(1)} %shard_map.197.refs_0_), channel_id=1, source_target_pairs={{0,4},{2,6},{4,0},{6,2},{8,12},{10,14},{12,8},{14,10},{16,20},{18,... | collective-permute-start | bytes 122888 | tf_op jit(solution)/shard_map/ppermute | solution.py:567
  53.9 0.5 collective-permute-start.20
  54.4 1.4 %collective-permute-done.22.refs_1_.refs_3_ = bf16[32,640]{1,0:T(8,128)(2,1)S(1)} collective-permute-done((bf16[32,640]{1,0:T(8,128)(2,1)S(1)}, bf16[32,640]{1,0:T(8,128)(2,1)S(1)}, u32[]{:S(2)}, u32[]{:S(2)}) %collective-permute-start.22) | collective-permute-done | bytes 40992 | tf_op jit(solution)/shard_map/ppermute | solution.py:567
  55.8 1.6 %shard_map.198 = (f32[256,1536]{1,0:T(8,128)}, f32[256,512]{1,0:T(8,128)}, f32[256,1536]{1,0:T(8,128)}, f32[256,512]{1,0:T(8,128)}) custom-call(bf16[32,640]{1,0:T(8,128)(2,1)S(1)} %shard_map.197.refs_0_, bf16[32,640]{1,0:T(8,128)(2,1)S(1)} %collective-permute-done.22.refs_1_.refs_3_, f32[64,256]{1,0:T(8,128)S(1)} %get-tuple-element.80.refs_5_.refs_2_.refs_4_, ...), custom_call_target="tpu_custom_call" | custom-call | flops 100663296 | bytes 1048576 | tf_op jit(solution)/shard_map/pallas_call | solution.py:814
  57.9 1.8 %shard_map.199 = (f32[256,1536]{1,0:T(8,128)}, f32[256,512]{1,0:T(8,128)}, f32[256,1536]{1,0:T(8,128)}, f32[256,512]{1,0:T(8,128)}, f32[32,1536]{1,0:T(8,128)}, ...) custom-call(bf16[32,640]{1,0:T(8,128)(2,1)S(1)} %shard_map.197.refs_, ...), custom_call_target="tpu_custom_call", output_to_operand_aliasing={{0}: (6, {}), {1}: (7, {}), {2}: (8, {}), {3}: (9, {})} | custom-call | flops 100663296 | bytes 1048576 | tf_op jit(solution)/shard_map/pallas_call | solution.py:823
  (27 shorter events, 1.9 us)
Async XLA Ops:
  0.6 3.7 %collective-permute-start = (bf16[256,1536]{1,0:T(8,128)(2,1)}, bf16[256,1536]{1,0:T(8,128)(2,1)S(1)}, u32[]{:S(2)}, u32[]{:S(2)}) collective-permute-start(bf16[256,1536]{1,0:T(8,128)(2,1)} %refs_4_.1), channel_id=1, source_target_pairs={{0,1},{1,0},{2,3},{3,2},{4,5},{5,4},{6,7},{7,6},{8,9},{9,8},{10,11... | collective-permute-start | bytes 2359304 | tf_op jit(solution)/shard_map/ppermute | solution.py:567
  1.2 3.2 %collective-permute-start.1 = (bf16[256,512]{1,0:T(8,128)(2,1)}, bf16[256,512]{1,0:T(8,128)(2,1)S(1)}, u32[]{:S(2)}, u32[]{:S(2)}) collective-permute-start(bf16[256,512]{1,0:T(8,128)(2,1)} %refs_7_.1), channel_id=1, source_target_pairs={{0,1},{1,0},{2,3},{3,2},{4,5},{5,4},{6,7},{7,6},{8,9},{9,8},{10,11... | collective-permute-start | bytes 786440 | tf_op jit(solution)/shard_map/ppermute | solution.py:567
  1.2 3.1 %collective-permute-start.2 = (f32[32,1536]{1,0:T(8,128)}, f32[32,1536]{1,0:T(8,128)S(1)}, u32[]{:S(2)}, u32[]{:S(2)}) collective-permute-start(f32[32,1536]{1,0:T(8,128)} %bitcast.27), channel_id=1, source_target_pairs={{0,1},{1,0},{2,3},{3,2},{4,5},{5,4},{6,7},{7,6},{8,9},{9,8},{10,11... | collective-permute-start | bytes 589832 | tf_op jit(solution)/shard_map/ppermute | solution.py:567
  1.7 2.7 %collective-permute-start.3 = (f32[32,512]{1,0:T(8,128)}, f32[32,512]{1,0:T(8,128)S(1)}, u32[]{:S(2)}, u32[]{:S(2)}) collective-permute-start(f32[32,512]{1,0:T(8,128)} %bitcast.29), channel_id=1, source_target_pairs={{0,1},{1,0},{2,3},{3,2},{4,5},{5,4},{6,7},{7,6},{8,9},{9,8},{10,11... | collective-permute-start | bytes 196616 | tf_op jit(solution)/shard_map/ppermute | solution.py:567
  12.5 1.4 %collective-permute-start.4 = (f32[64,256]{1,0:T(8,128)S(1)}, f32[64,256]{1,0:T(8,128)S(1)}, u32[]{:S(2)}, u32[]{:S(2)}) collective-permute-start(f32[64,256]{1,0:T(8,128)S(1)} %get-tuple-element.73), channel_id=1, source_target_pairs={{0,1},{1,0},{2,3},{3,2},{4,5},{5,4},{6,7},{7,6},{8,9},{9,8},{10,11... | collective-permute-start | bytes 196616 | tf_op jit(solution)/shard_map/ppermute | solution.py:567
  13.9 15.0 %collective-permute-start.13 = (bf16[256,2048]{1,0:T(8,128)(2,1)S(1)}, bf16[256,2048]{1,0:T(8,128)(2,1)S(1)}, u32[]{:S(2)}, u32[]{:S(2)}) collective-permute-start(bf16[256,2048]{1,0:T(8,128)(2,1)S(1)} %get-tuple-element.79.refs_3_), channel_id=1, source_target_pairs={{0,1},{1,0},{2,3},{3,2},{4,5},{5,4},{6,7},{7,6},{8,9},{9,8},{10,11... | collective-permute-start | bytes 3145736 | tf_op jit(solution)/shard_map/ppermute | solution.py:567
  14.4 5.7 %collective-permute-start.8 = (f32[8,144,144]{2,1,0:T(8,128)S(1)}, f32[8,144,144]{2,1,0:T(8,128)S(1)}, u32[]{:S(2)}, u32[]{:S(2)}) collective-permute-start(f32[8,144,144]{2,1,0:T(8,128)S(1)} %get-tuple-element.77.refs_0_), channel_id=1, source_target_pairs={{0,1},{1,0},{2,3},{3,2},{4,5},{5,4},{6,7},{7,6},{8,9},{9,8},{10,11... | collective-permute-start | bytes 1990664 | tf_op jit(solution)/shard_map/ppermute | solution.py:567
  14.5 8.6 %collective-permute-start.7 = (f32[64,256]{1,0:T(8,128)S(1)}, f32[64,256]{1,0:T(8,128)S(1)}, u32[]{:S(2)}, u32[]{:S(2)}) collective-permute-start(f32[64,256]{1,0:T(8,128)S(1)} %get-tuple-element.76.refs_0_), channel_id=1, source_target_pairs={{0,24},{2,26},{4,28},{6,30},{8,16},{10,18},{12,20},{14,22},{16,8},... | collective-permute-start | bytes 196616 | tf_op jit(solution)/shard_map/ppermute | solution.py:567
  19.5 5.9 %collective-permute-start.6 = (f32[64,256]{1,0:T(8,128)S(1)}, f32[64,256]{1,0:T(8,128)S(1)}, u32[]{:S(2)}, u32[]{:S(2)}) collective-permute-start(f32[64,256]{1,0:T(8,128)S(1)} %get-tuple-element.76.refs_0_), channel_id=1, source_target_pairs={{0,16},{2,18},{4,20},{6,22},{8,24},{10,26},{12,28},{14,30},{16,0},... | collective-permute-start | bytes 196616 | tf_op jit(solution)/shard_map/ppermute | solution.py:567
  19.5 5.9 %collective-permute-start.5 = (f32[64,256]{1,0:T(8,128)S(1)}, f32[64,256]{1,0:T(8,128)S(1)}, u32[]{:S(2)}, u32[]{:S(2)}) collective-permute-start(f32[64,256]{1,0:T(8,128)S(1)} %get-tuple-element.76.refs_0_), channel_id=1, source_target_pairs={{0,8},{2,10},{4,12},{6,14},{8,0},{10,2},{12,4},{14,6},{16,24},{18,... | collective-permute-start | bytes 196616 | tf_op jit(solution)/shard_map/ppermute | solution.py:567
  23.0 2.3 %collective-permute-start.9 = (f32[8,1024]{1,0:T(8,128)S(1)}, f32[8,1024]{1,0:T(8,128)S(1)}, u32[]{:S(2)}, u32[]{:S(2)}) collective-permute-start(f32[8,1024]{1,0:T(8,128)S(1)} %shard_map.191.refs_4_), channel_id=1, source_target_pairs={{0,1},{1,0},{2,3},{3,2},{4,5},{5,4},{6,7},{7,6},{8,9},{9,8},{10,11... | collective-permute-start | bytes 98312 | tf_op jit(solution)/shard_map/ppermute | solution.py:567
  25.4 5.3 %collective-permute-start.12 = (f32[64,256]{1,0:T(8,128)S(1)}, f32[64,256]{1,0:T(8,128)S(1)}, u32[]{:S(2)}, u32[]{:S(2)}) collective-permute-start(f32[64,256]{1,0:T(8,128)S(1)} %shard_map.192.refs_0_), channel_id=1, source_target_pairs={{0,6},{2,4},{4,2},{6,0},{8,14},{10,12},{12,10},{14,8},{16,22},{18,... | collective-permute-start | bytes 196616 | tf_op jit(solution)/shard_map/ppermute | solution.py:567
  27.9 4.3 %collective-permute-start.11 = (f32[64,256]{1,0:T(8,128)S(1)}, f32[64,256]{1,0:T(8,128)S(1)}, u32[]{:S(2)}, u32[]{:S(2)}) collective-permute-start(f32[64,256]{1,0:T(8,128)S(1)} %shard_map.192.refs_0_), channel_id=1, source_target_pairs={{0,4},{2,6},{4,0},{6,2},{8,12},{10,14},{12,8},{14,10},{16,20},{18,... | collective-permute-start | bytes 196616 | tf_op jit(solution)/shard_map/ppermute | solution.py:567
  28.4 4.3 %collective-permute-start.10 = (f32[64,256]{1,0:T(8,128)S(1)}, f32[64,256]{1,0:T(8,128)S(1)}, u32[]{:S(2)}, u32[]{:S(2)}) collective-permute-start(f32[64,256]{1,0:T(8,128)S(1)} %shard_map.192.refs_0_), channel_id=1, source_target_pairs={{0,2},{2,0},{4,6},{6,4},{8,10},{10,8},{12,14},{14,12},{16,18},{18,... | collective-permute-start | bytes 196616 | tf_op jit(solution)/shard_map/ppermute | solution.py:567
  36.1 5.2 %collective-permute-start.14 = (bf16[32,640]{1,0:T(8,128)(2,1)S(1)}, bf16[32,640]{1,0:T(8,128)(2,1)S(1)}, u32[]{:S(2)}, u32[]{:S(2)}) collective-permute-start(bf16[32,640]{1,0:T(8,128)(2,1)S(1)} %get-tuple-element.83), channel_id=1, source_target_pairs={{0,2},{2,0},{4,6},{6,4},{8,10},{10,8},{12,14},{14,12},{16,18},{18,... | collective-permute-start | bytes 122888 | tf_op jit(solution)/shard_map/ppermute | solution.py:567
  36.7 4.7 %collective-permute-start.15 = (bf16[32,640]{1,0:T(8,128)(2,1)S(1)}, bf16[32,640]{1,0:T(8,128)(2,1)S(1)}, u32[]{:S(2)}, u32[]{:S(2)}) collective-permute-start(bf16[32,640]{1,0:T(8,128)(2,1)S(1)} %get-tuple-element.84), channel_id=1, source_target_pairs={{0,4},{2,6},{4,0},{6,2},{8,12},{10,14},{12,8},{14,10},{16,20},{18,... | collective-permute-start | bytes 122888 | tf_op jit(solution)/shard_map/ppermute | solution.py:567
  38.2 4.9 %collective-permute-start.16 = (bf16[32,640]{1,0:T(8,128)(2,1)S(1)}, bf16[32,640]{1,0:T(8,128)(2,1)S(1)}, u32[]{:S(2)}, u32[]{:S(2)}) collective-permute-start(bf16[32,640]{1,0:T(8,128)(2,1)S(1)} %get-tuple-element.85), channel_id=1, source_target_pairs={{0,6},{2,4},{4,2},{6,0},{8,14},{10,12},{12,10},{14,8},{16,22},{18,... | collective-permute-start | bytes 122888 | tf_op jit(solution)/shard_map/ppermute | solution.py:567
  43.1 5.9 %collective-permute-start.19 = (bf16[32,640]{1,0:T(8,128)(2,1)S(1)}, bf16[32,640]{1,0:T(8,128)(2,1)S(1)}, u32[]{:S(2)}, u32[]{:S(2)}) collective-permute-start(bf16[32,640]{1,0:T(8,128)(2,1)S(1)} %shard_map.196.refs_0_), channel_id=1, source_target_pairs={{0,24},{2,26},{4,28},{6,30},{8,16},{10,18},{12,20},{14,22},{16,8},... | collective-permute-start | bytes 122888 | tf_op jit(solution)/shard_map/ppermute | solution.py:567
  45.9 4.9 %collective-permute-start.18 = (bf16[32,640]{1,0:T(8,128)(2,1)S(1)}, bf16[32,640]{1,0:T(8,128)(2,1)S(1)}, u32[]{:S(2)}, u32[]{:S(2)}) collective-permute-start(bf16[32,640]{1,0:T(8,128)(2,1)S(1)} %shard_map.196.refs_0_), channel_id=1, source_target_pairs={{0,16},{2,18},{4,20},{6,22},{8,24},{10,26},{12,28},{14,30},{16,0},... | collective-permute-start | bytes 122888 | tf_op jit(solution)/shard_map/ppermute | solution.py:567
  45.9 4.9 %collective-permute-start.17 = (bf16[32,640]{1,0:T(8,128)(2,1)S(1)}, bf16[32,640]{1,0:T(8,128)(2,1)S(1)}, u32[]{:S(2)}, u32[]{:S(2)}) collective-permute-start(bf16[32,640]{1,0:T(8,128)(2,1)S(1)} %shard_map.196.refs_0_), channel_id=1, source_target_pairs={{0,8},{2,10},{4,12},{6,14},{8,0},{10,2},{12,4},{14,6},{16,24},{18,... | collective-permute-start | bytes 122888 | tf_op jit(solution)/shard_map/ppermute | solution.py:567
  50.9 5.0 %collective-permute-start.22 = (bf16[32,640]{1,0:T(8,128)(2,1)S(1)}, bf16[32,640]{1,0:T(8,128)(2,1)S(1)}, u32[]{:S(2)}, u32[]{:S(2)}) collective-permute-start(bf16[32,640]{1,0:T(8,128)(2,1)S(1)} %shard_map.197.refs_0_), channel_id=1, source_target_pairs={{0,6},{2,4},{4,2},{6,0},{8,14},{10,12},{12,10},{14,8},{16,22},{18,... | collective-permute-start | bytes 122888 | tf_op jit(solution)/shard_map/ppermute | solution.py:567
  52.4 5.1 %collective-permute-start.21 = (bf16[32,640]{1,0:T(8,128)(2,1)S(1)}, bf16[32,640]{1,0:T(8,128)(2,1)S(1)}, u32[]{:S(2)}, u32[]{:S(2)}) collective-permute-start(bf16[32,640]{1,0:T(8,128)(2,1)S(1)} %shard_map.197.refs_0_), channel_id=1, source_target_pairs={{0,4},{2,6},{4,0},{6,2},{8,12},{10,14},{12,8},{14,10},{16,20},{18,... | collective-permute-start | bytes 122888 | tf_op jit(solution)/shard_map/ppermute | solution.py:567
  53.9 4.0 %collective-permute-start.20 = (bf16[32,640]{1,0:T(8,128)(2,1)S(1)}, bf16[32,640]{1,0:T(8,128)(2,1)S(1)}, u32[]{:S(2)}, u32[]{:S(2)}) collective-permute-start(bf16[32,640]{1,0:T(8,128)(2,1)S(1)} %shard_map.197.refs_0_), channel_id=1, source_target_pairs={{0,2},{2,0},{4,6},{6,4},{8,10},{10,8},{12,14},{14,12},{16,18},{18,... | collective-permute-start | bytes 122888 | tf_op jit(solution)/shard_map/ppermute | solution.py:567

commit v5 on v3

--- a/solution.py
+++ b/solution.py
@@ -12,6 +12,7 @@
 MASKED = -1e30
 LANES = 128
 SUBLANES = 8
+TILE_ROWS = 16
 READY_HEADS = 2
 F32 = jnp.float32
 BF16 = jnp.bfloat16
@@ -110,8 +111,8 @@
 
 def prepare_kernel(blocks, ready, *refs):
     sources, rest = refs[:12], refs[12:]
-    normed, part, bias, index_t, table_pad, bucket, *kept = rest[:16]
-    table, sems = rest[16:]
+    normed, normed_t, part, bias, index_t, table_pad, bucket, *kept = rest[:17]
+    table, sems = rest[17:]
     copies = fetch(list(zip(sources, [bucket, table] + kept)), sems)
     tokens, gain, w_own = kept[:3]
     me = lax.axis_index("mp")
@@ -128,15 +129,16 @@
         copy.wait()
     x_hat, _ = norm_forward(tokens[...])
     normed[...] = (x_hat * gain[...]).astype(BF16)
+    normed_t[...] = normed[...].T
     part[...] = nn(normed[:, block_columns(me, 0, blocks, width)], w_own[...])
     for copy in copies[5:]:
         copy.wait()
 
 
 def attend_kernel(blocks, share, *refs):
-    normed, part, bias_ready, index_t, table_pad, bucket, cot, region = refs[:8]
-    own, arrived = refs[8:12], refs[12 : 8 + 4 * blocks]
-    rest = refs[8 + 4 * blocks :]
+    normed, normed_t, part, bias_ready, index_t, table_pad, bucket, cot, region = refs[:9]
+    own, arrived = refs[9:13], refs[13 : 9 + 4 * blocks]
+    rest = refs[9 + 4 * blocks :]
     terms, lefts, rest = rest[:blocks], rest[blocks : 2 * blocks], rest[2 * blocks :]
     score_sum, packed, proj, mixed_grad, mixed, bias = rest
     w_in, w_out, in_basis, out_basis = (
@@ -173,14 +175,14 @@
                 if window == 0:
                     gather_bias(bias, range(heads.start, heads.stop), table_pad, index_t, bucket)
                 pair_bias = bias[heads]
-            q = proj[rows, start : start + LANES]
+            q = proj[rows, start : start + LANES] * jnp.asarray(scale, BF16)
             k = proj[rows, features + start : features + start + LANES]
             v = proj[rows, 2 * features + start : 2 * features + start + LANES]
             g = mixed_grad[rows, start : start + LANES]
             pick = [lane // head_size == sub for sub in range(per_group)]
             k_split = jnp.concatenate([jnp.where(own, k, jnp.zeros_like(k)) for own in pick], 0)
             v_split = jnp.concatenate([jnp.where(own, v, jnp.zeros_like(v)) for own in pick], 0)
-            scores = nt(k_split, q).reshape(per_group, span, span) * scale + pair_bias
+            scores = nt(k_split, q).reshape(per_group, span, span) + pair_bias
             scores = jnp.where(allowed[None], scores, MASKED)
             top = jnp.max(scores, axis=1, keepdims=True)
             raised = jnp.exp(scores - top)
@@ -209,14 +211,12 @@
             q_grad = joined([tn(score_b[at], k) for at in range(per_group)])
             mixed[rows, start : start + LANES] = out.astype(BF16)
             packed[rows, start : start + LANES] = (q_grad * scale).astype(BF16)
-            packed[rows, features + start : features + start + LANES] = (k_grad * scale).astype(
-                BF16
-            )
+            packed[rows, features + start : features + start + LANES] = k_grad.astype(BF16)
             packed[rows, 2 * features + start : 2 * features + start + LANES] = v_grad.astype(BF16)
     wide = 3 * features
     for step in range(blocks):
         columns = block_columns(me, step, blocks, width)
-        terms[step][:, :wide] = tn(normed[:, columns], packed[...]).astype(BF16)
+        terms[step][:, :wide] = nn(normed_t[columns, :], packed[...]).astype(BF16)
         terms[step][:, wide:] = tn(mixed[:, columns], cot[...]).astype(BF16)
         rank = in_basis[step].shape[0]
         for basis, at, place in (
@@ -346,25 +346,31 @@
     refs[-1][...] = tree_sum([ref[...] for ref in refs[:parts]])
 
 
-def stats_pieces(pair):
-    pieces = []
-    for at in range(2):
-        tile = pair[:, at * LANES : (at + 1) * LANES]
-        coarse, fine = halves(tile)
-        pieces += [coarse.astype(F32), fine.astype(F32)]
-    return jnp.concatenate(pieces, axis=0).astype(BF16)
-
-
-def stats_pair(pieces):
-    rows = pieces.shape[0] // 4
+def store_tiles(piece, right, stats):
+    rows, columns = right.shape
+    place = 0
+    for column in range(0, columns, LANES):
+        for row in range(0, rows, TILE_ROWS):
+            piece[place] = right[row : row + TILE_ROWS, column : column + LANES].astype(BF16)
+            place += 1
+    piece[place] = jnp.concatenate([stats[:, :LANES], stats[:, LANES:]], axis=0).astype(BF16)
+
+
+def load_right(piece, rows):
+    per_column = rows // TILE_ROWS
+    tiles = [piece[at].astype(F32) for at in range(piece.shape[0] - 1)]
     return jnp.concatenate(
         [
-            pieces[2 * at * rows : (2 * at + 1) * rows]
-            + pieces[(2 * at + 1) * rows : (2 * at + 2) * rows]
-            for at in range(2)
+            jnp.concatenate(tiles[at : at + per_column], axis=0)
+            for at in range(0, len(tiles), per_column)
         ],
         axis=1,
     )
+
+
+def load_stats(piece):
+    tile = piece[piece.shape[0] - 1].astype(F32)
+    return jnp.concatenate([tile[: TILE_ROWS // 2], tile[TILE_ROWS // 2 :]], axis=1)
 
 
 def orthonormal(problems):
@@ -433,17 +439,14 @@
         block = jnp.bitwise_xor(digit, step)
         columns = pl.ds(pl.multiple_of(block * quarter, quarter), quarter)
         pair = stacked(jnp.where(block < len(pieces) - 1, finished[0], finished[1]))
-        piece[:, :quarter] = folded(nn(pair, merged[:, columns].astype(BF16))).astype(BF16)
         stat_columns = pl.ds(pl.multiple_of(block * 2 * LANES, 2 * LANES), 2 * LANES)
-        piece[:, quarter:] = stats_pieces(sums[:, stat_columns])
+        right = folded(nn(pair, merged[:, columns].astype(BF16)))
+        store_tiles(piece, right, sums[:, stat_columns])
 
 
 def reduce_kernel(*refs):
     pieces, total = refs[:-2], refs[-1]
-    quarter = total.shape[1] - LANES
-    summed = tree_sum([piece[...].astype(F32) for piece in pieces])
-    total[:, :quarter] = summed[:, :quarter].astype(BF16)
-    total[:, quarter:] = stats_pieces(stats_pair(summed[:, quarter:]))
+    total[...] = tree_sum([piece[...].astype(F32) for piece in pieces]).astype(BF16)
 
 
 def update_blocks(share, steps, pieces, ortho, merged, results, updates, errors, sems, small):
@@ -455,7 +458,7 @@
     for at, step in enumerate(steps):
         block = jnp.bitwise_xor(lax.axis_index("dp") % 4, step)
         columns = pl.ds(pl.multiple_of(block * quarter, quarter), quarter)
-        right = pieces[step][:, :quarter].astype(F32) * share
+        right = load_right(pieces[step], rank) * share
         own_coarse, own_fine = halves(
             jnp.where(block < count - 1, ortho[:rank, :], ortho[rank:, :])
         )
@@ -495,20 +498,21 @@
 def last_kernel(share, stat_share, steps, parts, *refs):
     pieces, (ortho, merged) = refs[:parts], refs[parts : parts + 2]
     results, small_results = refs[parts + 6 : parts + 10], refs[parts + 10 : parts + 14]
-    rights, *small = refs[parts + 14 : parts + 19]
-    small_sems, updates, errors, sems = refs[parts + 19 :]
+    rights, stats_of, *small = refs[parts + 14 : parts + 20]
+    small_sems, updates, errors, sems = refs[parts + 20 :]
     in_basis, out_basis, table, gain = small
-    quarter = rights.shape[2] - LANES
+    quarter = rights.shape[2]
     copies = []
 
     def small_outputs():
         for step, piece in enumerate(pieces):
-            rights[step] = piece[...].astype(F32)
+            rights[step] = load_right(piece, rights.shape[1]) * share
+            stats_of[step] = load_stats(piece) * stat_share
         tiles = []
         for block in range(parts):
-            here = rights[jnp.bitwise_xor(lax.axis_index("dp") % 4, block)]
-            right = here[:, :quarter] * share
-            tiles.append(stats_pair(here[:, quarter:]) * stat_share)
+            place = jnp.bitwise_xor(lax.axis_index("dp") % 4, block)
+            right = rights[place]
+            tiles.append(stats_of[place])
             if block < parts - 1:
                 in_basis[:, block * quarter : (block + 1) * quarter] = right
             else:
@@ -631,10 +635,11 @@
         in_error[0],
         out_error[0],
     )
-    normed, part, bias, index_t, table_pad, bucket, *kept = call(
+    normed, normed_t, part, bias, index_t, table_pad, bucket, *kept = call(
         functools.partial(prepare_kernel, blocks, READY_HEADS),
         (
             shape((row_count, features), BF16),
+            shape((features, row_count), BF16),
             shape((row_count, wide), F32),
             shape((READY_HEADS, span, span), F32),
             shape((span, span), jnp.int32),
@@ -646,7 +651,7 @@
         flops=2 * row_count * width * wide,
         moved=4 << 20,
         in_specs=[HBM] * 12,
-        out_specs=[VMEM] * 16,
+        out_specs=[VMEM] * 17,
     )(*in_hbm(*operands))
     token_rows, gain, w_in_own, cot_rows, region, *own, in_errors, out_errors = kept
     in_basis_t, out_basis_t = own[1:]
@@ -665,9 +670,9 @@
         ],
         flops=4 * row_count * features * both,
         moved=8 << 20,
-        in_specs=[VMEM] * (12 + len(arrived)),
+        in_specs=[VMEM] * (13 + len(arrived)),
         out_specs=[VMEM] * (2 * blocks + 2),
-    )(normed, part, bias, index_t, table_pad, bucket, cot_rows, region, w_in_own, *own, *arrived)
+    )(normed, normed_t, part, bias, index_t, table_pad, bucket, cot_rows, region, w_in_own, *own, *arrived)
     *outputs, score_sum, packed = outputs
     terms, lefts = outputs[:blocks], outputs[blocks:]
     scores_of = [score_sum]
@@ -738,7 +743,8 @@
     )(*term_parts, in_errors, out_errors)
 
     quarter = both // parts
-    piece = shape((rank, quarter + LANES), BF16)
+    tiles = quarter // LANES * (rank // TILE_ROWS) + 1
+    piece = shape((tiles, TILE_ROWS, LANES), BF16)
     ortho, *pieces = call(
         functools.partial(ortho_kernel, 1.0 / n_dp, len(lefts), len(stats)),
         (shape((2 * rank, row_block), F32),) + (piece,) * parts,
@@ -811,7 +817,12 @@
     in_update, out_update, in_new_error, out_new_error, in_right, out_right, table, gain = call(
         functools.partial(last_kernel, 1.0 / n_dp, 1.0 / (n_dp * n_mp), late, parts),
         big + small,
-        [pltpu.VMEM((parts, rank, quarter + LANES), F32)] + buffers(*small) + staging(late),
+        [
+            pltpu.VMEM((parts, rank, quarter), F32),
+            pltpu.VMEM((parts, head_count, 2 * LANES), F32),
+        ]
+        + buffers(*small)
+        + staging(late),
         flops=24 * row_block * quarter * rank,
         moved=1 << 20,
         in_specs=[VMEM] * (parts + 2) + [HBM] * 4,

time: 58.8 us -> 58.7 us (level)
  no operation moved by 1% of the time
where the time goes in v5:
time: 58.7 us; the launch traced here: 58.5 us
  starting transfers between devices  22.8 us (39%)
  Pallas kernels  22.5 us (38%)
  waiting for transfers between devices  12.3 us (21%)
  between operations  0.95 us (2%)
    ppermute x23, starting transfers between devices, exchange(): lax.ppermute(value, axis, [(at, at ^ distance) for at in range(count)])  22.8 us
    ppermute x23, waiting for transfers between devices, exchange(): lax.ppermute(value, axis, [(at, at ^ distance) for at in range(count)])  12.3 us
    pallas_call x1, Pallas kernels, shards(): call(functools.partial(attend_kernel, blocks, 1.0 / n_mp), (shape((width,...  7.04 us
    pallas_call x1, Pallas kernels, shards(): call(functools.partial(ortho_kernel, 1.0 / n_dp, len(lefts), len(stats)),...  3.44 us
    pallas_call x1, Pallas kernels, shards(): call(functools.partial(table_kernel, blocks), shape((head_count, padded +...  2.98 us
    pallas_call x1, Pallas kernels, shards(): call(functools.partial(prepare_kernel, blocks, READY_HEADS), (shape((row_...  2.58 us
    pallas_call x1, Pallas kernels, shards(): call(functools.partial(last_kernel, 1.0 / n_dp, 1.0 / (n_dp * n_mp), late...  1.76 us
    pallas_call x1, Pallas kernels, shards(): call(functools.partial(token_kernel, blocks), (shape((row_count, features...  1.7 us
  transfers between devices with their start and end apart: 23, of which 10 were waited for; matrix products, arithmetic and copies ran while one was open for 0% of the time, Pallas kernels for 17%

profile of v5, /device:TPU:0, one launch (start us, length us, event | category | flops | bytes accessed | tf_op | source)
XLA Modules:
  0.0 58.5 jit_solution(15197054083237763303)
XLA Ops:
  0.6 0.5 collective-permute-start
  1.8 2.6 %shard_map.187 = (bf16[288,512]{1,0:T(8,128)(2,1)S(1)}, bf16[512,288]{1,0:T(8,128)(2,1)S(1)}, f32[288,1536]{1,0:T(8,128)S(1)}, f32[2,144,144]{2,1,0:T(8,128)S(1)...) custom-call(s32[144,144]{1,0:T(8,128)} %refs_0_.1, ...), custom_call_target="tpu_custom_call" | custom-call | flops 226492416 | bytes 4194304 | tf_op jit(solution)/shard_map/pallas_call | solution.py:638
  4.4 7.0 %shard_map.188 = (bf16[256,2048]{1,0:T(8,128)(2,1)S(1)}, bf16[256,2048]{1,0:T(8,128)(2,1)S(1)}, f32[64,256]{1,0:T(8,128)S(1)}, f32[64,256]{1,0:T(8,128)S(1)}, f3...) custom-call(bf16[288,512]{1,0:T(8,128)(2,1)S(1)} %get-tuple-element.54.refs_0_, ...), custom_call_target="tpu_custom_call" | custom-call | flops 1207959552 | bytes 8388608 | tf_op jit(solution)/shard_map/pallas_call | solution.py:660
  11.4 0.5 collective-permute-start.4
  11.9 0.7 %shard_map.189.left_own = f32[64,256]{1,0:T(8,128)S(1)} custom-call(f32[64,256]{1,0:T(8,128)S(1)} %get-tuple-element.70.term_left, f32[256,1536]{1,0:T(8,128)S(1)} %get-tuple-element.71.in_error.refs_2_, f32[256,512]{1,0:T(8,128)S(1)} %get-tuple-element.72.out_error.refs_3_, f32[32,1536]{1,0:T(8,128)S(1)} %get-tuple-element.65.refs_11_.in_basis, ...), custom_call_target="tpu_custom_call" | custom-call | flops 134217728 | bytes 3145728 | tf_op jit(solution)/shard_map/pallas_call | solution.py:692
  13.4 4.9 %collective-permute-start.7 = (f32[64,256]{1,0:T(8,128)S(1)}, f32[64,256]{1,0:T(8,128)S(1)}, u32[]{:S(2)}, u32[]{:S(2)}) collective-permute-start(f32[64,256]{1,0:T(8,128)S(1)} %get-tuple-element.76.refs_0_), channel_id=1, source_target_pairs={{0,24},{2,26},{4,28},{6,30},{8,16},{10,18},{12,20},{14,22},{16,8},... | collective-permute-start | bytes 196616 | tf_op jit(solution)/shard_map/ppermute | solution.py:560
  18.3 0.6 collective-permute-start.5
  18.9 3.0 %shard_map.191.refs_4_ = f32[8,1024]{1,0:T(8,128)S(1)} custom-call(f32[8,144,144]{2,1,0:T(8,128)S(1)} %get-tuple-element.77.refs_0_, f32[8,144,144]{2,1,0:T(8,128)S(1)} %collective-permute-done.8.refs_1_, bf16[256,2048]{1,0:T(8,128)(2,1)S(1)} %get-tuple-element.78.refs_2_.refs_0_, bf16[256,2048]{1,0:T(8,128)(2,1)S(1)} %get-tuple-element.79.refs_3_, ...), custom_call_target="tpu_custom_call" | custom-call | flops 452984832 | bytes 4194304 | tf_op jit(solution)/shard_map/pallas_call | solution.py:712
  22.0 2.2 %collective-permute-done.6.refs_2_ = f32[64,256]{1,0:T(8,128)S(1)} collective-permute-done((f32[64,256]{1,0:T(8,128)S(1)}, f32[64,256]{1,0:T(8,128)S(1)}, u32[]{:S(2)}, u32[]{:S(2)}) %collective-permute-start.6) | collective-permute-done | bytes 65568 | tf_op jit(solution)/shard_map/ppermute | solution.py:560
  24.2 2.5 %collective-permute-start.12 = (f32[64,256]{1,0:T(8,128)S(1)}, f32[64,256]{1,0:T(8,128)S(1)}, u32[]{:S(2)}, u32[]{:S(2)}) collective-permute-start(f32[64,256]{1,0:T(8,128)S(1)} %shard_map.192.refs_0_), channel_id=1, source_target_pairs={{0,6},{2,4},{4,2},{6,0},{8,14},{10,12},{12,10},{14,8},{16,22},{18,... | collective-permute-start | bytes 196616 | tf_op jit(solution)/shard_map/ppermute | solution.py:560
  26.7 0.5 collective-permute-start.11
  27.2 0.5 collective-permute-start.10
  27.8 0.6 shard_map.193.refs_6_.refs_3_.refs_5_
  28.3 1.2 %collective-permute-done.12.refs_3_ = f32[64,256]{1,0:T(8,128)S(1)} collective-permute-done((f32[64,256]{1,0:T(8,128)S(1)}, f32[64,256]{1,0:T(8,128)S(1)}, u32[]{:S(2)}, u32[]{:S(2)}) %collective-permute-start.12) | collective-permute-done | bytes 65568 | tf_op jit(solution)/shard_map/ppermute | solution.py:560
  29.6 1.4 %collective-permute-done.11.refs_2_ = f32[64,256]{1,0:T(8,128)S(1)} collective-permute-done((f32[64,256]{1,0:T(8,128)S(1)}, f32[64,256]{1,0:T(8,128)S(1)}, u32[]{:S(2)}, u32[]{:S(2)}) %collective-permute-start.11) | collective-permute-done | bytes 65568 | tf_op jit(solution)/shard_map/ppermute | solution.py:560
  31.0 0.5 collective-permute-done.10.refs_1_
  31.5 3.4 %shard_map.194 = (f32[64,256]{1,0:T(8,128)S(1)}, bf16[9,16,128]{2,1,0:T(8,128)(2,1)S(1)}, bf16[9,16,128]{2,1,0:T(8,128)(2,1)S(1)}, bf16[9,16,128]{2,1,0:T(8,128)(2,1)S(1)}, bf16[9,16,128]{2,1,0:T(8,128)(2,1)S(1)}) custom-call(f32[64,256]{1,0:T(8,128)S(1)} %shard_map.192.refs_0_, f32[64,256]{1,0:T(8,128)S(1)} %collective-permute-done.10.refs_1_, ...), custom_call_target="tpu_custom_call" | custom-call | flops 201326592 | bytes 3145728 | tf_op jit(solution)/shard_map/pallas_call | solution.py:748
  34.9 0.6 collective-permute-start.14
  35.5 1.5 %collective-permute-start.15 = (bf16[9,16,128]{2,1,0:T(8,128)(2,1)S(1)}, bf16[9,16,128]{2,1,0:T(8,128)(2,1)S(1)}, u32[]{:S(2)}, u32[]{:S(2)}) collective-permute-start(bf16[9,16,128]{2,1,0:T(8,128)(2,1)S(1)} %get-tuple-element.84), channel_id=1, source_target_pairs={{0,4},{2,6},{4,0},{6,2},{8,12},{10,14},{12,8},{14,10},{16,20},{18,... | collective-permute-start | bytes 110600 | tf_op jit(solution)/shard_map/ppermute | solution.py:560
  37.0 1.4 %collective-permute-start.16 = (bf16[9,16,128]{2,1,0:T(8,128)(2,1)S(1)}, bf16[9,16,128]{2,1,0:T(8,128)(2,1)S(1)}, u32[]{:S(2)}, u32[]{:S(2)}) collective-permute-start(bf16[9,16,128]{2,1,0:T(8,128)(2,1)S(1)} %get-tuple-element.85), channel_id=1, source_target_pairs={{0,6},{2,4},{4,2},{6,0},{8,14},{10,12},{12,10},{14,8},{16,22},{18,... | collective-permute-start | bytes 110600 | tf_op jit(solution)/shard_map/ppermute | solution.py:560
  38.5 1.7 %shard_map.195 = (bf16[288,512]{1,0:T(8,128)(2,1)}, f32[8,128]{1,0:T(8,128)S(1)}) custom-call(bf16[288,1536]{1,0:T(8,128)(2,1)S(1)} %get-tuple-element.67.packed, bf16[256,1536]{1,0:T(8,128)(2,1)S(1)} %get-tuple-element.63.refs_9_.refs_4_.refs_0_, bf16[256,1536]{1,0:T(8,128)(2,1)S(1)} %collective-permute-done.refs_13_.refs_5_.refs_1_, ...), custom_call_target="tpu_custom_call" | custom-call | flops 452984832 | bytes 4194304 | tf_op jit(solution)/shard_map/pallas_call | solution.py:758
  40.2 1.7 %collective-permute-done.16.refs_3_ = bf16[9,16,128]{2,1,0:T(8,128)(2,1)S(1)} collective-permute-done((bf16[9,16,128]{2,1,0:T(8,128)(2,1)S(1)}, bf16[9,16,128]{2,1,0:T(8,128)(2,1)S(1)}, u32[]{:S(2)}, u32[]{:S(2)}) %collective-permute-start.16) | collective-permute-done | bytes 36896 | tf_op jit(solution)/shard_map/ppermute | solution.py:560
  41.9 2.8 %collective-permute-start.19 = (bf16[9,16,128]{2,1,0:T(8,128)(2,1)S(1)}, bf16[9,16,128]{2,1,0:T(8,128)(2,1)S(1)}, u32[]{:S(2)}, u32[]{:S(2)}) collective-permute-start(bf16[9,16,128]{2,1,0:T(8,128)(2,1)S(1)} %shard_map.196.refs_0_), channel_id=1, source_target_pairs={{0,24},{2,26},{4,28},{6,30},{8,16},{10,18},{12,20},{14,22},{16,8},... | collective-permute-start | bytes 110600 | tf_op jit(solution)/shard_map/ppermute | solution.py:560
  44.7 1.6 %collective-permute-start.17 = (bf16[9,16,128]{2,1,0:T(8,128)(2,1)S(1)}, bf16[9,16,128]{2,1,0:T(8,128)(2,1)S(1)}, u32[]{:S(2)}, u32[]{:S(2)}) collective-permute-start(bf16[9,16,128]{2,1,0:T(8,128)(2,1)S(1)} %shard_map.196.refs_0_), channel_id=1, source_target_pairs={{0,8},{2,10},{4,12},{6,14},{8,0},{10,2},{12,4},{14,6},{16,24},{18,... | collective-permute-start | bytes 110600 | tf_op jit(solution)/shard_map/ppermute | solution.py:560
  46.4 1.4 %collective-permute-done.19.refs_3_ = bf16[9,16,128]{2,1,0:T(8,128)(2,1)S(1)} collective-permute-done((bf16[9,16,128]{2,1,0:T(8,128)(2,1)S(1)}, bf16[9,16,128]{2,1,0:T(8,128)(2,1)S(1)}, u32[]{:S(2)}, u32[]{:S(2)}) %collective-permute-start.19) | collective-permute-done | bytes 36896 | tf_op jit(solution)/shard_map/ppermute | solution.py:560
  47.7 1.9 %collective-permute-done.18.refs_2_ = bf16[9,16,128]{2,1,0:T(8,128)(2,1)S(1)} collective-permute-done((bf16[9,16,128]{2,1,0:T(8,128)(2,1)S(1)}, bf16[9,16,128]{2,1,0:T(8,128)(2,1)S(1)}, u32[]{:S(2)}, u32[]{:S(2)}) %collective-permute-start.18) | collective-permute-done | bytes 36896 | tf_op jit(solution)/shard_map/ppermute | solution.py:560
  49.6 1.5 %collective-permute-start.22 = (bf16[9,16,128]{2,1,0:T(8,128)(2,1)S(1)}, bf16[9,16,128]{2,1,0:T(8,128)(2,1)S(1)}, u32[]{:S(2)}, u32[]{:S(2)}) collective-permute-start(bf16[9,16,128]{2,1,0:T(8,128)(2,1)S(1)} %shard_map.197.refs_0_), channel_id=1, source_target_pairs={{0,6},{2,4},{4,2},{6,0},{8,14},{10,12},{12,10},{14,8},{16,22},{18,... | collective-permute-start | bytes 110600 | tf_op jit(solution)/shard_map/ppermute | solution.py:560
  51.1 1.5 %collective-permute-start.21 = (bf16[9,16,128]{2,1,0:T(8,128)(2,1)S(1)}, bf16[9,16,128]{2,1,0:T(8,128)(2,1)S(1)}, u32[]{:S(2)}, u32[]{:S(2)}) collective-permute-start(bf16[9,16,128]{2,1,0:T(8,128)(2,1)S(1)} %shard_map.197.refs_0_), channel_id=1, source_target_pairs={{0,4},{2,6},{4,0},{6,2},{8,12},{10,14},{12,8},{14,10},{16,20},{18,... | collective-permute-start | bytes 110600 | tf_op jit(solution)/shard_map/ppermute | solution.py:560
  52.6 0.6 collective-permute-start.20
  53.2 1.4 %collective-permute-done.22.refs_1_.refs_3_ = bf16[9,16,128]{2,1,0:T(8,128)(2,1)S(1)} collective-permute-done((bf16[9,16,128]{2,1,0:T(8,128)(2,1)S(1)}, bf16[9,16,128]{2,1,0:T(8,128)(2,1)S(1)}, u32[]{:S(2)}, u32[]{:S(2)}) %collective-permute-start.22) | collective-permute-done | bytes 36896 | tf_op jit(solution)/shard_map/ppermute | solution.py:560
  54.6 1.6 %shard_map.198 = (f32[256,1536]{1,0:T(8,128)}, f32[256,512]{1,0:T(8,128)}, f32[256,1536]{1,0:T(8,128)}, f32[256,512]{1,0:T(8,128)}) custom-call(bf16[9,16,128]{2,1,0:T(8,128)(2,1)S(1)} %shard_map.197.refs_0_, bf16[9,16,128]{2,1,0:T(8,128)(2,1)S(1)} %collective-permute-done.22.refs_1_.refs_3_, f32[64,256]{1,0:T(8,128)S(1)} %get-tuple-element.80.refs_5_.refs_2_.refs_4_, ...), custom_call_target="tpu_custom_call" | custom-call | flops 100663296 | bytes 1048576 | tf_op jit(solution)/shard_map/pallas_call | solution.py:808
  56.6 1.8 %shard_map.199 = (f32[256,1536]{1,0:T(8,128)}, f32[256,512]{1,0:T(8,128)}, f32[256,1536]{1,0:T(8,128)}, f32[256,512]{1,0:T(8,128)}, f32[32,1536]{1,0:T(8,128)}, ...) custom-call(bf16[9,16,128]{2,1,0:T(8,128)(2,1)S(1)} %shard_map.197.r, ...), custom_call_target="tpu_custom_call", output_to_operand_aliasing={{0}: (6, {}), {1}: (7, {}), {2}: (8, {}), {3}: (9, {})} | custom-call | flops 100663296 | bytes 1048576 | tf_op jit(solution)/shard_map/pallas_call | solution.py:817
  (27 shorter events, 1.9 us)
Async XLA Ops:
  0.6 3.7 %collective-permute-start = (bf16[256,1536]{1,0:T(8,128)(2,1)}, bf16[256,1536]{1,0:T(8,128)(2,1)S(1)}, u32[]{:S(2)}, u32[]{:S(2)}) collective-permute-start(bf16[256,1536]{1,0:T(8,128)(2,1)} %refs_4_.1), channel_id=1, source_target_pairs={{0,1},{1,0},{2,3},{3,2},{4,5},{5,4},{6,7},{7,6},{8,9},{9,8},{10,11... | collective-permute-start | bytes 2359304 | tf_op jit(solution)/shard_map/ppermute | solution.py:560
  1.2 3.2 %collective-permute-start.1 = (bf16[256,512]{1,0:T(8,128)(2,1)}, bf16[256,512]{1,0:T(8,128)(2,1)S(1)}, u32[]{:S(2)}, u32[]{:S(2)}) collective-permute-start(bf16[256,512]{1,0:T(8,128)(2,1)} %refs_7_.1), channel_id=1, source_target_pairs={{0,1},{1,0},{2,3},{3,2},{4,5},{5,4},{6,7},{7,6},{8,9},{9,8},{10,11... | collective-permute-start | bytes 786440 | tf_op jit(solution)/shard_map/ppermute | solution.py:560
  1.2 3.1 %collective-permute-start.2 = (f32[32,1536]{1,0:T(8,128)}, f32[32,1536]{1,0:T(8,128)S(1)}, u32[]{:S(2)}, u32[]{:S(2)}) collective-permute-start(f32[32,1536]{1,0:T(8,128)} %bitcast.27), channel_id=1, source_target_pairs={{0,1},{1,0},{2,3},{3,2},{4,5},{5,4},{6,7},{7,6},{8,9},{9,8},{10,11... | collective-permute-start | bytes 589832 | tf_op jit(solution)/shard_map/ppermute | solution.py:560
  1.7 2.7 %collective-permute-start.3 = (f32[32,512]{1,0:T(8,128)}, f32[32,512]{1,0:T(8,128)S(1)}, u32[]{:S(2)}, u32[]{:S(2)}) collective-permute-start(f32[32,512]{1,0:T(8,128)} %bitcast.29), channel_id=1, source_target_pairs={{0,1},{1,0},{2,3},{3,2},{4,5},{5,4},{6,7},{7,6},{8,9},{9,8},{10,11... | collective-permute-start | bytes 196616 | tf_op jit(solution)/shard_map/ppermute | solution.py:560
  11.4 1.4 %collective-permute-start.4 = (f32[64,256]{1,0:T(8,128)S(1)}, f32[64,256]{1,0:T(8,128)S(1)}, u32[]{:S(2)}, u32[]{:S(2)}) collective-permute-start(f32[64,256]{1,0:T(8,128)S(1)} %get-tuple-element.73), channel_id=1, source_target_pairs={{0,1},{1,0},{2,3},{3,2},{4,5},{5,4},{6,7},{7,6},{8,9},{9,8},{10,11... | collective-permute-start | bytes 196616 | tf_op jit(solution)/shard_map/ppermute | solution.py:560
  12.8 15.0 %collective-permute-start.13 = (bf16[256,2048]{1,0:T(8,128)(2,1)S(1)}, bf16[256,2048]{1,0:T(8,128)(2,1)S(1)}, u32[]{:S(2)}, u32[]{:S(2)}) collective-permute-start(bf16[256,2048]{1,0:T(8,128)(2,1)S(1)} %get-tuple-element.79.refs_3_), channel_id=1, source_target_pairs={{0,1},{1,0},{2,3},{3,2},{4,5},{5,4},{6,7},{7,6},{8,9},{9,8},{10,11... | collective-permute-start | bytes 3145736 | tf_op jit(solution)/shard_map/ppermute | solution.py:560
  13.2 5.7 %collective-permute-start.8 = (f32[8,144,144]{2,1,0:T(8,128)S(1)}, f32[8,144,144]{2,1,0:T(8,128)S(1)}, u32[]{:S(2)}, u32[]{:S(2)}) collective-permute-start(f32[8,144,144]{2,1,0:T(8,128)S(1)} %get-tuple-element.77.refs_0_), channel_id=1, source_target_pairs={{0,1},{1,0},{2,3},{3,2},{4,5},{5,4},{6,7},{7,6},{8,9},{9,8},{10,11... | collective-permute-start | bytes 1990664 | tf_op jit(solution)/shard_map/ppermute | solution.py:560
  13.4 8.6 %collective-permute-start.7 = (f32[64,256]{1,0:T(8,128)S(1)}, f32[64,256]{1,0:T(8,128)S(1)}, u32[]{:S(2)}, u32[]{:S(2)}) collective-permute-start(f32[64,256]{1,0:T(8,128)S(1)} %get-tuple-element.76.refs_0_), channel_id=1, source_target_pairs={{0,24},{2,26},{4,28},{6,30},{8,16},{10,18},{12,20},{14,22},{16,8},... | collective-permute-start | bytes 196616 | tf_op jit(solution)/shard_map/ppermute | solution.py:560
  18.3 5.9 %collective-permute-start.6 = (f32[64,256]{1,0:T(8,128)S(1)}, f32[64,256]{1,0:T(8,128)S(1)}, u32[]{:S(2)}, u32[]{:S(2)}) collective-permute-start(f32[64,256]{1,0:T(8,128)S(1)} %get-tuple-element.76.refs_0_), channel_id=1, source_target_pairs={{0,16},{2,18},{4,20},{6,22},{8,24},{10,26},{12,28},{14,30},{16,0},... | collective-permute-start | bytes 196616 | tf_op jit(solution)/shard_map/ppermute | solution.py:560
  18.3 5.9 %collective-permute-start.5 = (f32[64,256]{1,0:T(8,128)S(1)}, f32[64,256]{1,0:T(8,128)S(1)}, u32[]{:S(2)}, u32[]{:S(2)}) collective-permute-start(f32[64,256]{1,0:T(8,128)S(1)} %get-tuple-element.76.refs_0_), channel_id=1, source_target_pairs={{0,8},{2,10},{4,12},{6,14},{8,0},{10,2},{12,4},{14,6},{16,24},{18,... | collective-permute-start | bytes 196616 | tf_op jit(solution)/shard_map/ppermute | solution.py:560
  21.9 2.3 %collective-permute-start.9 = (f32[8,1024]{1,0:T(8,128)S(1)}, f32[8,1024]{1,0:T(8,128)S(1)}, u32[]{:S(2)}, u32[]{:S(2)}) collective-permute-start(f32[8,1024]{1,0:T(8,128)S(1)} %shard_map.191.refs_4_), channel_id=1, source_target_pairs={{0,1},{1,0},{2,3},{3,2},{4,5},{5,4},{6,7},{7,6},{8,9},{9,8},{10,11... | collective-permute-start | bytes 98312 | tf_op jit(solution)/shard_map/ppermute | solution.py:560
  24.2 5.3 %collective-permute-start.12 = (f32[64,256]{1,0:T(8,128)S(1)}, f32[64,256]{1,0:T(8,128)S(1)}, u32[]{:S(2)}, u32[]{:S(2)}) collective-permute-start(f32[64,256]{1,0:T(8,128)S(1)} %shard_map.192.refs_0_), channel_id=1, source_target_pairs={{0,6},{2,4},{4,2},{6,0},{8,14},{10,12},{12,10},{14,8},{16,22},{18,... | collective-permute-start | bytes 196616 | tf_op jit(solution)/shard_map/ppermute | solution.py:560
  26.7 4.3 %collective-permute-start.11 = (f32[64,256]{1,0:T(8,128)S(1)}, f32[64,256]{1,0:T(8,128)S(1)}, u32[]{:S(2)}, u32[]{:S(2)}) collective-permute-start(f32[64,256]{1,0:T(8,128)S(1)} %shard_map.192.refs_0_), channel_id=1, source_target_pairs={{0,4},{2,6},{4,0},{6,2},{8,12},{10,14},{12,8},{14,10},{16,20},{18,... | collective-permute-start | bytes 196616 | tf_op jit(solution)/shard_map/ppermute | solution.py:560
  27.2 4.3 %collective-permute-start.10 = (f32[64,256]{1,0:T(8,128)S(1)}, f32[64,256]{1,0:T(8,128)S(1)}, u32[]{:S(2)}, u32[]{:S(2)}) collective-permute-start(f32[64,256]{1,0:T(8,128)S(1)} %shard_map.192.refs_0_), channel_id=1, source_target_pairs={{0,2},{2,0},{4,6},{6,4},{8,10},{10,8},{12,14},{14,12},{16,18},{18,... | collective-permute-start | bytes 196616 | tf_op jit(solution)/shard_map/ppermute | solution.py:560
  34.9 5.2 %collective-permute-start.14 = (bf16[9,16,128]{2,1,0:T(8,128)(2,1)S(1)}, bf16[9,16,128]{2,1,0:T(8,128)(2,1)S(1)}, u32[]{:S(2)}, u32[]{:S(2)}) collective-permute-start(bf16[9,16,128]{2,1,0:T(8,128)(2,1)S(1)} %get-tuple-element.83), channel_id=1, source_target_pairs={{0,2},{2,0},{4,6},{6,4},{8,10},{10,8},{12,14},{14,12},{16,18},{18,... | collective-permute-start | bytes 110600 | tf_op jit(solution)/shard_map/ppermute | solution.py:560
  35.5 4.7 %collective-permute-start.15 = (bf16[9,16,128]{2,1,0:T(8,128)(2,1)S(1)}, bf16[9,16,128]{2,1,0:T(8,128)(2,1)S(1)}, u32[]{:S(2)}, u32[]{:S(2)}) collective-permute-start(bf16[9,16,128]{2,1,0:T(8,128)(2,1)S(1)} %get-tuple-element.84), channel_id=1, source_target_pairs={{0,4},{2,6},{4,0},{6,2},{8,12},{10,14},{12,8},{14,10},{16,20},{18,... | collective-permute-start | bytes 110600 | tf_op jit(solution)/shard_map/ppermute | solution.py:560
  37.0 4.9 %collective-permute-start.16 = (bf16[9,16,128]{2,1,0:T(8,128)(2,1)S(1)}, bf16[9,16,128]{2,1,0:T(8,128)(2,1)S(1)}, u32[]{:S(2)}, u32[]{:S(2)}) collective-permute-start(bf16[9,16,128]{2,1,0:T(8,128)(2,1)S(1)} %get-tuple-element.85), channel_id=1, source_target_pairs={{0,6},{2,4},{4,2},{6,0},{8,14},{10,12},{12,10},{14,8},{16,22},{18,... | collective-permute-start | bytes 110600 | tf_op jit(solution)/shard_map/ppermute | solution.py:560
  41.9 5.8 %collective-permute-start.19 = (bf16[9,16,128]{2,1,0:T(8,128)(2,1)S(1)}, bf16[9,16,128]{2,1,0:T(8,128)(2,1)S(1)}, u32[]{:S(2)}, u32[]{:S(2)}) collective-permute-start(bf16[9,16,128]{2,1,0:T(8,128)(2,1)S(1)} %shard_map.196.refs_0_), channel_id=1, source_target_pairs={{0,24},{2,26},{4,28},{6,30},{8,16},{10,18},{12,20},{14,22},{16,8},... | collective-permute-start | bytes 110600 | tf_op jit(solution)/shard_map/ppermute | solution.py:560
  44.7 4.9 %collective-permute-start.18 = (bf16[9,16,128]{2,1,0:T(8,128)(2,1)S(1)}, bf16[9,16,128]{2,1,0:T(8,128)(2,1)S(1)}, u32[]{:S(2)}, u32[]{:S(2)}) collective-permute-start(bf16[9,16,128]{2,1,0:T(8,128)(2,1)S(1)} %shard_map.196.refs_0_), channel_id=1, source_target_pairs={{0,16},{2,18},{4,20},{6,22},{8,24},{10,26},{12,28},{14,30},{16,0},... | collective-permute-start | bytes 110600 | tf_op jit(solution)/shard_map/ppermute | solution.py:560
  44.7 4.9 %collective-permute-start.17 = (bf16[9,16,128]{2,1,0:T(8,128)(2,1)S(1)}, bf16[9,16,128]{2,1,0:T(8,128)(2,1)S(1)}, u32[]{:S(2)}, u32[]{:S(2)}) collective-permute-start(bf16[9,16,128]{2,1,0:T(8,128)(2,1)S(1)} %shard_map.196.refs_0_), channel_id=1, source_target_pairs={{0,8},{2,10},{4,12},{6,14},{8,0},{10,2},{12,4},{14,6},{16,24},{18,... | collective-permute-start | bytes 110600 | tf_op jit(solution)/shard_map/ppermute | solution.py:560
  49.6 4.9 %collective-permute-start.22 = (bf16[9,16,128]{2,1,0:T(8,128)(2,1)S(1)}, bf16[9,16,128]{2,1,0:T(8,128)(2,1)S(1)}, u32[]{:S(2)}, u32[]{:S(2)}) collective-permute-start(bf16[9,16,128]{2,1,0:T(8,128)(2,1)S(1)} %shard_map.197.refs_0_), channel_id=1, source_target_pairs={{0,6},{2,4},{4,2},{6,0},{8,14},{10,12},{12,10},{14,8},{16,22},{18,... | collective-permute-start | bytes 110600 | tf_op jit(solution)/shard_map/ppermute | solution.py:560
  51.1 5.1 %collective-permute-start.21 = (bf16[9,16,128]{2,1,0:T(8,128)(2,1)S(1)}, bf16[9,16,128]{2,1,0:T(8,128)(2,1)S(1)}, u32[]{:S(2)}, u32[]{:S(2)}) collective-permute-start(bf16[9,16,128]{2,1,0:T(8,128)(2,1)S(1)} %shard_map.197.refs_0_), channel_id=1, source_target_pairs={{0,4},{2,6},{4,0},{6,2},{8,12},{10,14},{12,8},{14,10},{16,20},{18,... | collective-permute-start | bytes 110600 | tf_op jit(solution)/shard_map/ppermute | solution.py:560
  52.6 4.0 %collective-permute-start.20 = (bf16[9,16,128]{2,1,0:T(8,128)(2,1)S(1)}, bf16[9,16,128]{2,1,0:T(8,128)(2,1)S(1)}, u32[]{:S(2)}, u32[]{:S(2)}) collective-permute-start(bf16[9,16,128]{2,1,0:T(8,128)(2,1)S(1)} %shard_map.197.refs_0_), channel_id=1, source_target_pairs={{0,2},{2,0},{4,6},{6,4},{8,10},{10,8},{12,14},{14,12},{16,18},{18,... | collective-permute-start | bytes 110600 | tf_op jit(solution)/shard_map/ppermute | solution.py:560

commit v6 on v5

--- a/solution.py
+++ b/solution.py
@@ -110,9 +110,9 @@
 
 
 def prepare_kernel(blocks, ready, *refs):
-    sources, rest = refs[:12], refs[12:]
-    normed, normed_t, part, bias, index_t, table_pad, bucket, *kept = rest[:17]
-    table, sems = rest[17:]
+    sources, rest = refs[:10], refs[10:]
+    normed, normed_t, part, bias, index_t, table_pad, bucket, *kept = rest[:15]
+    table, sems = rest[15:]
     copies = fetch(list(zip(sources, [bucket, table] + kept)), sems)
     tokens, gain, w_own = kept[:3]
     me = lax.axis_index("mp")
@@ -125,11 +125,12 @@
     table_pad[:, : table.shape[1]] = table[...]
     index_t[...] = bucket[...].T
     gather_bias(bias, range(ready), table_pad, index_t, bucket)
-    for copy in copies[2:5]:
+    for copy in copies[2:4]:
         copy.wait()
     x_hat, _ = norm_forward(tokens[...])
     normed[...] = (x_hat * gain[...]).astype(BF16)
     normed_t[...] = normed[...].T
+    copies[4].wait()
     part[...] = nn(normed[:, block_columns(me, 0, blocks, width)], w_own[...])
     for copy in copies[5:]:
         copy.wait()
@@ -138,9 +139,10 @@
 def attend_kernel(blocks, share, *refs):
     normed, normed_t, part, bias_ready, index_t, table_pad, bucket, cot, region = refs[:9]
     own, arrived = refs[9:13], refs[13 : 9 + 4 * blocks]
-    rest = refs[9 + 4 * blocks :]
+    sources, rest = refs[9 + 4 * blocks : 11 + 4 * blocks], refs[11 + 4 * blocks :]
     terms, lefts, rest = rest[:blocks], rest[blocks : 2 * blocks], rest[2 * blocks :]
-    score_sum, packed, proj, mixed_grad, mixed, bias = rest
+    score_sum, packed, in_error, out_error, proj, mixed_grad, mixed, bias, sems = rest
+    copies = fetch(list(zip(sources, (in_error, out_error))), sems)
     w_in, w_out, in_basis, out_basis = (
         [own[at]] + list(arrived[at : at + blocks - 1]) for at in range(4)
     )
@@ -225,6 +227,8 @@
         ):
             left = folded(nt(stacked(basis[...]), terms[step][:, at])) * share
             lefts[step][place : place + rank, :] = left
+    for copy in copies:
+        copy.wait()
 
 
 def token_kernel(blocks, packed, *refs):
@@ -632,8 +636,6 @@
         cot_rows,
         region_ids,
         *own[1:],
-        in_error[0],
-        out_error[0],
     )
     normed, normed_t, part, bias, index_t, table_pad, bucket, *kept = call(
         functools.partial(prepare_kernel, blocks, READY_HEADS),
@@ -647,13 +649,14 @@
             shape((span, span), jnp.int32),
         )
         + tuple(shape(array.shape, array.dtype) for array in operands[2:]),
-        [pltpu.VMEM(bias_table.shape, F32), pltpu.SemaphoreType.DMA((12,))],
+        [pltpu.VMEM(bias_table.shape, F32), pltpu.SemaphoreType.DMA((10,))],
         flops=2 * row_count * width * wide,
         moved=4 << 20,
-        in_specs=[HBM] * 12,
-        out_specs=[VMEM] * 17,
+        in_specs=[HBM] * 10,
+        out_specs=[VMEM] * 15,
     )(*in_hbm(*operands))
-    token_rows, gain, w_in_own, cot_rows, region, *own, in_errors, out_errors = kept
+    token_rows, gain, w_in_own, cot_rows, region, *own = kept
+    errors = (in_error[0], out_error[0])
     in_basis_t, out_basis_t = own[1:]
 
     left_shape = shape((2 * rank, width), F32)
@@ -661,19 +664,21 @@
         functools.partial(attend_kernel, blocks, 1.0 / n_mp),
         (shape((width, both), BF16),) * blocks
         + (left_shape,) * blocks
-        + (shape((head_count, span, span), F32), shape((row_count, wide), BF16)),
+        + (shape((head_count, span, span), F32), shape((row_count, wide), BF16))
+        + tuple(shape(array.shape, F32) for array in errors),
         [
             pltpu.VMEM((row_count, wide), BF16),
             pltpu.VMEM((row_count, features), BF16),
             pltpu.VMEM((row_count, features), BF16),
             pltpu.VMEM((head_count, span, span), F32),
+            pltpu.SemaphoreType.DMA((2,)),
         ],
         flops=4 * row_count * features * both,
         moved=8 << 20,
-        in_specs=[VMEM] * (13 + len(arrived)),
-        out_specs=[VMEM] * (2 * blocks + 2),
-    )(normed, normed_t, part, bias, index_t, table_pad, bucket, cot_rows, region, w_in_own, *own, *arrived)
-    *outputs, score_sum, packed = outputs
+        in_specs=[VMEM] * (13 + len(arrived)) + [HBM] * 2,
+        out_specs=[VMEM] * (2 * blocks + 4),
+    )(normed, normed_t, part, bias, index_t, table_pad, bucket, cot_rows, region, w_in_own, *own, *arrived, *in_hbm(*errors))
+    *outputs, score_sum, packed, in_errors, out_errors = outputs
     terms, lefts = outputs[:blocks], outputs[blocks:]
     scores_of = [score_sum]
 

time: 58.7 us -> 59.4 us (1.012)
  Pallas kernels: 22.5 us -> 23.1 us
where the time goes in v6:
time: 59.4 us; the launch traced here: 59.2 us
  Pallas kernels  23.1 us (39%)
  starting transfers between devices  22.8 us (38%)
  waiting for transfers between devices  12.3 us (21%)
  between operations  0.95 us (2%)
    ppermute x23, starting transfers between devices, exchange(): lax.ppermute(value, axis, [(at, at ^ distance) for at in range(count)])  22.8 us
    ppermute x23, waiting for transfers between devices, exchange(): lax.ppermute(value, axis, [(at, at ^ distance) for at in range(count)])  12.3 us
    pallas_call x1, Pallas kernels, shards(): call(functools.partial(attend_kernel, blocks, 1.0 / n_mp), (shape((width,...  7.53 us
    pallas_call x1, Pallas kernels, shards(): call(functools.partial(ortho_kernel, 1.0 / n_dp, len(lefts), len(stats)),...  3.43 us
    pallas_call x1, Pallas kernels, shards(): call(functools.partial(table_kernel, blocks), shape((head_count, padded +...  2.98 us
    pallas_call x1, Pallas kernels, shards(): call(functools.partial(prepare_kernel, blocks, READY_HEADS), (shape((row_...  2.74 us
    pallas_call x1, Pallas kernels, shards(): call(functools.partial(last_kernel, 1.0 / n_dp, 1.0 / (n_dp * n_mp), late...  1.76 us
    pallas_call x1, Pallas kernels, shards(): call(functools.partial(token_kernel, blocks), (shape((row_count, features...  1.71 us
  transfers between devices with their start and end apart: 23, of which 10 were waited for; matrix products, arithmetic and copies ran while one was open for 0% of the time, Pallas kernels for 17%

profile of v6, /device:TPU:0, one launch (start us, length us, event | category | flops | bytes accessed | tf_op | source)
XLA Modules:
  0.0 59.2 jit_solution(6881839158999661454)
XLA Ops:
  0.6 0.5 collective-permute-start
  1.8 2.7 %shard_map.187 = (bf16[288,512]{1,0:T(8,128)(2,1)S(1)}, bf16[512,288]{1,0:T(8,128)(2,1)S(1)}, f32[288,1536]{1,0:T(8,128)S(1)}, f32[2,144,144]{2,1,0:T(8,128)S(1)...) custom-call(s32[144,144]{1,0:T(8,128)} %refs_0_.1, ...), custom_call_target="tpu_custom_call" | custom-call | flops 226492416 | bytes 4194304 | tf_op jit(solution)/shard_map/pallas_call | solution.py:640
  4.5 7.5 %shard_map.188 = (bf16[256,2048]{1,0:T(8,128)(2,1)S(1)}, bf16[256,2048]{1,0:T(8,128)(2,1)S(1)}, f32[64,256]{1,0:T(8,128)S(1)}, f32[64,256]{1,0:T(8,128)S(1)}, f3...) custom-call(bf16[288,512]{1,0:T(8,128)(2,1)S(1)} %get-tuple-element., ...), custom_call_target="tpu_custom_call" | custom-call | flops 1207959552 | bytes 8388608 | tf_op jit(solution)/shard_map/pallas_call | solution.py:663
  12.1 0.5 collective-permute-start.4
  12.6 0.7 %shard_map.189.left_own = f32[64,256]{1,0:T(8,128)S(1)} custom-call(f32[64,256]{1,0:T(8,128)S(1)} %get-tuple-element.70.term_left, f32[256,1536]{1,0:T(8,128)S(1)} %get-tuple-element.71.in_error.refs_2_, f32[256,512]{1,0:T(8,128)S(1)} %get-tuple-element.72.out_error.refs_3_, f32[32,1536]{1,0:T(8,128)S(1)} %get-tuple-element.65.refs_11_.in_basis, ...), custom_call_target="tpu_custom_call" | custom-call | flops 134217728 | bytes 3145728 | tf_op jit(solution)/shard_map/pallas_call | solution.py:697
  14.0 5.0 %collective-permute-start.7 = (f32[64,256]{1,0:T(8,128)S(1)}, f32[64,256]{1,0:T(8,128)S(1)}, u32[]{:S(2)}, u32[]{:S(2)}) collective-permute-start(f32[64,256]{1,0:T(8,128)S(1)} %get-tuple-element.76.refs_0_), channel_id=1, source_target_pairs={{0,24},{2,26},{4,28},{6,30},{8,16},{10,18},{12,20},{14,22},{16,8},... | collective-permute-start | bytes 196616 | tf_op jit(solution)/shard_map/ppermute | solution.py:564
  19.0 0.6 collective-permute-start.5
  19.6 3.0 %shard_map.191.refs_4_ = f32[8,1024]{1,0:T(8,128)S(1)} custom-call(f32[8,144,144]{2,1,0:T(8,128)S(1)} %get-tuple-element.77.refs_0_, f32[8,144,144]{2,1,0:T(8,128)S(1)} %collective-permute-done.8.refs_1_, bf16[256,2048]{1,0:T(8,128)(2,1)S(1)} %get-tuple-element.78.refs_2_.refs_0_, bf16[256,2048]{1,0:T(8,128)(2,1)S(1)} %get-tuple-element.79.refs_3_, ...), custom_call_target="tpu_custom_call" | custom-call | flops 452984832 | bytes 4194304 | tf_op jit(solution)/shard_map/pallas_call | solution.py:717
  22.7 2.2 %collective-permute-done.6.refs_2_ = f32[64,256]{1,0:T(8,128)S(1)} collective-permute-done((f32[64,256]{1,0:T(8,128)S(1)}, f32[64,256]{1,0:T(8,128)S(1)}, u32[]{:S(2)}, u32[]{:S(2)}) %collective-permute-start.6) | collective-permute-done | bytes 65568 | tf_op jit(solution)/shard_map/ppermute | solution.py:564
  24.9 2.5 %collective-permute-start.12 = (f32[64,256]{1,0:T(8,128)S(1)}, f32[64,256]{1,0:T(8,128)S(1)}, u32[]{:S(2)}, u32[]{:S(2)}) collective-permute-start(f32[64,256]{1,0:T(8,128)S(1)} %shard_map.192.refs_0_), channel_id=1, source_target_pairs={{0,6},{2,4},{4,2},{6,0},{8,14},{10,12},{12,10},{14,8},{16,22},{18,... | collective-permute-start | bytes 196616 | tf_op jit(solution)/shard_map/ppermute | solution.py:564
  27.4 0.5 collective-permute-start.11
  27.9 0.5 collective-permute-start.10
  28.5 0.6 shard_map.193.refs_6_.refs_3_.refs_5_
  29.0 1.2 %collective-permute-done.12.refs_3_ = f32[64,256]{1,0:T(8,128)S(1)} collective-permute-done((f32[64,256]{1,0:T(8,128)S(1)}, f32[64,256]{1,0:T(8,128)S(1)}, u32[]{:S(2)}, u32[]{:S(2)}) %collective-permute-start.12) | collective-permute-done | bytes 65568 | tf_op jit(solution)/shard_map/ppermute | solution.py:564
  30.3 1.4 %collective-permute-done.11.refs_2_ = f32[64,256]{1,0:T(8,128)S(1)} collective-permute-done((f32[64,256]{1,0:T(8,128)S(1)}, f32[64,256]{1,0:T(8,128)S(1)}, u32[]{:S(2)}, u32[]{:S(2)}) %collective-permute-start.11) | collective-permute-done | bytes 65568 | tf_op jit(solution)/shard_map/ppermute | solution.py:564
  31.7 0.5 collective-permute-done.10.refs_1_
  32.2 3.4 %shard_map.194 = (f32[64,256]{1,0:T(8,128)S(1)}, bf16[9,16,128]{2,1,0:T(8,128)(2,1)S(1)}, bf16[9,16,128]{2,1,0:T(8,128)(2,1)S(1)}, bf16[9,16,128]{2,1,0:T(8,128)(2,1)S(1)}, bf16[9,16,128]{2,1,0:T(8,128)(2,1)S(1)}) custom-call(f32[64,256]{1,0:T(8,128)S(1)} %shard_map.192.refs_0_, f32[64,256]{1,0:T(8,128)S(1)} %collective-permute-done.10.refs_1_, ...), custom_call_target="tpu_custom_call" | custom-call | flops 201326592 | bytes 3145728 | tf_op jit(solution)/shard_map/pallas_call | solution.py:753
  35.6 0.6 collective-permute-start.14
  36.2 1.5 %collective-permute-start.15 = (bf16[9,16,128]{2,1,0:T(8,128)(2,1)S(1)}, bf16[9,16,128]{2,1,0:T(8,128)(2,1)S(1)}, u32[]{:S(2)}, u32[]{:S(2)}) collective-permute-start(bf16[9,16,128]{2,1,0:T(8,128)(2,1)S(1)} %get-tuple-element.84), channel_id=1, source_target_pairs={{0,4},{2,6},{4,0},{6,2},{8,12},{10,14},{12,8},{14,10},{16,20},{18,... | collective-permute-start | bytes 110600 | tf_op jit(solution)/shard_map/ppermute | solution.py:564
  37.7 1.4 %collective-permute-start.16 = (bf16[9,16,128]{2,1,0:T(8,128)(2,1)S(1)}, bf16[9,16,128]{2,1,0:T(8,128)(2,1)S(1)}, u32[]{:S(2)}, u32[]{:S(2)}) collective-permute-start(bf16[9,16,128]{2,1,0:T(8,128)(2,1)S(1)} %get-tuple-element.85), channel_id=1, source_target_pairs={{0,6},{2,4},{4,2},{6,0},{8,14},{10,12},{12,10},{14,8},{16,22},{18,... | collective-permute-start | bytes 110600 | tf_op jit(solution)/shard_map/ppermute | solution.py:564
  39.2 1.7 %shard_map.195 = (bf16[288,512]{1,0:T(8,128)(2,1)}, f32[8,128]{1,0:T(8,128)S(1)}) custom-call(bf16[288,1536]{1,0:T(8,128)(2,1)S(1)} %get-tuple-element.67.packed, bf16[256,1536]{1,0:T(8,128)(2,1)S(1)} %get-tuple-element.63.refs_9_.refs_4_.refs_0_, bf16[256,1536]{1,0:T(8,128)(2,1)S(1)} %collective-permute-done.refs_13_.refs_5_.refs_1_, ...), custom_call_target="tpu_custom_call" | custom-call | flops 452984832 | bytes 4194304 | tf_op jit(solution)/shard_map/pallas_call | solution.py:763
  40.9 1.7 %collective-permute-done.16.refs_3_ = bf16[9,16,128]{2,1,0:T(8,128)(2,1)S(1)} collective-permute-done((bf16[9,16,128]{2,1,0:T(8,128)(2,1)S(1)}, bf16[9,16,128]{2,1,0:T(8,128)(2,1)S(1)}, u32[]{:S(2)}, u32[]{:S(2)}) %collective-permute-start.16) | collective-permute-done | bytes 36896 | tf_op jit(solution)/shard_map/ppermute | solution.py:564
  42.6 2.8 %collective-permute-start.19 = (bf16[9,16,128]{2,1,0:T(8,128)(2,1)S(1)}, bf16[9,16,128]{2,1,0:T(8,128)(2,1)S(1)}, u32[]{:S(2)}, u32[]{:S(2)}) collective-permute-start(bf16[9,16,128]{2,1,0:T(8,128)(2,1)S(1)} %shard_map.196.refs_0_), channel_id=1, source_target_pairs={{0,24},{2,26},{4,28},{6,30},{8,16},{10,18},{12,20},{14,22},{16,8},... | collective-permute-start | bytes 110600 | tf_op jit(solution)/shard_map/ppermute | solution.py:564
  45.4 1.6 %collective-permute-start.17 = (bf16[9,16,128]{2,1,0:T(8,128)(2,1)S(1)}, bf16[9,16,128]{2,1,0:T(8,128)(2,1)S(1)}, u32[]{:S(2)}, u32[]{:S(2)}) collective-permute-start(bf16[9,16,128]{2,1,0:T(8,128)(2,1)S(1)} %shard_map.196.refs_0_), channel_id=1, source_target_pairs={{0,8},{2,10},{4,12},{6,14},{8,0},{10,2},{12,4},{14,6},{16,24},{18,... | collective-permute-start | bytes 110600 | tf_op jit(solution)/shard_map/ppermute | solution.py:564
  47.1 1.4 %collective-permute-done.19.refs_3_ = bf16[9,16,128]{2,1,0:T(8,128)(2,1)S(1)} collective-permute-done((bf16[9,16,128]{2,1,0:T(8,128)(2,1)S(1)}, bf16[9,16,128]{2,1,0:T(8,128)(2,1)S(1)}, u32[]{:S(2)}, u32[]{:S(2)}) %collective-permute-start.19) | collective-permute-done | bytes 36896 | tf_op jit(solution)/shard_map/ppermute | solution.py:564
  48.4 1.8 %collective-permute-done.18.refs_2_ = bf16[9,16,128]{2,1,0:T(8,128)(2,1)S(1)} collective-permute-done((bf16[9,16,128]{2,1,0:T(8,128)(2,1)S(1)}, bf16[9,16,128]{2,1,0:T(8,128)(2,1)S(1)}, u32[]{:S(2)}, u32[]{:S(2)}) %collective-permute-start.18) | collective-permute-done | bytes 36896 | tf_op jit(solution)/shard_map/ppermute | solution.py:564
  50.3 1.5 %collective-permute-start.22 = (bf16[9,16,128]{2,1,0:T(8,128)(2,1)S(1)}, bf16[9,16,128]{2,1,0:T(8,128)(2,1)S(1)}, u32[]{:S(2)}, u32[]{:S(2)}) collective-permute-start(bf16[9,16,128]{2,1,0:T(8,128)(2,1)S(1)} %shard_map.197.refs_0_), channel_id=1, source_target_pairs={{0,6},{2,4},{4,2},{6,0},{8,14},{10,12},{12,10},{14,8},{16,22},{18,... | collective-permute-start | bytes 110600 | tf_op jit(solution)/shard_map/ppermute | solution.py:564
  51.8 1.5 %collective-permute-start.21 = (bf16[9,16,128]{2,1,0:T(8,128)(2,1)S(1)}, bf16[9,16,128]{2,1,0:T(8,128)(2,1)S(1)}, u32[]{:S(2)}, u32[]{:S(2)}) collective-permute-start(bf16[9,16,128]{2,1,0:T(8,128)(2,1)S(1)} %shard_map.197.refs_0_), channel_id=1, source_target_pairs={{0,4},{2,6},{4,0},{6,2},{8,12},{10,14},{12,8},{14,10},{16,20},{18,... | collective-permute-start | bytes 110600 | tf_op jit(solution)/shard_map/ppermute | solution.py:564
  53.3 0.5 collective-permute-start.20
  53.9 1.4 %collective-permute-done.22.refs_1_.refs_3_ = bf16[9,16,128]{2,1,0:T(8,128)(2,1)S(1)} collective-permute-done((bf16[9,16,128]{2,1,0:T(8,128)(2,1)S(1)}, bf16[9,16,128]{2,1,0:T(8,128)(2,1)S(1)}, u32[]{:S(2)}, u32[]{:S(2)}) %collective-permute-start.22) | collective-permute-done | bytes 36896 | tf_op jit(solution)/shard_map/ppermute | solution.py:564
  55.2 1.6 %shard_map.198 = (f32[256,1536]{1,0:T(8,128)}, f32[256,512]{1,0:T(8,128)}, f32[256,1536]{1,0:T(8,128)}, f32[256,512]{1,0:T(8,128)}) custom-call(bf16[9,16,128]{2,1,0:T(8,128)(2,1)S(1)} %shard_map.197.refs_0_, bf16[9,16,128]{2,1,0:T(8,128)(2,1)S(1)} %collective-permute-done.22.refs_1_.refs_3_, f32[64,256]{1,0:T(8,128)S(1)} %get-tuple-element.80.refs_5_.refs_2_.refs_4_, ...), custom_call_target="tpu_custom_call" | custom-call | flops 100663296 | bytes 1048576 | tf_op jit(solution)/shard_map/pallas_call | solution.py:813
  57.3 1.8 %shard_map.199 = (f32[256,1536]{1,0:T(8,128)}, f32[256,512]{1,0:T(8,128)}, f32[256,1536]{1,0:T(8,128)}, f32[256,512]{1,0:T(8,128)}, f32[32,1536]{1,0:T(8,128)}, ...) custom-call(bf16[9,16,128]{2,1,0:T(8,128)(2,1)S(1)} %shard_map.197.r, ...), custom_call_target="tpu_custom_call", output_to_operand_aliasing={{0}: (6, {}), {1}: (7, {}), {2}: (8, {}), {3}: (9, {})} | custom-call | flops 100663296 | bytes 1048576 | tf_op jit(solution)/shard_map/pallas_call | solution.py:822
  (27 shorter events, 1.9 us)
Async XLA Ops:
  0.6 3.9 %collective-permute-start = (bf16[256,1536]{1,0:T(8,128)(2,1)}, bf16[256,1536]{1,0:T(8,128)(2,1)S(1)}, u32[]{:S(2)}, u32[]{:S(2)}) collective-permute-start(bf16[256,1536]{1,0:T(8,128)(2,1)} %refs_4_.1), channel_id=1, source_target_pairs={{0,1},{1,0},{2,3},{3,2},{4,5},{5,4},{6,7},{7,6},{8,9},{9,8},{10,11... | collective-permute-start | bytes 2359304 | tf_op jit(solution)/shard_map/ppermute | solution.py:564
  1.2 3.4 %collective-permute-start.1 = (bf16[256,512]{1,0:T(8,128)(2,1)}, bf16[256,512]{1,0:T(8,128)(2,1)S(1)}, u32[]{:S(2)}, u32[]{:S(2)}) collective-permute-start(bf16[256,512]{1,0:T(8,128)(2,1)} %refs_7_.1), channel_id=1, source_target_pairs={{0,1},{1,0},{2,3},{3,2},{4,5},{5,4},{6,7},{7,6},{8,9},{9,8},{10,11... | collective-permute-start | bytes 786440 | tf_op jit(solution)/shard_map/ppermute | solution.py:564
  1.2 3.3 %collective-permute-start.2 = (f32[32,1536]{1,0:T(8,128)}, f32[32,1536]{1,0:T(8,128)S(1)}, u32[]{:S(2)}, u32[]{:S(2)}) collective-permute-start(f32[32,1536]{1,0:T(8,128)} %bitcast.27), channel_id=1, source_target_pairs={{0,1},{1,0},{2,3},{3,2},{4,5},{5,4},{6,7},{7,6},{8,9},{9,8},{10,11... | collective-permute-start | bytes 589832 | tf_op jit(solution)/shard_map/ppermute | solution.py:564
  1.7 2.8 %collective-permute-start.3 = (f32[32,512]{1,0:T(8,128)}, f32[32,512]{1,0:T(8,128)S(1)}, u32[]{:S(2)}, u32[]{:S(2)}) collective-permute-start(f32[32,512]{1,0:T(8,128)} %bitcast.29), channel_id=1, source_target_pairs={{0,1},{1,0},{2,3},{3,2},{4,5},{5,4},{6,7},{7,6},{8,9},{9,8},{10,11... | collective-permute-start | bytes 196616 | tf_op jit(solution)/shard_map/ppermute | solution.py:564
  12.1 1.4 %collective-permute-start.4 = (f32[64,256]{1,0:T(8,128)S(1)}, f32[64,256]{1,0:T(8,128)S(1)}, u32[]{:S(2)}, u32[]{:S(2)}) collective-permute-start(f32[64,256]{1,0:T(8,128)S(1)} %get-tuple-element.73), channel_id=1, source_target_pairs={{0,1},{1,0},{2,3},{3,2},{4,5},{5,4},{6,7},{7,6},{8,9},{9,8},{10,11... | collective-permute-start | bytes 196616 | tf_op jit(solution)/shard_map/ppermute | solution.py:564
  13.5 15.0 %collective-permute-start.13 = (bf16[256,2048]{1,0:T(8,128)(2,1)S(1)}, bf16[256,2048]{1,0:T(8,128)(2,1)S(1)}, u32[]{:S(2)}, u32[]{:S(2)}) collective-permute-start(bf16[256,2048]{1,0:T(8,128)(2,1)S(1)} %get-tuple-element.79.refs_3_), channel_id=1, source_target_pairs={{0,1},{1,0},{2,3},{3,2},{4,5},{5,4},{6,7},{7,6},{8,9},{9,8},{10,11... | collective-permute-start | bytes 3145736 | tf_op jit(solution)/shard_map/ppermute | solution.py:564
  13.9 5.7 %collective-permute-start.8 = (f32[8,144,144]{2,1,0:T(8,128)S(1)}, f32[8,144,144]{2,1,0:T(8,128)S(1)}, u32[]{:S(2)}, u32[]{:S(2)}) collective-permute-start(f32[8,144,144]{2,1,0:T(8,128)S(1)} %get-tuple-element.77.refs_0_), channel_id=1, source_target_pairs={{0,1},{1,0},{2,3},{3,2},{4,5},{5,4},{6,7},{7,6},{8,9},{9,8},{10,11... | collective-permute-start | bytes 1990664 | tf_op jit(solution)/shard_map/ppermute | solution.py:564
  14.0 8.6 %collective-permute-start.7 = (f32[64,256]{1,0:T(8,128)S(1)}, f32[64,256]{1,0:T(8,128)S(1)}, u32[]{:S(2)}, u32[]{:S(2)}) collective-permute-start(f32[64,256]{1,0:T(8,128)S(1)} %get-tuple-element.76.refs_0_), channel_id=1, source_target_pairs={{0,24},{2,26},{4,28},{6,30},{8,16},{10,18},{12,20},{14,22},{16,8},... | collective-permute-start | bytes 196616 | tf_op jit(solution)/shard_map/ppermute | solution.py:564
  19.0 5.9 %collective-permute-start.6 = (f32[64,256]{1,0:T(8,128)S(1)}, f32[64,256]{1,0:T(8,128)S(1)}, u32[]{:S(2)}, u32[]{:S(2)}) collective-permute-start(f32[64,256]{1,0:T(8,128)S(1)} %get-tuple-element.76.refs_0_), channel_id=1, source_target_pairs={{0,16},{2,18},{4,20},{6,22},{8,24},{10,26},{12,28},{14,30},{16,0},... | collective-permute-start | bytes 196616 | tf_op jit(solution)/shard_map/ppermute | solution.py:564
  19.0 5.9 %collective-permute-start.5 = (f32[64,256]{1,0:T(8,128)S(1)}, f32[64,256]{1,0:T(8,128)S(1)}, u32[]{:S(2)}, u32[]{:S(2)}) collective-permute-start(f32[64,256]{1,0:T(8,128)S(1)} %get-tuple-element.76.refs_0_), channel_id=1, source_target_pairs={{0,8},{2,10},{4,12},{6,14},{8,0},{10,2},{12,4},{14,6},{16,24},{18,... | collective-permute-start | bytes 196616 | tf_op jit(solution)/shard_map/ppermute | solution.py:564
  22.6 2.3 %collective-permute-start.9 = (f32[8,1024]{1,0:T(8,128)S(1)}, f32[8,1024]{1,0:T(8,128)S(1)}, u32[]{:S(2)}, u32[]{:S(2)}) collective-permute-start(f32[8,1024]{1,0:T(8,128)S(1)} %shard_map.191.refs_4_), channel_id=1, source_target_pairs={{0,1},{1,0},{2,3},{3,2},{4,5},{5,4},{6,7},{7,6},{8,9},{9,8},{10,11... | collective-permute-start | bytes 98312 | tf_op jit(solution)/shard_map/ppermute | solution.py:564
  24.9 5.3 %collective-permute-start.12 = (f32[64,256]{1,0:T(8,128)S(1)}, f32[64,256]{1,0:T(8,128)S(1)}, u32[]{:S(2)}, u32[]{:S(2)}) collective-permute-start(f32[64,256]{1,0:T(8,128)S(1)} %shard_map.192.refs_0_), channel_id=1, source_target_pairs={{0,6},{2,4},{4,2},{6,0},{8,14},{10,12},{12,10},{14,8},{16,22},{18,... | collective-permute-start | bytes 196616 | tf_op jit(solution)/shard_map/ppermute | solution.py:564
  27.4 4.3 %collective-permute-start.11 = (f32[64,256]{1,0:T(8,128)S(1)}, f32[64,256]{1,0:T(8,128)S(1)}, u32[]{:S(2)}, u32[]{:S(2)}) collective-permute-start(f32[64,256]{1,0:T(8,128)S(1)} %shard_map.192.refs_0_), channel_id=1, source_target_pairs={{0,4},{2,6},{4,0},{6,2},{8,12},{10,14},{12,8},{14,10},{16,20},{18,... | collective-permute-start | bytes 196616 | tf_op jit(solution)/shard_map/ppermute | solution.py:564
  27.9 4.3 %collective-permute-start.10 = (f32[64,256]{1,0:T(8,128)S(1)}, f32[64,256]{1,0:T(8,128)S(1)}, u32[]{:S(2)}, u32[]{:S(2)}) collective-permute-start(f32[64,256]{1,0:T(8,128)S(1)} %shard_map.192.refs_0_), channel_id=1, source_target_pairs={{0,2},{2,0},{4,6},{6,4},{8,10},{10,8},{12,14},{14,12},{16,18},{18,... | collective-permute-start | bytes 196616 | tf_op jit(solution)/shard_map/ppermute | solution.py:564
  35.6 5.2 %collective-permute-start.14 = (bf16[9,16,128]{2,1,0:T(8,128)(2,1)S(1)}, bf16[9,16,128]{2,1,0:T(8,128)(2,1)S(1)}, u32[]{:S(2)}, u32[]{:S(2)}) collective-permute-start(bf16[9,16,128]{2,1,0:T(8,128)(2,1)S(1)} %get-tuple-element.83), channel_id=1, source_target_pairs={{0,2},{2,0},{4,6},{6,4},{8,10},{10,8},{12,14},{14,12},{16,18},{18,... | collective-permute-start | bytes 110600 | tf_op jit(solution)/shard_map/ppermute | solution.py:564
  36.2 4.7 %collective-permute-start.15 = (bf16[9,16,128]{2,1,0:T(8,128)(2,1)S(1)}, bf16[9,16,128]{2,1,0:T(8,128)(2,1)S(1)}, u32[]{:S(2)}, u32[]{:S(2)}) collective-permute-start(bf16[9,16,128]{2,1,0:T(8,128)(2,1)S(1)} %get-tuple-element.84), channel_id=1, source_target_pairs={{0,4},{2,6},{4,0},{6,2},{8,12},{10,14},{12,8},{14,10},{16,20},{18,... | collective-permute-start | bytes 110600 | tf_op jit(solution)/shard_map/ppermute | solution.py:564
  37.7 4.9 %collective-permute-start.16 = (bf16[9,16,128]{2,1,0:T(8,128)(2,1)S(1)}, bf16[9,16,128]{2,1,0:T(8,128)(2,1)S(1)}, u32[]{:S(2)}, u32[]{:S(2)}) collective-permute-start(bf16[9,16,128]{2,1,0:T(8,128)(2,1)S(1)} %get-tuple-element.85), channel_id=1, source_target_pairs={{0,6},{2,4},{4,2},{6,0},{8,14},{10,12},{12,10},{14,8},{16,22},{18,... | collective-permute-start | bytes 110600 | tf_op jit(solution)/shard_map/ppermute | solution.py:564
  42.6 5.8 %collective-permute-start.19 = (bf16[9,16,128]{2,1,0:T(8,128)(2,1)S(1)}, bf16[9,16,128]{2,1,0:T(8,128)(2,1)S(1)}, u32[]{:S(2)}, u32[]{:S(2)}) collective-permute-start(bf16[9,16,128]{2,1,0:T(8,128)(2,1)S(1)} %shard_map.196.refs_0_), channel_id=1, source_target_pairs={{0,24},{2,26},{4,28},{6,30},{8,16},{10,18},{12,20},{14,22},{16,8},... | collective-permute-start | bytes 110600 | tf_op jit(solution)/shard_map/ppermute | solution.py:564
  45.4 4.9 %collective-permute-start.18 = (bf16[9,16,128]{2,1,0:T(8,128)(2,1)S(1)}, bf16[9,16,128]{2,1,0:T(8,128)(2,1)S(1)}, u32[]{:S(2)}, u32[]{:S(2)}) collective-permute-start(bf16[9,16,128]{2,1,0:T(8,128)(2,1)S(1)} %shard_map.196.refs_0_), channel_id=1, source_target_pairs={{0,16},{2,18},{4,20},{6,22},{8,24},{10,26},{12,28},{14,30},{16,0},... | collective-permute-start | bytes 110600 | tf_op jit(solution)/shard_map/ppermute | solution.py:564
  45.4 4.9 %collective-permute-start.17 = (bf16[9,16,128]{2,1,0:T(8,128)(2,1)S(1)}, bf16[9,16,128]{2,1,0:T(8,128)(2,1)S(1)}, u32[]{:S(2)}, u32[]{:S(2)}) collective-permute-start(bf16[9,16,128]{2,1,0:T(8,128)(2,1)S(1)} %shard_map.196.refs_0_), channel_id=1, source_target_pairs={{0,8},{2,10},{4,12},{6,14},{8,0},{10,2},{12,4},{14,6},{16,24},{18,... | collective-permute-start | bytes 110600 | tf_op jit(solution)/shard_map/ppermute | solution.py:564
  50.3 4.9 %collective-permute-start.22 = (bf16[9,16,128]{2,1,0:T(8,128)(2,1)S(1)}, bf16[9,16,128]{2,1,0:T(8,128)(2,1)S(1)}, u32[]{:S(2)}, u32[]{:S(2)}) collective-permute-start(bf16[9,16,128]{2,1,0:T(8,128)(2,1)S(1)} %shard_map.197.refs_0_), channel_id=1, source_target_pairs={{0,6},{2,4},{4,2},{6,0},{8,14},{10,12},{12,10},{14,8},{16,22},{18,... | collective-permute-start | bytes 110600 | tf_op jit(solution)/shard_map/ppermute | solution.py:564
  51.8 5.1 %collective-permute-start.21 = (bf16[9,16,128]{2,1,0:T(8,128)(2,1)S(1)}, bf16[9,16,128]{2,1,0:T(8,128)(2,1)S(1)}, u32[]{:S(2)}, u32[]{:S(2)}) collective-permute-start(bf16[9,16,128]{2,1,0:T(8,128)(2,1)S(1)} %shard_map.197.refs_0_), channel_id=1, source_target_pairs={{0,4},{2,6},{4,0},{6,2},{8,12},{10,14},{12,8},{14,10},{16,20},{18,... | collective-permute-start | bytes 110600 | tf_op jit(solution)/shard_map/ppermute | solution.py:564
  53.3 4.0 %collective-permute-start.20 = (bf16[9,16,128]{2,1,0:T(8,128)(2,1)S(1)}, bf16[9,16,128]{2,1,0:T(8,128)(2,1)S(1)}, u32[]{:S(2)}, u32[]{:S(2)}) collective-permute-start(bf16[9,16,128]{2,1,0:T(8,128)(2,1)S(1)} %shard_map.197.refs_0_), channel_id=1, source_target_pairs={{0,2},{2,0},{4,6},{6,4},{8,10},{10,8},{12,14},{14,12},{16,18},{18,... | collective-permute-start | bytes 110600 | tf_op jit(solution)/shard_map/ppermute | solution.py:564

commit v7 on v3

--- a/solution.py
+++ b/solution.py
@@ -400,7 +400,9 @@
             unit = current * inverse
             if column + 1 < rank:
                 ahead = spread(residual, column + 1)
-                step = dots(spread(original, column + 1), current) * inverse
+                next_tile, next_at = divmod(column + 1, SUBLANES)
+                found = {q: dots(original[q], current) * inverse for q in range(next_tile, tiles)}
+                step = found[next_tile][next_at : next_at + 1]
                 own = dots(ahead, current) * inverse
                 following = ahead - unit * (step + own - step * (square * inverse * inverse))
                 if column:
@@ -408,8 +410,8 @@
                     following = following - known[which] + (step * inverse) * cross
             finished[tile] = jnp.where(place == at, unit, finished[tile])
             if column + 1 < rank:
-                for q in range((column + 1) // SUBLANES, tiles):
-                    residual[q] = residual[q] - (dots(original[q], current) * inverse) * unit
+                for q in found:
+                    residual[q] = residual[q] - found[q] * unit
                 currents[which] = following
             if column + 2 < rank:
                 far = spread(residual, column + 2)

time: 58.8 us -> 58.8 us (level)
  no operation moved by 1% of the time
where the time goes in v7:
time: 58.8 us; the launch traced here: 58.6 us
  starting transfers between devices  22.8 us (39%)
  Pallas kernels  22.5 us (38%)
  waiting for transfers between devices  12.4 us (21%)
  between operations  0.95 us (2%)
    ppermute x23, starting transfers between devices, exchange(): lax.ppermute(value, axis, [(at, at ^ distance) for at in range(count)])  22.8 us
    ppermute x23, waiting for transfers between devices, exchange(): lax.ppermute(value, axis, [(at, at ^ distance) for at in range(count)])  12.4 us
    pallas_call x1, Pallas kernels, shards(): call(functools.partial(attend_kernel, blocks, 1.0 / n_mp), (shape((width,...  7.04 us
    pallas_call x1, Pallas kernels, shards(): call(functools.partial(ortho_kernel, 1.0 / n_dp, len(lefts), len(stats)),...  3.38 us
    pallas_call x1, Pallas kernels, shards(): call(functools.partial(table_kernel, blocks), shape((head_count, padded +...  2.98 us
    pallas_call x1, Pallas kernels, shards(): call(functools.partial(prepare_kernel, blocks, READY_HEADS), (shape((row_...  2.58 us
    pallas_call x1, Pallas kernels, shards(): call(functools.partial(last_kernel, 1.0 / n_dp, 1.0 / (n_dp * n_mp), late...  1.77 us
    pallas_call x1, Pallas kernels, shards(): call(functools.partial(token_kernel, blocks), (shape((row_count, features...  1.71 us
  transfers between devices with their start and end apart: 23, of which 10 were waited for; matrix products, arithmetic and copies ran while one was open for 0% of the time, Pallas kernels for 17%

profile of v7, /device:TPU:0, one launch (start us, length us, event | category | flops | bytes accessed | tf_op | source)
XLA Modules:
  0.0 58.6 jit_solution(5737999394791294582)
XLA Ops:
  0.6 0.5 collective-permute-start
  1.8 2.6 %shard_map.187 = (bf16[288,512]{1,0:T(8,128)(2,1)S(1)}, f32[288,1536]{1,0:T(8,128)S(1)}, f32[2,144,144]{2,1,0:T(8,128)S(1)}, s32[144,144]{1,0:T(8,128)S(1)}, f32...) custom-call(s32[144,144]{1,0:T(8,128)} %refs_0_.1, ...), custom_call_target="tpu_custom_call" | custom-call | flops 226492416 | bytes 4194304 | tf_op jit(solution)/shard_map/pallas_call | solution.py:636
  4.4 7.0 %shard_map.188 = (bf16[256,2048]{1,0:T(8,128)(2,1)S(1)}, bf16[256,2048]{1,0:T(8,128)(2,1)S(1)}, f32[64,256]{1,0:T(8,128)S(1)}, f32[64,256]{1,0:T(8,128)S(1)}, f3...) custom-call(bf16[288,512]{1,0:T(8,128)(2,1)S(1)} %get-tuple-element.53.refs_0_, ...), custom_call_target="tpu_custom_call" | custom-call | flops 1207959552 | bytes 8388608 | tf_op jit(solution)/shard_map/pallas_call | solution.py:657
  11.4 0.5 collective-permute-start.4
  11.9 0.7 %shard_map.189.left_own = f32[64,256]{1,0:T(8,128)S(1)} custom-call(f32[64,256]{1,0:T(8,128)S(1)} %get-tuple-element.68.term_left, f32[256,1536]{1,0:T(8,128)S(1)} %get-tuple-element.69.in_error.refs_2_, f32[256,512]{1,0:T(8,128)S(1)} %get-tuple-element.70.out_error.refs_3_, f32[32,1536]{1,0:T(8,128)S(1)} %get-tuple-element.63.refs_10_.in_basis, ...), custom_call_target="tpu_custom_call" | custom-call | flops 134217728 | bytes 3145728 | tf_op jit(solution)/shard_map/pallas_call | solution.py:689
  13.4 4.9 %collective-permute-start.7 = (f32[64,256]{1,0:T(8,128)S(1)}, f32[64,256]{1,0:T(8,128)S(1)}, u32[]{:S(2)}, u32[]{:S(2)}) collective-permute-start(f32[64,256]{1,0:T(8,128)S(1)} %get-tuple-element.74.refs_0_), channel_id=1, source_target_pairs={{0,24},{2,26},{4,28},{6,30},{8,16},{10,18},{12,20},{14,22},{16,8},... | collective-permute-start | bytes 196616 | tf_op jit(solution)/shard_map/ppermute | solution.py:558
  18.3 0.6 collective-permute-start.5
  18.9 3.0 %shard_map.191.refs_4_ = f32[8,1024]{1,0:T(8,128)S(1)} custom-call(f32[8,144,144]{2,1,0:T(8,128)S(1)} %get-tuple-element.75.refs_0_, f32[8,144,144]{2,1,0:T(8,128)S(1)} %collective-permute-done.8.refs_1_, bf16[256,2048]{1,0:T(8,128)(2,1)S(1)} %get-tuple-element.76.refs_2_.refs_0_, bf16[256,2048]{1,0:T(8,128)(2,1)S(1)} %get-tuple-element.77.refs_3_, ...), custom_call_target="tpu_custom_call" | custom-call | flops 452984832 | bytes 4194304 | tf_op jit(solution)/shard_map/pallas_call | solution.py:709
  21.9 2.3 %collective-permute-done.6.refs_2_ = f32[64,256]{1,0:T(8,128)S(1)} collective-permute-done((f32[64,256]{1,0:T(8,128)S(1)}, f32[64,256]{1,0:T(8,128)S(1)}, u32[]{:S(2)}, u32[]{:S(2)}) %collective-permute-start.6) | collective-permute-done | bytes 65568 | tf_op jit(solution)/shard_map/ppermute | solution.py:558
  24.2 2.5 %collective-permute-start.12 = (f32[64,256]{1,0:T(8,128)S(1)}, f32[64,256]{1,0:T(8,128)S(1)}, u32[]{:S(2)}, u32[]{:S(2)}) collective-permute-start(f32[64,256]{1,0:T(8,128)S(1)} %shard_map.192.refs_0_), channel_id=1, source_target_pairs={{0,6},{2,4},{4,2},{6,0},{8,14},{10,12},{12,10},{14,8},{16,22},{18,... | collective-permute-start | bytes 196616 | tf_op jit(solution)/shard_map/ppermute | solution.py:558
  26.7 0.5 collective-permute-start.11
  27.2 0.5 collective-permute-start.10
  27.8 0.6 shard_map.193.refs_6_.refs_3_.refs_5_
  28.3 1.2 %collective-permute-done.12.refs_3_ = f32[64,256]{1,0:T(8,128)S(1)} collective-permute-done((f32[64,256]{1,0:T(8,128)S(1)}, f32[64,256]{1,0:T(8,128)S(1)}, u32[]{:S(2)}, u32[]{:S(2)}) %collective-permute-start.12) | collective-permute-done | bytes 65568 | tf_op jit(solution)/shard_map/ppermute | solution.py:558
  29.6 1.4 %collective-permute-done.11.refs_2_ = f32[64,256]{1,0:T(8,128)S(1)} collective-permute-done((f32[64,256]{1,0:T(8,128)S(1)}, f32[64,256]{1,0:T(8,128)S(1)}, u32[]{:S(2)}, u32[]{:S(2)}) %collective-permute-start.11) | collective-permute-done | bytes 65568 | tf_op jit(solution)/shard_map/ppermute | solution.py:558
  31.0 0.5 collective-permute-done.10.refs_1_
  31.5 3.4 %shard_map.194 = (f32[64,256]{1,0:T(8,128)S(1)}, bf16[32,640]{1,0:T(8,128)(2,1)S(1)}, bf16[32,640]{1,0:T(8,128)(2,1)S(1)}, bf16[32,640]{1,0:T(8,128)(2,1)S(1)}, bf16[32,640]{1,0:T(8,128)(2,1)S(1)}) custom-call(f32[64,256]{1,0:T(8,128)S(1)} %shard_map.192.refs_0_, f32[64,256]{1,0:T(8,128)S(1)} %collective-permute-done.10.refs_1_, ...), custom_call_target="tpu_custom_call" | custom-call | flops 201326592 | bytes 3145728 | tf_op jit(solution)/shard_map/pallas_call | solution.py:744
  34.9 0.6 collective-permute-start.14
  35.5 1.5 %collective-permute-start.15 = (bf16[32,640]{1,0:T(8,128)(2,1)S(1)}, bf16[32,640]{1,0:T(8,128)(2,1)S(1)}, u32[]{:S(2)}, u32[]{:S(2)}) collective-permute-start(bf16[32,640]{1,0:T(8,128)(2,1)S(1)} %get-tuple-element.82), channel_id=1, source_target_pairs={{0,4},{2,6},{4,0},{6,2},{8,12},{10,14},{12,8},{14,10},{16,20},{18,... | collective-permute-start | bytes 122888 | tf_op jit(solution)/shard_map/ppermute | solution.py:558
  37.0 1.4 %collective-permute-start.16 = (bf16[32,640]{1,0:T(8,128)(2,1)S(1)}, bf16[32,640]{1,0:T(8,128)(2,1)S(1)}, u32[]{:S(2)}, u32[]{:S(2)}) collective-permute-start(bf16[32,640]{1,0:T(8,128)(2,1)S(1)} %get-tuple-element.83), channel_id=1, source_target_pairs={{0,6},{2,4},{4,2},{6,0},{8,14},{10,12},{12,10},{14,8},{16,22},{18,... | collective-permute-start | bytes 122888 | tf_op jit(solution)/shard_map/ppermute | solution.py:558
  38.4 1.7 %shard_map.195 = (bf16[288,512]{1,0:T(8,128)(2,1)}, f32[8,128]{1,0:T(8,128)S(1)}) custom-call(bf16[288,1536]{1,0:T(8,128)(2,1)S(1)} %get-tuple-element.65.packed, bf16[256,1536]{1,0:T(8,128)(2,1)S(1)} %get-tuple-element.61.refs_8_.refs_4_.refs_0_, bf16[256,1536]{1,0:T(8,128)(2,1)S(1)} %collective-permute-done.refs_12_.refs_5_.refs_1_, ...), custom_call_target="tpu_custom_call" | custom-call | flops 452984832 | bytes 4194304 | tf_op jit(solution)/shard_map/pallas_call | solution.py:754
  40.2 1.7 %collective-permute-done.16.refs_3_ = bf16[32,640]{1,0:T(8,128)(2,1)S(1)} collective-permute-done((bf16[32,640]{1,0:T(8,128)(2,1)S(1)}, bf16[32,640]{1,0:T(8,128)(2,1)S(1)}, u32[]{:S(2)}, u32[]{:S(2)}) %collective-permute-start.16) | collective-permute-done | bytes 40992 | tf_op jit(solution)/shard_map/ppermute | solution.py:558
  41.9 2.8 %collective-permute-start.19 = (bf16[32,640]{1,0:T(8,128)(2,1)S(1)}, bf16[32,640]{1,0:T(8,128)(2,1)S(1)}, u32[]{:S(2)}, u32[]{:S(2)}) collective-permute-start(bf16[32,640]{1,0:T(8,128)(2,1)S(1)} %shard_map.196.refs_0_), channel_id=1, source_target_pairs={{0,24},{2,26},{4,28},{6,30},{8,16},{10,18},{12,20},{14,22},{16,8},... | collective-permute-start | bytes 122888 | tf_op jit(solution)/shard_map/ppermute | solution.py:558
  44.7 1.7 %collective-permute-start.17 = (bf16[32,640]{1,0:T(8,128)(2,1)S(1)}, bf16[32,640]{1,0:T(8,128)(2,1)S(1)}, u32[]{:S(2)}, u32[]{:S(2)}) collective-permute-start(bf16[32,640]{1,0:T(8,128)(2,1)S(1)} %shard_map.196.refs_0_), channel_id=1, source_target_pairs={{0,8},{2,10},{4,12},{6,14},{8,0},{10,2},{12,4},{14,6},{16,24},{18,... | collective-permute-start | bytes 122888 | tf_op jit(solution)/shard_map/ppermute | solution.py:558
  46.4 1.4 %collective-permute-done.19.refs_3_ = bf16[32,640]{1,0:T(8,128)(2,1)S(1)} collective-permute-done((bf16[32,640]{1,0:T(8,128)(2,1)S(1)}, bf16[32,640]{1,0:T(8,128)(2,1)S(1)}, u32[]{:S(2)}, u32[]{:S(2)}) %collective-permute-start.19) | collective-permute-done | bytes 40992 | tf_op jit(solution)/shard_map/ppermute | solution.py:558
  47.8 1.8 %collective-permute-done.18.refs_2_ = bf16[32,640]{1,0:T(8,128)(2,1)S(1)} collective-permute-done((bf16[32,640]{1,0:T(8,128)(2,1)S(1)}, bf16[32,640]{1,0:T(8,128)(2,1)S(1)}, u32[]{:S(2)}, u32[]{:S(2)}) %collective-permute-start.18) | collective-permute-done | bytes 40992 | tf_op jit(solution)/shard_map/ppermute | solution.py:558
  49.6 1.5 %collective-permute-start.22 = (bf16[32,640]{1,0:T(8,128)(2,1)S(1)}, bf16[32,640]{1,0:T(8,128)(2,1)S(1)}, u32[]{:S(2)}, u32[]{:S(2)}) collective-permute-start(bf16[32,640]{1,0:T(8,128)(2,1)S(1)} %shard_map.197.refs_0_), channel_id=1, source_target_pairs={{0,6},{2,4},{4,2},{6,0},{8,14},{10,12},{12,10},{14,8},{16,22},{18,... | collective-permute-start | bytes 122888 | tf_op jit(solution)/shard_map/ppermute | solution.py:558
  51.2 1.5 %collective-permute-start.21 = (bf16[32,640]{1,0:T(8,128)(2,1)S(1)}, bf16[32,640]{1,0:T(8,128)(2,1)S(1)}, u32[]{:S(2)}, u32[]{:S(2)}) collective-permute-start(bf16[32,640]{1,0:T(8,128)(2,1)S(1)} %shard_map.197.refs_0_), channel_id=1, source_target_pairs={{0,4},{2,6},{4,0},{6,2},{8,12},{10,14},{12,8},{14,10},{16,20},{18,... | collective-permute-start | bytes 122888 | tf_op jit(solution)/shard_map/ppermute | solution.py:558
  52.7 0.5 collective-permute-start.20
  53.2 1.4 %collective-permute-done.22.refs_1_.refs_3_ = bf16[32,640]{1,0:T(8,128)(2,1)S(1)} collective-permute-done((bf16[32,640]{1,0:T(8,128)(2,1)S(1)}, bf16[32,640]{1,0:T(8,128)(2,1)S(1)}, u32[]{:S(2)}, u32[]{:S(2)}) %collective-permute-start.22) | collective-permute-done | bytes 40992 | tf_op jit(solution)/shard_map/ppermute | solution.py:558
  54.6 1.6 %shard_map.198 = (f32[256,1536]{1,0:T(8,128)}, f32[256,512]{1,0:T(8,128)}, f32[256,1536]{1,0:T(8,128)}, f32[256,512]{1,0:T(8,128)}) custom-call(bf16[32,640]{1,0:T(8,128)(2,1)S(1)} %shard_map.197.refs_0_, bf16[32,640]{1,0:T(8,128)(2,1)S(1)} %collective-permute-done.22.refs_1_.refs_3_, f32[64,256]{1,0:T(8,128)S(1)} %get-tuple-element.78.refs_5_.refs_2_.refs_4_, ...), custom_call_target="tpu_custom_call" | custom-call | flops 100663296 | bytes 1048576 | tf_op jit(solution)/shard_map/pallas_call | solution.py:804
  56.7 1.8 %shard_map.199 = (f32[256,1536]{1,0:T(8,128)}, f32[256,512]{1,0:T(8,128)}, f32[256,1536]{1,0:T(8,128)}, f32[256,512]{1,0:T(8,128)}, f32[32,1536]{1,0:T(8,128)}, ...) custom-call(bf16[32,640]{1,0:T(8,128)(2,1)S(1)} %shard_map.197.refs_, ...), custom_call_target="tpu_custom_call", output_to_operand_aliasing={{0}: (6, {}), {1}: (7, {}), {2}: (8, {}), {3}: (9, {})} | custom-call | flops 100663296 | bytes 1048576 | tf_op jit(solution)/shard_map/pallas_call | solution.py:813
  (27 shorter events, 1.9 us)
Async XLA Ops:
  0.6 3.7 %collective-permute-start = (bf16[256,1536]{1,0:T(8,128)(2,1)}, bf16[256,1536]{1,0:T(8,128)(2,1)S(1)}, u32[]{:S(2)}, u32[]{:S(2)}) collective-permute-start(bf16[256,1536]{1,0:T(8,128)(2,1)} %refs_4_.1), channel_id=1, source_target_pairs={{0,1},{1,0},{2,3},{3,2},{4,5},{5,4},{6,7},{7,6},{8,9},{9,8},{10,11... | collective-permute-start | bytes 2359304 | tf_op jit(solution)/shard_map/ppermute | solution.py:558
  1.2 3.2 %collective-permute-start.1 = (bf16[256,512]{1,0:T(8,128)(2,1)}, bf16[256,512]{1,0:T(8,128)(2,1)S(1)}, u32[]{:S(2)}, u32[]{:S(2)}) collective-permute-start(bf16[256,512]{1,0:T(8,128)(2,1)} %refs_7_.1), channel_id=1, source_target_pairs={{0,1},{1,0},{2,3},{3,2},{4,5},{5,4},{6,7},{7,6},{8,9},{9,8},{10,11... | collective-permute-start | bytes 786440 | tf_op jit(solution)/shard_map/ppermute | solution.py:558
  1.2 3.1 %collective-permute-start.2 = (f32[32,1536]{1,0:T(8,128)}, f32[32,1536]{1,0:T(8,128)S(1)}, u32[]{:S(2)}, u32[]{:S(2)}) collective-permute-start(f32[32,1536]{1,0:T(8,128)} %bitcast.27), channel_id=1, source_target_pairs={{0,1},{1,0},{2,3},{3,2},{4,5},{5,4},{6,7},{7,6},{8,9},{9,8},{10,11... | collective-permute-start | bytes 589832 | tf_op jit(solution)/shard_map/ppermute | solution.py:558
  1.7 2.7 %collective-permute-start.3 = (f32[32,512]{1,0:T(8,128)}, f32[32,512]{1,0:T(8,128)S(1)}, u32[]{:S(2)}, u32[]{:S(2)}) collective-permute-start(f32[32,512]{1,0:T(8,128)} %bitcast.29), channel_id=1, source_target_pairs={{0,1},{1,0},{2,3},{3,2},{4,5},{5,4},{6,7},{7,6},{8,9},{9,8},{10,11... | collective-permute-start | bytes 196616 | tf_op jit(solution)/shard_map/ppermute | solution.py:558
  11.4 1.4 %collective-permute-start.4 = (f32[64,256]{1,0:T(8,128)S(1)}, f32[64,256]{1,0:T(8,128)S(1)}, u32[]{:S(2)}, u32[]{:S(2)}) collective-permute-start(f32[64,256]{1,0:T(8,128)S(1)} %get-tuple-element.71), channel_id=1, source_target_pairs={{0,1},{1,0},{2,3},{3,2},{4,5},{5,4},{6,7},{7,6},{8,9},{9,8},{10,11... | collective-permute-start | bytes 196616 | tf_op jit(solution)/shard_map/ppermute | solution.py:558
  12.8 15.0 %collective-permute-start.13 = (bf16[256,2048]{1,0:T(8,128)(2,1)S(1)}, bf16[256,2048]{1,0:T(8,128)(2,1)S(1)}, u32[]{:S(2)}, u32[]{:S(2)}) collective-permute-start(bf16[256,2048]{1,0:T(8,128)(2,1)S(1)} %get-tuple-element.77.refs_3_), channel_id=1, source_target_pairs={{0,1},{1,0},{2,3},{3,2},{4,5},{5,4},{6,7},{7,6},{8,9},{9,8},{10,11... | collective-permute-start | bytes 3145736 | tf_op jit(solution)/shard_map/ppermute | solution.py:558
  13.2 5.6 %collective-permute-start.8 = (f32[8,144,144]{2,1,0:T(8,128)S(1)}, f32[8,144,144]{2,1,0:T(8,128)S(1)}, u32[]{:S(2)}, u32[]{:S(2)}) collective-permute-start(f32[8,144,144]{2,1,0:T(8,128)S(1)} %get-tuple-element.75.refs_0_), channel_id=1, source_target_pairs={{0,1},{1,0},{2,3},{3,2},{4,5},{5,4},{6,7},{7,6},{8,9},{9,8},{10,11... | collective-permute-start | bytes 1990664 | tf_op jit(solution)/shard_map/ppermute | solution.py:558
  13.4 8.5 %collective-permute-start.7 = (f32[64,256]{1,0:T(8,128)S(1)}, f32[64,256]{1,0:T(8,128)S(1)}, u32[]{:S(2)}, u32[]{:S(2)}) collective-permute-start(f32[64,256]{1,0:T(8,128)S(1)} %get-tuple-element.74.refs_0_), channel_id=1, source_target_pairs={{0,24},{2,26},{4,28},{6,30},{8,16},{10,18},{12,20},{14,22},{16,8},... | collective-permute-start | bytes 196616 | tf_op jit(solution)/shard_map/ppermute | solution.py:558
  18.3 5.9 %collective-permute-start.6 = (f32[64,256]{1,0:T(8,128)S(1)}, f32[64,256]{1,0:T(8,128)S(1)}, u32[]{:S(2)}, u32[]{:S(2)}) collective-permute-start(f32[64,256]{1,0:T(8,128)S(1)} %get-tuple-element.74.refs_0_), channel_id=1, source_target_pairs={{0,16},{2,18},{4,20},{6,22},{8,24},{10,26},{12,28},{14,30},{16,0},... | collective-permute-start | bytes 196616 | tf_op jit(solution)/shard_map/ppermute | solution.py:558
  18.3 5.9 %collective-permute-start.5 = (f32[64,256]{1,0:T(8,128)S(1)}, f32[64,256]{1,0:T(8,128)S(1)}, u32[]{:S(2)}, u32[]{:S(2)}) collective-permute-start(f32[64,256]{1,0:T(8,128)S(1)} %get-tuple-element.74.refs_0_), channel_id=1, source_target_pairs={{0,8},{2,10},{4,12},{6,14},{8,0},{10,2},{12,4},{14,6},{16,24},{18,... | collective-permute-start | bytes 196616 | tf_op jit(solution)/shard_map/ppermute | solution.py:558
  21.8 2.4 %collective-permute-start.9 = (f32[8,1024]{1,0:T(8,128)S(1)}, f32[8,1024]{1,0:T(8,128)S(1)}, u32[]{:S(2)}, u32[]{:S(2)}) collective-permute-start(f32[8,1024]{1,0:T(8,128)S(1)} %shard_map.191.refs_4_), channel_id=1, source_target_pairs={{0,1},{1,0},{2,3},{3,2},{4,5},{5,4},{6,7},{7,6},{8,9},{9,8},{10,11... | collective-permute-start | bytes 98312 | tf_op jit(solution)/shard_map/ppermute | solution.py:558
  24.2 5.3 %collective-permute-start.12 = (f32[64,256]{1,0:T(8,128)S(1)}, f32[64,256]{1,0:T(8,128)S(1)}, u32[]{:S(2)}, u32[]{:S(2)}) collective-permute-start(f32[64,256]{1,0:T(8,128)S(1)} %shard_map.192.refs_0_), channel_id=1, source_target_pairs={{0,6},{2,4},{4,2},{6,0},{8,14},{10,12},{12,10},{14,8},{16,22},{18,... | collective-permute-start | bytes 196616 | tf_op jit(solution)/shard_map/ppermute | solution.py:558
  26.7 4.3 %collective-permute-start.11 = (f32[64,256]{1,0:T(8,128)S(1)}, f32[64,256]{1,0:T(8,128)S(1)}, u32[]{:S(2)}, u32[]{:S(2)}) collective-permute-start(f32[64,256]{1,0:T(8,128)S(1)} %shard_map.192.refs_0_), channel_id=1, source_target_pairs={{0,4},{2,6},{4,0},{6,2},{8,12},{10,14},{12,8},{14,10},{16,20},{18,... | collective-permute-start | bytes 196616 | tf_op jit(solution)/shard_map/ppermute | solution.py:558
  27.2 4.3 %collective-permute-start.10 = (f32[64,256]{1,0:T(8,128)S(1)}, f32[64,256]{1,0:T(8,128)S(1)}, u32[]{:S(2)}, u32[]{:S(2)}) collective-permute-start(f32[64,256]{1,0:T(8,128)S(1)} %shard_map.192.refs_0_), channel_id=1, source_target_pairs={{0,2},{2,0},{4,6},{6,4},{8,10},{10,8},{12,14},{14,12},{16,18},{18,... | collective-permute-start | bytes 196616 | tf_op jit(solution)/shard_map/ppermute | solution.py:558
  34.9 5.3 %collective-permute-start.14 = (bf16[32,640]{1,0:T(8,128)(2,1)S(1)}, bf16[32,640]{1,0:T(8,128)(2,1)S(1)}, u32[]{:S(2)}, u32[]{:S(2)}) collective-permute-start(bf16[32,640]{1,0:T(8,128)(2,1)S(1)} %get-tuple-element.81), channel_id=1, source_target_pairs={{0,2},{2,0},{4,6},{6,4},{8,10},{10,8},{12,14},{14,12},{16,18},{18,... | collective-permute-start | bytes 122888 | tf_op jit(solution)/shard_map/ppermute | solution.py:558
  35.5 4.7 %collective-permute-start.15 = (bf16[32,640]{1,0:T(8,128)(2,1)S(1)}, bf16[32,640]{1,0:T(8,128)(2,1)S(1)}, u32[]{:S(2)}, u32[]{:S(2)}) collective-permute-start(bf16[32,640]{1,0:T(8,128)(2,1)S(1)} %get-tuple-element.82), channel_id=1, source_target_pairs={{0,4},{2,6},{4,0},{6,2},{8,12},{10,14},{12,8},{14,10},{16,20},{18,... | collective-permute-start | bytes 122888 | tf_op jit(solution)/shard_map/ppermute | solution.py:558
  37.0 4.9 %collective-permute-start.16 = (bf16[32,640]{1,0:T(8,128)(2,1)S(1)}, bf16[32,640]{1,0:T(8,128)(2,1)S(1)}, u32[]{:S(2)}, u32[]{:S(2)}) collective-permute-start(bf16[32,640]{1,0:T(8,128)(2,1)S(1)} %get-tuple-element.83), channel_id=1, source_target_pairs={{0,6},{2,4},{4,2},{6,0},{8,14},{10,12},{12,10},{14,8},{16,22},{18,... | collective-permute-start | bytes 122888 | tf_op jit(solution)/shard_map/ppermute | solution.py:558
  41.9 5.9 %collective-permute-start.19 = (bf16[32,640]{1,0:T(8,128)(2,1)S(1)}, bf16[32,640]{1,0:T(8,128)(2,1)S(1)}, u32[]{:S(2)}, u32[]{:S(2)}) collective-permute-start(bf16[32,640]{1,0:T(8,128)(2,1)S(1)} %shard_map.196.refs_0_), channel_id=1, source_target_pairs={{0,24},{2,26},{4,28},{6,30},{8,16},{10,18},{12,20},{14,22},{16,8},... | collective-permute-start | bytes 122888 | tf_op jit(solution)/shard_map/ppermute | solution.py:558
  44.7 4.9 %collective-permute-start.18 = (bf16[32,640]{1,0:T(8,128)(2,1)S(1)}, bf16[32,640]{1,0:T(8,128)(2,1)S(1)}, u32[]{:S(2)}, u32[]{:S(2)}) collective-permute-start(bf16[32,640]{1,0:T(8,128)(2,1)S(1)} %shard_map.196.refs_0_), channel_id=1, source_target_pairs={{0,16},{2,18},{4,20},{6,22},{8,24},{10,26},{12,28},{14,30},{16,0},... | collective-permute-start | bytes 122888 | tf_op jit(solution)/shard_map/ppermute | solution.py:558
  44.7 4.9 %collective-permute-start.17 = (bf16[32,640]{1,0:T(8,128)(2,1)S(1)}, bf16[32,640]{1,0:T(8,128)(2,1)S(1)}, u32[]{:S(2)}, u32[]{:S(2)}) collective-permute-start(bf16[32,640]{1,0:T(8,128)(2,1)S(1)} %shard_map.196.refs_0_), channel_id=1, source_target_pairs={{0,8},{2,10},{4,12},{6,14},{8,0},{10,2},{12,4},{14,6},{16,24},{18,... | collective-permute-start | bytes 122888 | tf_op jit(solution)/shard_map/ppermute | solution.py:558
  49.6 5.0 %collective-permute-start.22 = (bf16[32,640]{1,0:T(8,128)(2,1)S(1)}, bf16[32,640]{1,0:T(8,128)(2,1)S(1)}, u32[]{:S(2)}, u32[]{:S(2)}) collective-permute-start(bf16[32,640]{1,0:T(8,128)(2,1)S(1)} %shard_map.197.refs_0_), channel_id=1, source_target_pairs={{0,6},{2,4},{4,2},{6,0},{8,14},{10,12},{12,10},{14,8},{16,22},{18,... | collective-permute-start | bytes 122888 | tf_op jit(solution)/shard_map/ppermute | solution.py:558
  51.2 5.1 %collective-permute-start.21 = (bf16[32,640]{1,0:T(8,128)(2,1)S(1)}, bf16[32,640]{1,0:T(8,128)(2,1)S(1)}, u32[]{:S(2)}, u32[]{:S(2)}) collective-permute-start(bf16[32,640]{1,0:T(8,128)(2,1)S(1)} %shard_map.197.refs_0_), channel_id=1, source_target_pairs={{0,4},{2,6},{4,0},{6,2},{8,12},{10,14},{12,8},{14,10},{16,20},{18,... | collective-permute-start | bytes 122888 | tf_op jit(solution)/shard_map/ppermute | solution.py:558
  52.7 4.0 %collective-permute-start.20 = (bf16[32,640]{1,0:T(8,128)(2,1)S(1)}, bf16[32,640]{1,0:T(8,128)(2,1)S(1)}, u32[]{:S(2)}, u32[]{:S(2)}) collective-permute-start(bf16[32,640]{1,0:T(8,128)(2,1)S(1)} %shard_map.197.refs_0_), channel_id=1, source_target_pairs={{0,2},{2,0},{4,6},{6,4},{8,10},{10,8},{12,14},{14,12},{16,18},{18,... | collective-permute-start | bytes 122888 | tf_op jit(solution)/shard_map/ppermute | solution.py:558
